TPU v7x, 32 devices: a whole 2x2x4 slice. The times are simulated.
32 devices in a mesh: site: 4 (over z), patch: 8 (over y, x, core).
Axes of the slice: x: 2, y: 2, z: 4, core: 2. Of those that a mesh axis runs over, the one named last changes fastest.
Arguments:
- slip_rates: bfloat16 [128, 64, 256], P('patch', 'site'), may hold values from -6 to 6
- green_tiles: bfloat16 [4, 256, 2, 1024], P('site', 'patch'), may hold values from -0.03125 to 0.03125
- patch_slot: int32 [128], replicated, may hold values from 0 to 255, as said below
Outputs:
- seismograms: float32 [4, 64, 2, 1280], P('site', 'patch')
Inputs may be any that keep to these rules, and one draw needn't show every extreme that they name: The values of patch_slot all differ. Patch p belongs to owner patch_slot[p] // 32 and fills its slot patch_slot[p] % 32; each owner has 1 to 32 patches in its first slots, and some owner has exactly 32. The 16 patches p with the same p // 16 include at most 4 of any one owner, and some such group includes exactly 4 of one owner.
All inputs are finite; a program needn't handle non-finite values.
Results may differ from a plain program's by a relative error of at most 0.0003.
Values may be sent and summed in bfloat16 or wider, within the bound.
No kernel may reach another device: no remote copies, remote signals or barrier semaphores. Data moves between devices by JAX's collectives and lax.ppermute only.
A program may use at most 64 MiB of HBM per device.

v0:
```python
import functools

import jax
import jax.numpy as jnp
from jax import lax
from jax.experimental import pallas as pl
from jax.experimental.pallas import tpu as pltpu
from jax.sharding import PartitionSpec as P

BLOCK = 16
LANES = 128
ROWS = 8
VMEM_LIMIT = 32 * 1024 * 1024
LARGEST = 32767.0
STEPS = 16
SMALLEST = 1e-30


def round_up(value, unit):
    return -(-value // unit) * unit


def params(limit=VMEM_LIMIT):
    return pltpu.CompilerParams(vmem_limit_bytes=limit)


def arrange_half(slip_ref, out_ref, core, owner):
    patches, both, samples = slip_ref.shape
    rows = both // 2
    per_reg = LANES // BLOCK
    blocks = samples // BLOCK
    depth = patches * BLOCK
    lane_block = lax.broadcasted_iota(jnp.int32, (rows, LANES), 1) // BLOCK
    for group in range(depth // LANES):
        done = {}
        for place in range(per_reg):
            full = slip_ref[group * per_reg + place].astype(jnp.float32)
            source = jnp.where(core == 0, full[:rows], full[rows:])
            for reg in range(samples // LANES):
                piece = source[:, reg * LANES : (reg + 1) * LANES]
                for inner in range(per_reg):
                    turn = (place - inner) % per_reg * BLOCK
                    moved = pltpu.roll(piece, turn, 1) if turn else piece
                    block = reg * per_reg + inner
                    if block in done:
                        moved = jnp.where(lane_block == place, moved, done[block])
                    done[block] = moved
        lanes = pl.ds(pl.multiple_of(owner * depth + group * LANES, LANES), LANES)
        for block in range(0, blocks, 2):
            pair = jnp.concatenate([done[block], done[block + 1]], axis=0)
            out_ref[block * rows : (block + 2) * rows, lanes] = pair.astype(jnp.bfloat16)


def arrange_own_kernel(
    slip_hbm, slots_hbm, green_hbm, out_ref, slots_ref, green_ref, slip_ref, sems
):
    fetch_slips = pltpu.make_async_copy(slip_hbm, slip_ref, sems.at[0])
    fetch_slots = pltpu.make_async_copy(slots_hbm, slots_ref, sems.at[1])
    fetch_greens = pltpu.make_async_copy(green_hbm, green_ref, sems.at[2])
    fetch_slips.start()
    fetch_slots.start()
    fetch_greens.start()
    fetch_slips.wait()
    core = lax.rem(lax.axis_index("patch"), 2)
    arrange_half(slip_ref, out_ref, core, core)
    fetch_slots.wait()
    fetch_greens.wait()


def arrange_other_kernel(slip_ref, green_ref, block_ref, out_ref):
    core = lax.rem(lax.axis_index("patch"), 2)
    arrange_half(slip_ref, out_ref, core, 1 - core)


def in_hbm(*values):
    return [pltpu.with_memory_space_constraint(value, pltpu.HBM) for value in values]


def arrange_own(slips, slots, greens):
    patches, both, samples = slips.shape
    block = jax.ShapeDtypeStruct(
        (samples // BLOCK * both // 2, 2 * patches * BLOCK), jnp.bfloat16
    )
    return pl.pallas_call(
        arrange_own_kernel,
        in_specs=[pl.BlockSpec(memory_space=pltpu.HBM)] * 3,
        out_shape=(
            block,
            jax.ShapeDtypeStruct(slots.shape, slots.dtype),
            jax.ShapeDtypeStruct(greens.shape, greens.dtype),
        ),
        scratch_shapes=[
            pltpu.VMEM(slips.shape, slips.dtype),
            pltpu.SemaphoreType.DMA((3,)),
        ],
        compiler_params=params(),
        name="arrange_own",
    )(*in_hbm(slips, slots, greens))


def arrange_other(slips, greens, block):
    return pl.pallas_call(
        arrange_other_kernel,
        in_specs=[
            pl.BlockSpec(memory_space=pltpu.VMEM),
            pl.BlockSpec(memory_space=pl.ANY),
            pl.BlockSpec(memory_space=pltpu.VMEM),
        ],
        out_shape=jax.ShapeDtypeStruct(block.shape, block.dtype),
        input_output_aliases={2: 0},
        compiler_params=params(),
        name="arrange_other",
    )(slips, greens, block)


def earlier_in_chip(count, per_chip):
    q = lax.broadcasted_iota(jnp.int32, (count, count), 0)
    p = lax.broadcasted_iota(jnp.int32, (count, count), 1)
    return ((q < p) & (q // per_chip == p // per_chip)).astype(jnp.float32).astype(jnp.bfloat16)


def one_hot(condition):
    return condition.astype(jnp.float32).astype(jnp.bfloat16)


def route_kernel(chips, per_chip, capacity, slots_ref, own_ref, other_ref, pick_ref, *out_refs):
    width, components, lags = own_ref.shape
    half = capacity // 2
    count = slots_ref.shape[1]
    own = lax.axis_index("patch")
    chip, core = own // 2, lax.rem(own, 2)
    slots = slots_ref[...]
    owner = slots // width
    mine = owner // 2 == chip
    place = slots % width + jnp.where(owner % 2 == core, 0, width)
    marks = jnp.broadcast_to(one_hot(mine), (16, count))
    rank = jnp.dot(marks, earlier_in_chip(count, per_chip), preferred_element_type=jnp.float32)
    rank = rank[:1].astype(jnp.int32)
    target = (lax.broadcasted_iota(jnp.int32, (1, count), 1) // per_chip) ^ chip
    code = jnp.where(mine, target * capacity + rank, -1)
    code_pick = one_hot(lax.broadcasted_iota(jnp.int32, (chips * capacity, count), 0) == code)
    slot_pick = one_hot(lax.broadcasted_iota(jnp.int32, (2 * width, count), 0) == place)
    pick = lax.dot_general(
        code_pick, slot_pick, (((1,), (1,)), ((), ())), preferred_element_type=jnp.float32
    ).astype(jnp.bfloat16)
    tiles = jnp.concatenate([own_ref[...], other_ref[...]], axis=0).astype(jnp.float32)
    by_comp = []
    for comp in range(components):
        both = tiles[:, comp, :].astype(jnp.bfloat16)
        chosen = jnp.dot(pick, both, preferred_element_type=jnp.float32)
        chosen = [chosen[step * capacity : (step + 1) * capacity] for step in range(chips)]
        last = chosen[-1]
        sent = [chosen[0]]
        for step in range(1, chips - 1, 2):
            sent.append(jnp.where(core == 0, chosen[step], chosen[step + 1]))
        sent.append(jnp.where(core == 0, last[:half], last[half:]))
        by_comp.append(sent)
    for values, out_ref in zip(zip(*by_comp), out_refs):
        out_ref[...] = jnp.concatenate(values, axis=0).astype(jnp.bfloat16)
    here = pltpu.roll(slots, lax.rem(count - chip * per_chip, count), 1)[:, :per_chip]
    owner = (here // (2 * width)) ^ chip
    marks = lax.broadcasted_iota(jnp.int32, (round_up(chips, 16), per_chip), 0) == owner
    rank = jnp.dot(
        one_hot(marks), earlier_in_chip(per_chip, per_chip), preferred_element_type=jnp.float32
    )
    rank = jnp.sum(jnp.where(marks, rank, 0.0), axis=0, keepdims=True).astype(jnp.int32)
    from_other = jnp.where(owner == chips - 1, rank // half, 1 - owner % 2) != core
    base = (owner - jnp.where(owner == chips - 1, 0, 1 - owner % 2)) * capacity
    code = base + jnp.where(
        owner == chips - 1,
        jnp.where(from_other, half, 0) + rank % half,
        jnp.where(from_other, capacity, 0) + rank,
    )
    code = jnp.where(owner == 0, rank, code)
    pick_ref[...] = one_hot(lax.broadcasted_iota(jnp.int32, pick_ref.shape, 0) == code)


def route_tiles(slots, own, other, chips, per_chip, capacity):
    components, lags = own.shape[1:]
    pick = jax.ShapeDtypeStruct((chips * capacity, per_chip), jnp.bfloat16)
    shape = jax.ShapeDtypeStruct((components * capacity, lags), jnp.bfloat16)
    part = jax.ShapeDtypeStruct((components * capacity // 2, lags), jnp.bfloat16)
    return pl.pallas_call(
        functools.partial(route_kernel, chips, per_chip, capacity),
        out_shape=(pick,) + (shape,) * (chips // 2) + (part,),
        compiler_params=params(),
        name="route_tiles",
    )(slots, own, other)


def pass_on(value, *others):
    def kernel(*refs):
        pass

    return pl.pallas_call(
        kernel,
        in_specs=[pl.BlockSpec(memory_space=pl.ANY)] * (1 + len(others)),
        out_specs=pl.BlockSpec(memory_space=pl.ANY),
        out_shape=jax.ShapeDtypeStruct(value.shape, value.dtype),
        input_output_aliases={0: 0},
        compiler_params=params(),
        name="pass_on",
    )(value, *others)


def shift_kernel(pick_ref, *refs):
    pieces, out_ref = refs[:-1], refs[-1]
    count = pick_ref.shape[1]
    components = sum(piece.shape[0] for piece in pieces) // pick_ref.shape[0]
    lags = pieces[0].shape[1]
    span = out_ref.shape[1] // components
    tail = jnp.zeros((BLOCK, span - lags), jnp.float32)
    for comp in range(components):
        arrived = []
        for piece in pieces:
            size = piece.shape[0] // components
            arrived.append(piece[...].astype(jnp.float32)[comp * size : (comp + 1) * size])
        arrived = jnp.concatenate(arrived, axis=0).astype(jnp.bfloat16)
        tiles = lax.dot_general(
            pick_ref[...], arrived, (((0,), (0,)), ((), ())), preferred_element_type=jnp.float32
        )
        for patch in range(count):
            row = jnp.broadcast_to(tiles[patch : patch + 1], (BLOCK, lags))
            wide = jnp.concatenate([row, tail], axis=1)
            moved = pltpu.roll(wide, 0, 1, stride=1, stride_axis=0)
            out_ref[
                patch * BLOCK : (patch + 1) * BLOCK, comp * span : (comp + 1) * span
            ] = moved.astype(jnp.bfloat16)


def shift_tiles(pick, pieces, components):
    lags = pieces[0].shape[1]
    span = round_up(lags + BLOCK, LANES)
    shape = jax.ShapeDtypeStruct((pick.shape[1] * BLOCK, components * span), jnp.bfloat16)
    return pl.pallas_call(
        shift_kernel, out_shape=shape, compiler_params=params(), name="shift_tiles"
    )(pick, *pieces)


def convolve_blocks(shifted_ref, slip_refs, stack_ref, product_ref, out_ref, rows):
    length = out_ref.shape[2]
    components = out_ref.shape[1] // rows
    height = slip_refs[0].shape[0]
    width = shifted_ref.shape[1] // components
    per_reg = LANES // BLOCK
    blocks = height // rows
    for step, ref in enumerate(slip_refs):
        stack_ref[step * height : (step + 1) * height] = ref[...]
    for comp in range(components):
        product_ref[...] = jnp.dot(
            stack_ref[...],
            shifted_ref[:, comp * width : (comp + 1) * width],
            preferred_element_type=jnp.float32,
        )
        for step in range(len(slip_refs)):
            total = None
            for inner in range(per_reg):
                part = None
                for outer in range(inner, blocks, per_reg):
                    lead = outer // per_reg * LANES
                    start = step * height + outer * rows
                    block = product_ref[start : start + rows, :]
                    pieces = [jnp.zeros((rows, lead), jnp.float32)] if lead else []
                    pieces.append(block[:, : min(width, length - lead)])
                    if length > lead + width:
                        pieces.append(jnp.zeros((rows, length - lead - width), jnp.float32))
                    block = jnp.concatenate(pieces, axis=1) if len(pieces) > 1 else pieces[0]
                    part = block if part is None else part + block
                if inner:
                    part = pltpu.roll(part, inner * BLOCK, 1)
                total = part if total is None else total + part
            out_ref[step, comp * rows : (comp + 1) * rows, :] = total


def convolve_first_kernel(rows, shifted_ref, *refs):
    slip_refs, (out_ref, stack_ref, product_ref) = refs[:-3], refs[-3:]
    convolve_blocks(shifted_ref, slip_refs, stack_ref, product_ref, out_ref, rows)


def convolve_scratch(shifted, count, height, depth, components):
    return [
        pltpu.VMEM((count * height, depth), jnp.bfloat16),
        pltpu.VMEM((count * height, shifted.shape[1] // components), jnp.float32),
    ]


def convolve_first(shifted, slips, rows, components, length):
    shape = jax.ShapeDtypeStruct((len(slips), components * rows, length), jnp.float32)
    return pl.pallas_call(
        functools.partial(convolve_first_kernel, rows),
        out_shape=shape,
        scratch_shapes=convolve_scratch(shifted, len(slips), *slips[0].shape, components),
        compiler_params=params(),
        name="convolve_first",
    )(shifted, *slips)


def unit_of(exponent):
    return jnp.exp2(exponent.astype(jnp.float32) * (1.0 / STEPS)) * (1.0 / LARGEST)


def convolve_last_kernel(rows, shifted_ref, slip_ref, first_ref, *refs):
    out_refs, (stack_ref, product_ref, last_ref) = refs[:-3], refs[-3:]
    convolve_blocks(shifted_ref, [slip_ref], stack_ref, product_ref, last_ref, rows)
    count = first_ref.shape[0]
    length = first_ref.shape[2]
    turn = lax.axis_index("site") ^ (lax.axis_index("patch") // 2)
    last = last_ref[0]
    for step, ref in enumerate(out_refs):
        source = step ^ turn
        total = jnp.where(source == count, last, first_ref[jnp.minimum(source, count - 1)])
        if step == 0:
            ref[...] = total
            continue
        peak = jnp.maximum(jnp.max(jnp.abs(total), axis=1, keepdims=True), SMALLEST)
        exponent = jnp.ceil(jnp.log2(peak) * STEPS).astype(jnp.int32)
        scaled = jnp.round(total * (1.0 / unit_of(exponent)))
        whole = jnp.clip(scaled, -LARGEST, LARGEST).astype(jnp.int32)
        ref[:, :length] = whole.astype(jnp.int16)
        ref[:, length:] = jnp.broadcast_to(
            exponent, (exponent.shape[0], ref.shape[1] - length)
        ).astype(jnp.int16)


def convolve_last(shifted, slip, first, rows, components):
    count, height, length = first.shape
    own = jax.ShapeDtypeStruct((height, length), jnp.float32)
    sent = jax.ShapeDtypeStruct((height, round_up(length, LANES) + LANES), jnp.int16)
    return pl.pallas_call(
        functools.partial(convolve_last_kernel, rows),
        out_shape=(own,) + (sent,) * count,
        scratch_shapes=convolve_scratch(shifted, 1, *slip.shape, components)
        + [pltpu.VMEM((1, height, length), jnp.float32)],
        compiler_params=params(),
        name="convolve_last",
    )(shifted, slip, first)


def add_kernel(own_ref, *refs):
    sent_refs, out_ref = refs[:-1], refs[-1]
    part, components, length = out_ref.shape
    rows = own_ref.shape[0] // components
    total = own_ref[...]
    for ref in sent_refs:
        unit = unit_of(ref[:, length:].astype(jnp.int32)[:, :1])
        total = total + ref[:, :length].astype(jnp.int32).astype(jnp.float32) * unit
    for comp in range(components):
        out_ref[:, comp, :] = total[comp * rows : comp * rows + part]


def add_up(own, sent, part, components):
    return pl.pallas_call(
        add_kernel,
        out_shape=jax.ShapeDtypeStruct((part, components, own.shape[1]), jnp.float32),
        compiler_params=params(),
        name="add_up",
    )(own, *sent)


def local(slip_rates, green_tiles, patch_slot):
    devices = lax.axis_size("patch")
    sites = lax.axis_size("site")
    chips = devices // 2
    patches, held, samples = slip_rates.shape
    components, lags = green_tiles.shape[2:]
    length = samples + lags
    part = held // 2
    rows = round_up(part, ROWS)
    assert chips == sites and sites & (sites - 1) == 0

    def over_patch(value, offset):
        return lax.ppermute(value, "patch", [(i, i ^ offset) for i in range(devices)])

    slips = slip_rates
    if rows > part:
        slips = slips.reshape(patches, 2, part, samples)
        slips = jnp.pad(slips, ((0, 0), (0, 0), (0, rows - part), (0, 0)))
        slips = slips.reshape(patches, 2 * rows, samples)
    greens = green_tiles[0]
    other, other_tiles = over_patch(slips, 1), over_patch(greens, 1)
    block, slots, greens = arrange_own(slips, patch_slot.reshape(1, -1), greens)
    block = arrange_other(other, other_tiles, block)

    share = 2 * max(1, patches // devices)
    capacity = round_up(4 * share, 16)
    pick, *pieces = route_tiles(slots, greens, other_tiles, chips, 2 * patches, capacity)
    arrived = []
    for index, piece in enumerate(pieces[1:]):
        hops = [(2 * index + 1, 2 * index + 2), (chips - 1, chips - 1)][index == len(pieces) - 2]
        arrived.append(
            lax.ppermute(piece, "patch", [(i, i ^ (2 * hops[i % 2])) for i in range(devices)])
        )

    blocks = {0: block}
    for step in [2**i for i in range(sites.bit_length())] + list(range(sites)):
        if 0 < step < sites and step not in blocks:
            low = step & -step
            blocks[step] = lax.ppermute(
                blocks[step - low], "site", [(i, i ^ low) for i in range(sites)]
            )
            if step == sites // 2:
                blocks[step] = pass_on(blocks[step], *arrived)
    pieces = pieces[:1]
    for piece in arrived:
        pieces += [piece, over_patch(piece, 1)]
    shifted = shift_tiles(pick, pieces, components)

    slips = [blocks[step] for step in range(sites)]
    first = convolve_first(shifted, slips[:-1], rows, components, length)
    sums = convolve_last(shifted, slips[-1], first, rows, components)
    sent = [over_patch(sums[step], 2 * step) for step in range(1, chips)]
    return add_up(sums[0], sent, part, components)[None]


def solution(mesh):
    in_specs = (P("patch", "site", None), P("site", "patch", None, None), P())
    out_specs = P("site", "patch", None, None)
    return jax.shard_map(local, mesh=mesh, in_specs=in_specs, out_specs=out_specs, check_vma=False)
```

profile of v0, /device:TPU:0, one launch (start us, length us, event | category | flops | bytes accessed | tf_op | source)
XLA Modules:
  0.0 26.9 jit_solution(12494203149057601946)
XLA Ops:
  0.0 0.5 %collective-permute-start = (bf16[32,2,1024]{2,1,0:T(2,128)(2,1)}, bf16[32,2,1024]{2,1,0:T(2,128)(2,1)S(1)}, u32[]{:S(2)}, u32[]{:S(2)}) collective-permute-start(bf16[32,2,1024]{2,1,0:T(2,128)(2,1)} %bitcast.3), channel_id=1, source_target_pairs={{0,1},{1,0},{2,3},{3,2},{4,5},{5,4},{6,7},{7,6},{8,9},{9,8},{10,11... | collective-permute-start | bytes 393224 | tf_op jit(solution)/shard_map/ppermute | solution.py:372
  0.5 0.1 collective-permute-start.5
  0.5 1.1 %arrange_own.1 = (bf16[128,512]{1,0:T(8,128)(2,1)S(1)}, s32[1,128]{1,0:T(1,128)S(1)}, bf16[32,2,1024]{2,1,0:T(2,128)(2,1)S(1)}) custom-call(bf16[16,16,256]{2,1,0:T(8,128)(2,1)} %slip_hbm.1, s32[1,128]{1,0:T(1,128)} %bitcast.5, bf16[32,2,1024]{2,1,0:T(2,128)(2,1)} %bitcast.4), custom_call_target="tpu_custom_call" | custom-call | tf_op jit(solution)/shard_map/arrange_own/pallas_call | solution.py:84
  1.6 0.0 collective-permute-done.other_ref.green_ref
  1.7 0.4 %collective-permute-done.5.slip_ref = bf16[16,16,256]{2,1,0:T(8,128)(2,1)S(1)} collective-permute-done((bf16[16,16,256]{2,1,0:T(8,128)(2,1)}, bf16[16,16,256]{2,1,0:T(8,128)(2,1)S(1)}, u32[]{:S(2)}, u32[]{:S(2)}) %collective-permute-start.5) | collective-permute-done | bytes 131104 | tf_op jit(solution)/shard_map/ppermute | solution.py:372
  2.0 0.2 arrange_other.1.refs_0_
  2.2 3.8 %collective-permute-start.6 = (bf16[128,512]{1,0:T(8,128)(2,1)S(1)}, bf16[128,512]{1,0:T(8,128)(2,1)S(1)}, u32[]{:S(2)}, u32[]{:S(2)}) collective-permute-start(bf16[128,512]{1,0:T(8,128)(2,1)S(1)} %arrange_other.1.refs_0_), channel_id=1, source_target_pairs={{0,16},{8,24},{16,0},{24,8},{1,17},{9,25},{17,1},{25,9},{2,18},{10... | collective-permute-start | bytes 393224 | tf_op jit(solution)/shard_map/ppermute | solution.py:398
  6.0 0.9 %route_tiles.1 = (bf16[64,32]{1,0:T(8,128)(2,1)S(1)}, bf16[32,1024]{1,0:T(8,128)(2,1)S(1)}, bf16[32,1024]{1,0:T(8,128)(2,1)S(1)}, bf16[16,1024]{1,0:T(8,128)(2,1)S(1)}) custom-call(s32[1,128]{1,0:T(1,128)S(1)} %get-tuple-element.16.slots_ref, bf16[32,2,1024]{2,1,0:T(2,128)(2,1)S(1)} %get-tuple-element.17.own_ref, ...), custom_call_target="tpu_custom_call" | custom-call | tf_op jit(solution)/shard_map/route_tiles/pallas_call | solution.py:183
  7.0 1.6 %collective-permute-start.1 = (bf16[32,1024]{1,0:T(8,128)(2,1)S(1)}, bf16[32,1024]{1,0:T(8,128)(2,1)S(1)}, u32[]{:S(2)}, u32[]{:S(2)}) collective-permute-start(bf16[32,1024]{1,0:T(8,128)(2,1)S(1)} %get-tuple-element.20), channel_id=1, source_target_pairs={{0,2},{1,5},{2,0},{3,7},{4,6},{5,1},{6,4},{7,3},{8,10},{9,13},{10,... | collective-permute-start | bytes 196616 | tf_op jit(solution)/shard_map/ppermute | solution.py:391
  8.5 1.5 %collective-permute-start.3 = (bf16[16,1024]{1,0:T(8,128)(2,1)S(1)}, bf16[16,1024]{1,0:T(8,128)(2,1)S(1)}, u32[]{:S(2)}, u32[]{:S(2)}) collective-permute-start(bf16[16,1024]{1,0:T(8,128)(2,1)S(1)} %get-tuple-element.21), channel_id=1, source_target_pairs={{0,6},{1,7},{2,4},{3,5},{4,2},{5,3},{6,0},{7,1},{8,14},{9,15},{10,... | collective-permute-start | bytes 98312 | tf_op jit(solution)/shard_map/ppermute | solution.py:391
  10.0 1.6 %collective-permute-start.8 = (bf16[128,512]{1,0:T(8,128)(2,1)S(1)}, bf16[128,512]{1,0:T(8,128)(2,1)S(1)}, u32[]{:S(2)}, u32[]{:S(2)}) collective-permute-start(bf16[128,512]{1,0:T(8,128)(2,1)S(1)} %arrange_other.1.refs_0_), channel_id=1, source_target_pairs={{0,8},{8,0},{16,24},{24,16},{1,9},{9,1},{17,25},{25,17},{2,10},{10... | collective-permute-start | bytes 393224 | tf_op jit(solution)/shard_map/ppermute | solution.py:398
  11.6 1.7 %collective-permute-done.3.refs_3_.refs_2_ = bf16[16,1024]{1,0:T(8,128)(2,1)S(1)} collective-permute-done((bf16[16,1024]{1,0:T(8,128)(2,1)S(1)}, bf16[16,1024]{1,0:T(8,128)(2,1)S(1)}, u32[]{:S(2)}, u32[]{:S(2)}) %collective-permute-start.3) | collective-permute-done | bytes 32800 | tf_op jit(solution)/shard_map/ppermute | solution.py:391
  13.4 0.0 collective-permute-done.1.refs_1_
  13.4 0.0 collective-permute-done.6.refs_0_
  13.4 1.6 %collective-permute-start.7 = (bf16[128,512]{1,0:T(8,128)(2,1)S(1)}, bf16[128,512]{1,0:T(8,128)(2,1)S(1)}, u32[]{:S(2)}, u32[]{:S(2)}) collective-permute-start(bf16[128,512]{1,0:T(8,128)(2,1)S(1)} %pass_on.1.refs_2_), channel_id=1, source_target_pairs={{0,8},{8,0},{16,24},{24,16},{1,9},{9,1},{17,25},{25,17},{2,10},{10... | collective-permute-start | bytes 393224 | tf_op jit(solution)/shard_map/ppermute | solution.py:398
  15.0 0.0 collective-permute-start.2
  15.0 0.5 %collective-permute-start.4 = (bf16[16,1024]{1,0:T(8,128)(2,1)S(1)}, bf16[16,1024]{1,0:T(8,128)(2,1)S(1)}, u32[]{:S(2)}, u32[]{:S(2)}) collective-permute-start(bf16[16,1024]{1,0:T(8,128)(2,1)S(1)} %collective-permute-done.3.refs_3_.refs_2_), channel_id=1, source_target_pairs={{0,1},{1,0},{2,3},{3,2},{4,5},{5,4},{6,7},{7,6},{8,9},{9,8},{10,11... | collective-permute-start | bytes 98312 | tf_op jit(solution)/shard_map/ppermute | solution.py:372
  15.5 0.9 %collective-permute-done.4.refs_4_ = bf16[16,1024]{1,0:T(8,128)(2,1)S(1)} collective-permute-done((bf16[16,1024]{1,0:T(8,128)(2,1)S(1)}, bf16[16,1024]{1,0:T(8,128)(2,1)S(1)}, u32[]{:S(2)}, u32[]{:S(2)}) %collective-permute-start.4) | collective-permute-done | bytes 32800 | tf_op jit(solution)/shard_map/ppermute | solution.py:372
  16.4 0.0 collective-permute-done.2.refs_2_
  16.4 0.8 %shift_tiles.1.shifted_ref = bf16[512,2304]{1,0:T(8,128)(2,1)S(1)} custom-call(bf16[64,32]{1,0:T(8,128)(2,1)S(1)} %get-tuple-element.18.pick_ref, bf16[32,1024]{1,0:T(8,128)(2,1)S(1)} %get-tuple-element.19.refs_0_, bf16[32,1024]{1,0:T(8,128)(2,1)S(1)} %collective-permute-done.1.refs_1_, bf16[32,1024]{1,0:T(8,128)(2,1)S(1)} %collective-permute-done.2.refs_2_, ...), custom_call_target="tpu_custom_call" | custom-call | tf_op jit(solution)/shard_map/shift_tiles/pallas_call | solution.py:235
  17.2 0.0 collective-permute-done.8.refs_1_
  17.2 1.3 %convolve_first.1.first_ref = f32[3,16,1280]{2,1,0:T(8,128)S(1)} custom-call(bf16[512,2304]{1,0:T(8,128)(2,1)S(1)} %shift_tiles.1.shifted_ref, bf16[128,512]{1,0:T(8,128)(2,1)S(1)} %arrange_other.1.refs_0_, bf16[128,512]{1,0:T(8,128)(2,1)S(1)} %collective-permute-done.8.refs_1_, bf16[128,512]{1,0:T(8,128)(2,1)S(1)} %pass_on.1.refs_2_), custom_call_target="tpu_custom_call" | custom-call | tf_op jit(solution)/shard_map/convolve_first/pallas_call | solution.py:289
  18.5 0.0 collective-permute-done.7.slip_ref
  18.5 0.7 %convolve_last.1 = (f32[16,1280]{1,0:T(8,128)S(1)}, s16[16,1408]{1,0:T(8,128)(2,1)S(1)}, s16[16,1408]{1,0:T(8,128)(2,1)S(1)}, s16[16,1408]{1,0:T(8,128)(2,1)S(1)}) custom-call(bf16[512,2304]{1,0:T(8,128)(2,1)S(1)} %shift_tiles.1.shifted_ref, bf16[128,512]{1,0:T(8,128)(2,1)S(1)} %collective-permute-done.7.slip_ref, f32[3,16,1280]{2,1,0:T(8,128)S(1)} %convolve_first.1.first_ref), custom_call_target="tpu_custom_call" | custom-call | tf_op jit(solution)/shard_map/convolve_last/pallas_call | solution.py:329
  19.2 1.6 %collective-permute-start.10 = (s16[16,1408]{1,0:T(8,128)(2,1)S(1)}, s16[16,1408]{1,0:T(8,128)(2,1)S(1)}, u32[]{:S(2)}, u32[]{:S(2)}) collective-permute-start(s16[16,1408]{1,0:T(8,128)(2,1)S(1)} %get-tuple-element.25), channel_id=1, source_target_pairs={{0,4},{1,5},{2,6},{3,7},{4,0},{5,1},{6,2},{7,3},{8,12},{9,13},{10,... | collective-permute-start | bytes 135176 | tf_op jit(solution)/shard_map/ppermute | solution.py:372
  20.8 1.3 %collective-permute-start.11 = (s16[16,1408]{1,0:T(8,128)(2,1)S(1)}, s16[16,1408]{1,0:T(8,128)(2,1)S(1)}, u32[]{:S(2)}, u32[]{:S(2)}) collective-permute-start(s16[16,1408]{1,0:T(8,128)(2,1)S(1)} %get-tuple-element.26), channel_id=1, source_target_pairs={{0,6},{1,7},{2,4},{3,5},{4,2},{5,3},{6,0},{7,1},{8,14},{9,15},{10,... | collective-permute-start | bytes 135176 | tf_op jit(solution)/shard_map/ppermute | solution.py:372
  22.1 0.6 %collective-permute-start.9 = (s16[16,1408]{1,0:T(8,128)(2,1)S(1)}, s16[16,1408]{1,0:T(8,128)(2,1)S(1)}, u32[]{:S(2)}, u32[]{:S(2)}) collective-permute-start(s16[16,1408]{1,0:T(8,128)(2,1)S(1)} %get-tuple-element.24), channel_id=1, source_target_pairs={{0,2},{1,3},{2,0},{3,1},{4,6},{5,7},{6,4},{7,5},{8,10},{9,11},{10,... | collective-permute-start | bytes 135176 | tf_op jit(solution)/shard_map/ppermute | solution.py:372
  22.8 0.6 %collective-permute-done.10.refs_1_ = s16[16,1408]{1,0:T(8,128)(2,1)S(1)} collective-permute-done((s16[16,1408]{1,0:T(8,128)(2,1)S(1)}, s16[16,1408]{1,0:T(8,128)(2,1)S(1)}, u32[]{:S(2)}, u32[]{:S(2)}) %collective-permute-start.10) | collective-permute-done | bytes 45088 | tf_op jit(solution)/shard_map/ppermute | solution.py:372
  23.3 2.5 %collective-permute-done.11.refs_2_ = s16[16,1408]{1,0:T(8,128)(2,1)S(1)} collective-permute-done((s16[16,1408]{1,0:T(8,128)(2,1)S(1)}, s16[16,1408]{1,0:T(8,128)(2,1)S(1)}, u32[]{:S(2)}, u32[]{:S(2)}) %collective-permute-start.11) | collective-permute-done | bytes 45088 | tf_op jit(solution)/shard_map/ppermute | solution.py:372
  25.8 0.4 %collective-permute-done.9.refs_0_ = s16[16,1408]{1,0:T(8,128)(2,1)S(1)} collective-permute-done((s16[16,1408]{1,0:T(8,128)(2,1)S(1)}, s16[16,1408]{1,0:T(8,128)(2,1)S(1)}, u32[]{:S(2)}, u32[]{:S(2)}) %collective-permute-start.9) | collective-permute-done | bytes 45088 | tf_op jit(solution)/shard_map/ppermute | solution.py:372
  26.2 0.7 %add_up.1 = f32[8,2,1280]{2,1,0:T(2,128)} custom-call(f32[16,1280]{1,0:T(8,128)S(1)} %get-tuple-element.23.own_ref, s16[16,1408]{1,0:T(8,128)(2,1)S(1)} %collective-permute-done.9.refs_0_, s16[16,1408]{1,0:T(8,128)(2,1)S(1)} %collective-permute-done.10.refs_1_, s16[16,1408]{1,0:T(8,128)(2,1)S(1)} %collective-permute-done.11.refs_2_), custom_call_target="tpu_custom_call" | custom-call | tf_op jit(solution)/shard_map/add_up/pallas_call | solution.py:352
  (1 shorter events, 0.0 us)
Async XLA Ops:
  0.0 1.6 %collective-permute-start = (bf16[32,2,1024]{2,1,0:T(2,128)(2,1)}, bf16[32,2,1024]{2,1,0:T(2,128)(2,1)S(1)}, u32[]{:S(2)}, u32[]{:S(2)}) collective-permute-start(bf16[32,2,1024]{2,1,0:T(2,128)(2,1)} %bitcast.3), channel_id=1, source_target_pairs={{0,1},{1,0},{2,3},{3,2},{4,5},{5,4},{6,7},{7,6},{8,9},{9,8},{10,11... | collective-permute-start | bytes 393224 | tf_op jit(solution)/shard_map/ppermute | solution.py:372
  0.5 1.6 %collective-permute-start.5 = (bf16[16,16,256]{2,1,0:T(8,128)(2,1)}, bf16[16,16,256]{2,1,0:T(8,128)(2,1)S(1)}, u32[]{:S(2)}, u32[]{:S(2)}) collective-permute-start(bf16[16,16,256]{2,1,0:T(8,128)(2,1)} %slip_hbm.1), channel_id=1, source_target_pairs={{0,1},{1,0},{2,3},{3,2},{4,5},{5,4},{6,7},{7,6},{8,9},{9,8},{10,11... | collective-permute-start | bytes 393224 | tf_op jit(solution)/shard_map/ppermute | solution.py:372
  2.2 11.2 %collective-permute-start.6 = (bf16[128,512]{1,0:T(8,128)(2,1)S(1)}, bf16[128,512]{1,0:T(8,128)(2,1)S(1)}, u32[]{:S(2)}, u32[]{:S(2)}) collective-permute-start(bf16[128,512]{1,0:T(8,128)(2,1)S(1)} %arrange_other.1.refs_0_), channel_id=1, source_target_pairs={{0,16},{8,24},{16,0},{24,8},{1,17},{9,25},{17,1},{25,9},{2,18},{10... | collective-permute-start | bytes 393224 | tf_op jit(solution)/shard_map/ppermute | solution.py:398
  7.0 6.4 %collective-permute-start.1 = (bf16[32,1024]{1,0:T(8,128)(2,1)S(1)}, bf16[32,1024]{1,0:T(8,128)(2,1)S(1)}, u32[]{:S(2)}, u32[]{:S(2)}) collective-permute-start(bf16[32,1024]{1,0:T(8,128)(2,1)S(1)} %get-tuple-element.20), channel_id=1, source_target_pairs={{0,2},{1,5},{2,0},{3,7},{4,6},{5,1},{6,4},{7,3},{8,10},{9,13},{10,... | collective-permute-start | bytes 196616 | tf_op jit(solution)/shard_map/ppermute | solution.py:391
  8.5 4.8 %collective-permute-start.3 = (bf16[16,1024]{1,0:T(8,128)(2,1)S(1)}, bf16[16,1024]{1,0:T(8,128)(2,1)S(1)}, u32[]{:S(2)}, u32[]{:S(2)}) collective-permute-start(bf16[16,1024]{1,0:T(8,128)(2,1)S(1)} %get-tuple-element.21), channel_id=1, source_target_pairs={{0,6},{1,7},{2,4},{3,5},{4,2},{5,3},{6,0},{7,1},{8,14},{9,15},{10,... | collective-permute-start | bytes 98312 | tf_op jit(solution)/shard_map/ppermute | solution.py:391
  10.0 7.2 %collective-permute-start.8 = (bf16[128,512]{1,0:T(8,128)(2,1)S(1)}, bf16[128,512]{1,0:T(8,128)(2,1)S(1)}, u32[]{:S(2)}, u32[]{:S(2)}) collective-permute-start(bf16[128,512]{1,0:T(8,128)(2,1)S(1)} %arrange_other.1.refs_0_), channel_id=1, source_target_pairs={{0,8},{8,0},{16,24},{24,16},{1,9},{9,1},{17,25},{25,17},{2,10},{10... | collective-permute-start | bytes 393224 | tf_op jit(solution)/shard_map/ppermute | solution.py:398
  13.4 5.1 %collective-permute-start.7 = (bf16[128,512]{1,0:T(8,128)(2,1)S(1)}, bf16[128,512]{1,0:T(8,128)(2,1)S(1)}, u32[]{:S(2)}, u32[]{:S(2)}) collective-permute-start(bf16[128,512]{1,0:T(8,128)(2,1)S(1)} %pass_on.1.refs_2_), channel_id=1, source_target_pairs={{0,8},{8,0},{16,24},{24,16},{1,9},{9,1},{17,25},{25,17},{2,10},{10... | collective-permute-start | bytes 393224 | tf_op jit(solution)/shard_map/ppermute | solution.py:398
  15.0 1.4 %collective-permute-start.2 = (bf16[32,1024]{1,0:T(8,128)(2,1)S(1)}, bf16[32,1024]{1,0:T(8,128)(2,1)S(1)}, u32[]{:S(2)}, u32[]{:S(2)}) collective-permute-start(bf16[32,1024]{1,0:T(8,128)(2,1)S(1)} %collective-permute-done.1.refs_1_), channel_id=1, source_target_pairs={{0,1},{1,0},{2,3},{3,2},{4,5},{5,4},{6,7},{7,6},{8,9},{9,8},{10,11... | collective-permute-start | bytes 196616 | tf_op jit(solution)/shard_map/ppermute | solution.py:372
  15.0 1.4 %collective-permute-start.4 = (bf16[16,1024]{1,0:T(8,128)(2,1)S(1)}, bf16[16,1024]{1,0:T(8,128)(2,1)S(1)}, u32[]{:S(2)}, u32[]{:S(2)}) collective-permute-start(bf16[16,1024]{1,0:T(8,128)(2,1)S(1)} %collective-permute-done.3.refs_3_.refs_2_), channel_id=1, source_target_pairs={{0,1},{1,0},{2,3},{3,2},{4,5},{5,4},{6,7},{7,6},{8,9},{9,8},{10,11... | collective-permute-start | bytes 98312 | tf_op jit(solution)/shard_map/ppermute | solution.py:372
  19.2 4.1 %collective-permute-start.10 = (s16[16,1408]{1,0:T(8,128)(2,1)S(1)}, s16[16,1408]{1,0:T(8,128)(2,1)S(1)}, u32[]{:S(2)}, u32[]{:S(2)}) collective-permute-start(s16[16,1408]{1,0:T(8,128)(2,1)S(1)} %get-tuple-element.25), channel_id=1, source_target_pairs={{0,4},{1,5},{2,6},{3,7},{4,0},{5,1},{6,2},{7,3},{8,12},{9,13},{10,... | collective-permute-start | bytes 135176 | tf_op jit(solution)/shard_map/ppermute | solution.py:372
  20.8 5.0 %collective-permute-start.11 = (s16[16,1408]{1,0:T(8,128)(2,1)S(1)}, s16[16,1408]{1,0:T(8,128)(2,1)S(1)}, u32[]{:S(2)}, u32[]{:S(2)}) collective-permute-start(s16[16,1408]{1,0:T(8,128)(2,1)S(1)} %get-tuple-element.26), channel_id=1, source_target_pairs={{0,6},{1,7},{2,4},{3,5},{4,2},{5,3},{6,0},{7,1},{8,14},{9,15},{10,... | collective-permute-start | bytes 135176 | tf_op jit(solution)/shard_map/ppermute | solution.py:372
  22.1 4.0 %collective-permute-start.9 = (s16[16,1408]{1,0:T(8,128)(2,1)S(1)}, s16[16,1408]{1,0:T(8,128)(2,1)S(1)}, u32[]{:S(2)}, u32[]{:S(2)}) collective-permute-start(s16[16,1408]{1,0:T(8,128)(2,1)S(1)} %get-tuple-element.24), channel_id=1, source_target_pairs={{0,2},{1,3},{2,0},{3,1},{4,6},{5,7},{6,4},{7,5},{8,10},{9,11},{10,... | collective-permute-start | bytes 135176 | tf_op jit(solution)/shard_map/ppermute | solution.py:372
where the time goes:
time: 27.1 us; the launch traced here: 26.9 us
  starting transfers between devices  14.7 us (54%)
  waiting for transfers between devices  6.38 us (24%)
  Pallas kernels  5.81 us (21%)
    ppermute x3, starting transfers between devices, local(): lax.ppermute(blocks[step - low], 'site', [(i, i ^ low) for i in range(sit...  7.05 us
    ppermute x7, waiting for transfers between devices, over_patch(): lax.ppermute(value, 'patch', [(i, i ^ offset) for i in range(devices)])  4.62 us
    ppermute x7, starting transfers between devices, over_patch(): lax.ppermute(value, 'patch', [(i, i ^ offset) for i in range(devices)])  4.57 us
    ppermute x2, starting transfers between devices, local(): lax.ppermute(piece, 'patch', [(i, i ^ 2 * hops[i % 2]) for i in range(dev...  3.05 us
    ppermute x2, waiting for transfers between devices, local(): lax.ppermute(piece, 'patch', [(i, i ^ 2 * hops[i % 2]) for i in range(dev...  1.75 us
    pallas_call x1, Pallas kernels, convolve_first(): pl.pallas_call(functools.partial(convolve_first_kernel, rows), out_shape=...  1.27 us
    pallas_call x1, Pallas kernels, arrange_own(): pl.pallas_call(arrange_own_kernel, in_specs=[pl.BlockSpec(memory_space=pl...  1.13 us
    pallas_call x1, Pallas kernels, route_tiles(): pl.pallas_call(functools.partial(route_kernel, chips, per_chip, capacity)...  0.93 us
  transfers between devices with their start and end apart: 12, of which 6 were waited for; matrix products, arithmetic and copies ran while one was open for 0% of the time, Pallas kernels for 15%

commit v1 on v0

--- a/solution.py
+++ b/solution.py
@@ -52,7 +52,19 @@
 
 
 def arrange_own_kernel(
-    slip_hbm, slots_hbm, green_hbm, out_ref, slots_ref, green_ref, slip_ref, sems
+    chips,
+    per_chip,
+    capacity,
+    slip_hbm,
+    slots_hbm,
+    green_hbm,
+    out_ref,
+    send_ref,
+    pick_ref,
+    green_ref,
+    slip_ref,
+    slots_ref,
+    sems,
 ):
     fetch_slips = pltpu.make_async_copy(slip_hbm, slip_ref, sems.at[0])
     fetch_slots = pltpu.make_async_copy(slots_hbm, slots_ref, sems.at[1])
@@ -60,10 +72,11 @@
     fetch_slips.start()
     fetch_slots.start()
     fetch_greens.start()
+    fetch_slots.wait()
+    mark_tiles(chips, per_chip, capacity, green_hbm.shape[0], slots_ref, send_ref, pick_ref)
     fetch_slips.wait()
     core = lax.rem(lax.axis_index("patch"), 2)
     arrange_half(slip_ref, out_ref, core, core)
-    fetch_slots.wait()
     fetch_greens.wait()
 
 
@@ -76,21 +89,24 @@
     return [pltpu.with_memory_space_constraint(value, pltpu.HBM) for value in values]
 
 
-def arrange_own(slips, slots, greens):
+def arrange_own(slips, slots, greens, chips, per_chip, capacity):
     patches, both, samples = slips.shape
+    width = greens.shape[0]
     block = jax.ShapeDtypeStruct(
         (samples // BLOCK * both // 2, 2 * patches * BLOCK), jnp.bfloat16
     )
     return pl.pallas_call(
-        arrange_own_kernel,
+        functools.partial(arrange_own_kernel, chips, per_chip, capacity),
         in_specs=[pl.BlockSpec(memory_space=pltpu.HBM)] * 3,
         out_shape=(
             block,
-            jax.ShapeDtypeStruct(slots.shape, slots.dtype),
+            jax.ShapeDtypeStruct((chips * capacity, 2 * width), jnp.bfloat16),
+            jax.ShapeDtypeStruct((chips * capacity, per_chip), jnp.bfloat16),
             jax.ShapeDtypeStruct(greens.shape, greens.dtype),
         ),
         scratch_shapes=[
             pltpu.VMEM(slips.shape, slips.dtype),
+            pltpu.VMEM(slots.shape, slots.dtype),
             pltpu.SemaphoreType.DMA((3,)),
         ],
         compiler_params=params(),
@@ -123,8 +139,7 @@
     return condition.astype(jnp.float32).astype(jnp.bfloat16)
 
 
-def route_kernel(chips, per_chip, capacity, slots_ref, own_ref, other_ref, pick_ref, *out_refs):
-    width, components, lags = own_ref.shape
+def mark_tiles(chips, per_chip, capacity, width, slots_ref, send_ref, pick_ref):
     half = capacity // 2
     count = slots_ref.shape[1]
     own = lax.axis_index("patch")
@@ -140,23 +155,9 @@
     code = jnp.where(mine, target * capacity + rank, -1)
     code_pick = one_hot(lax.broadcasted_iota(jnp.int32, (chips * capacity, count), 0) == code)
     slot_pick = one_hot(lax.broadcasted_iota(jnp.int32, (2 * width, count), 0) == place)
-    pick = lax.dot_general(
+    send_ref[...] = lax.dot_general(
         code_pick, slot_pick, (((1,), (1,)), ((), ())), preferred_element_type=jnp.float32
     ).astype(jnp.bfloat16)
-    tiles = jnp.concatenate([own_ref[...], other_ref[...]], axis=0).astype(jnp.float32)
-    by_comp = []
-    for comp in range(components):
-        both = tiles[:, comp, :].astype(jnp.bfloat16)
-        chosen = jnp.dot(pick, both, preferred_element_type=jnp.float32)
-        chosen = [chosen[step * capacity : (step + 1) * capacity] for step in range(chips)]
-        last = chosen[-1]
-        sent = [chosen[0]]
-        for step in range(1, chips - 1, 2):
-            sent.append(jnp.where(core == 0, chosen[step], chosen[step + 1]))
-        sent.append(jnp.where(core == 0, last[:half], last[half:]))
-        by_comp.append(sent)
-    for values, out_ref in zip(zip(*by_comp), out_refs):
-        out_ref[...] = jnp.concatenate(values, axis=0).astype(jnp.bfloat16)
     here = pltpu.roll(slots, lax.rem(count - chip * per_chip, count), 1)[:, :per_chip]
     owner = (here // (2 * width)) ^ chip
     marks = lax.broadcasted_iota(jnp.int32, (round_up(chips, 16), per_chip), 0) == owner
@@ -175,17 +176,37 @@
     pick_ref[...] = one_hot(lax.broadcasted_iota(jnp.int32, pick_ref.shape, 0) == code)
 
 
-def route_tiles(slots, own, other, chips, per_chip, capacity):
+def route_kernel(chips, send_ref, own_ref, other_ref, *out_refs):
+    capacity = send_ref.shape[0] // chips
+    half = capacity // 2
+    core = lax.rem(lax.axis_index("patch"), 2)
+    tiles = jnp.concatenate([own_ref[...], other_ref[...]], axis=0).astype(jnp.float32)
+    by_comp = []
+    for comp in range(own_ref.shape[1]):
+        both = tiles[:, comp, :].astype(jnp.bfloat16)
+        chosen = jnp.dot(send_ref[...], both, preferred_element_type=jnp.float32)
+        chosen = [chosen[step * capacity : (step + 1) * capacity] for step in range(chips)]
+        last = chosen[-1]
+        sent = [chosen[0]]
+        for step in range(1, chips - 1, 2):
+            sent.append(jnp.where(core == 0, chosen[step], chosen[step + 1]))
+        sent.append(jnp.where(core == 0, last[:half], last[half:]))
+        by_comp.append(sent)
+    for values, out_ref in zip(zip(*by_comp), out_refs):
+        out_ref[...] = jnp.concatenate(values, axis=0).astype(jnp.bfloat16)
+
+
+def route_tiles(send, own, other, chips):
     components, lags = own.shape[1:]
-    pick = jax.ShapeDtypeStruct((chips * capacity, per_chip), jnp.bfloat16)
-    shape = jax.ShapeDtypeStruct((components * capacity, lags), jnp.bfloat16)
-    part = jax.ShapeDtypeStruct((components * capacity // 2, lags), jnp.bfloat16)
-    return pl.pallas_call(
-        functools.partial(route_kernel, chips, per_chip, capacity),
-        out_shape=(pick,) + (shape,) * (chips // 2) + (part,),
+    rows = components * send.shape[0] // chips
+    shape = jax.ShapeDtypeStruct((rows, lags), jnp.bfloat16)
+    part = jax.ShapeDtypeStruct((rows // 2, lags), jnp.bfloat16)
+    return pl.pallas_call(
+        functools.partial(route_kernel, chips),
+        out_shape=(shape,) * (chips // 2) + (part,),
         compiler_params=params(),
         name="route_tiles",
-    )(slots, own, other)
+    )(send, own, other)
 
 
 def pass_on(value, *others):
@@ -378,18 +399,24 @@
         slips = slips.reshape(patches, 2 * rows, samples)
     greens = green_tiles[0]
     other, other_tiles = over_patch(slips, 1), over_patch(greens, 1)
-    block, slots, greens = arrange_own(slips, patch_slot.reshape(1, -1), greens)
-    block = arrange_other(other, other_tiles, block)
-
     share = 2 * max(1, patches // devices)
     capacity = round_up(4 * share, 16)
-    pick, *pieces = route_tiles(slots, greens, other_tiles, chips, 2 * patches, capacity)
+    block, send, pick, greens = arrange_own(
+        slips, patch_slot.reshape(1, -1), greens, chips, 2 * patches, capacity
+    )
+    block = arrange_other(other, other_tiles, block)
+
+    pieces = list(route_tiles(send, greens, other_tiles, chips))
     arrived = []
     for index, piece in enumerate(pieces[1:]):
         hops = [(2 * index + 1, 2 * index + 2), (chips - 1, chips - 1)][index == len(pieces) - 2]
         arrived.append(
             lax.ppermute(piece, "patch", [(i, i ^ (2 * hops[i % 2])) for i in range(devices)])
         )
+
+    pieces = pieces[:1]
+    for piece in arrived:
+        pieces += [piece, over_patch(piece, 1)]
 
     blocks = {0: block}
     for step in [2**i for i in range(sites.bit_length())] + list(range(sites)):
@@ -399,16 +426,14 @@
                 blocks[step - low], "site", [(i, i ^ low) for i in range(sites)]
             )
             if step == sites // 2:
-                blocks[step] = pass_on(blocks[step], *arrived)
-    pieces = pieces[:1]
-    for piece in arrived:
-        pieces += [piece, over_patch(piece, 1)]
+                blocks[step] = pass_on(blocks[step], *pieces[1:])
     shifted = shift_tiles(pick, pieces, components)
 
     slips = [blocks[step] for step in range(sites)]
     first = convolve_first(shifted, slips[:-1], rows, components, length)
     sums = convolve_last(shifted, slips[-1], first, rows, components)
-    sent = [over_patch(sums[step], 2 * step) for step in range(1, chips)]
+    order = [1, chips - 1] + list(range(2, chips - 1))
+    sent = [over_patch(sums[step], 2 * step) for step in order]
     return add_up(sums[0], sent, part, components)[None]
 
 

time: 27.1 us -> 29.7 us (1.096)
  waiting for transfers between devices: 6.38 us -> 9.66 us
  starting transfers between devices: 14.7 us -> 14 us
    ppermute x3, waiting for transfers between devices: 0.01 us -> 3.77 us  [local(): lax.ppermute(blocks[step - low], 'site', [(i, i ^ low) for i in range(sit...]
    ppermute x7, waiting for transfers between devices: 4.62 us -> 2.57 us  [over_patch(): lax.ppermute(value, 'patch', [(i, i ^ offset) for i in range(devices)])]
    ppermute x2, waiting for transfers between devices: 1.75 us -> 3.32 us  [local(): lax.ppermute(piece, 'patch', [(i, i ^ 2 * hops[i % 2]) for i in range(dev...]
    ppermute x3, starting transfers between devices: 7.05 us -> 5.48 us  [local(): lax.ppermute(blocks[step - low], 'site', [(i, i ^ low) for i in range(sit...]
    ppermute x2, starting transfers between devices: 3.05 us -> 4.49 us  [local(): lax.ppermute(piece, 'patch', [(i, i ^ 2 * hops[i % 2]) for i in range(dev...]
    ppermute x7, starting transfers between devices: 4.57 us -> 4.07 us  [over_patch(): lax.ppermute(value, 'patch', [(i, i ^ offset) for i in range(devices)])]
where the time goes in v1:
time: 29.7 us; the launch traced here: 29.6 us
  starting transfers between devices  14 us (47%)
  waiting for transfers between devices  9.66 us (33%)
  Pallas kernels  5.79 us (19%)
    ppermute x3, starting transfers between devices, local(): lax.ppermute(blocks[step - low], 'site', [(i, i ^ low) for i in range(sit...  5.48 us
    ppermute x2, starting transfers between devices, local(): lax.ppermute(piece, 'patch', [(i, i ^ 2 * hops[i % 2]) for i in range(dev...  4.49 us
    ppermute x7, starting transfers between devices, over_patch(): lax.ppermute(value, 'patch', [(i, i ^ offset) for i in range(devices)])  4.07 us
    ppermute x3, waiting for transfers between devices, local(): lax.ppermute(blocks[step - low], 'site', [(i, i ^ low) for i in range(sit...  3.77 us
    ppermute x2, waiting for transfers between devices, local(): lax.ppermute(piece, 'patch', [(i, i ^ 2 * hops[i % 2]) for i in range(dev...  3.32 us
    ppermute x7, waiting for transfers between devices, over_patch(): lax.ppermute(value, 'patch', [(i, i ^ offset) for i in range(devices)])  2.57 us
    pallas_call x1, Pallas kernels, convolve_first(): pl.pallas_call(functools.partial(convolve_first_kernel, rows), out_shape=...  1.27 us
    pallas_call x1, Pallas kernels, arrange_own(): pl.pallas_call(functools.partial(arrange_own_kernel, chips, per_chip, cap...  1.21 us
  transfers between devices with their start and end apart: 12, of which 6 were waited for; matrix products, arithmetic and copies ran while one was open for 0% of the time, Pallas kernels for 15%

profile of v1, /device:TPU:0, one launch (start us, length us, event | category | flops | bytes accessed | tf_op | source)
XLA Modules:
  0.0 29.6 jit_solution(3647910701594126944)
XLA Ops:
  0.0 0.5 %collective-permute-start = (bf16[32,2,1024]{2,1,0:T(2,128)(2,1)}, bf16[32,2,1024]{2,1,0:T(2,128)(2,1)S(1)}, u32[]{:S(2)}, u32[]{:S(2)}) collective-permute-start(bf16[32,2,1024]{2,1,0:T(2,128)(2,1)} %bitcast.3), channel_id=1, source_target_pairs={{0,1},{1,0},{2,3},{3,2},{4,5},{5,4},{6,7},{7,6},{8,9},{9,8},{10,11... | collective-permute-start | bytes 393224 | tf_op jit(solution)/shard_map/ppermute | solution.py:393
  0.5 0.1 collective-permute-start.5
  0.5 1.2 %arrange_own.1 = (bf16[128,512]{1,0:T(8,128)(2,1)S(1)}, bf16[64,64]{1,0:T(8,128)(2,1)S(1)}, bf16[64,32]{1,0:T(8,128)(2,1)S(1)}, bf16[32,2,1024]{2,1,0:T(2,128)(2,1)S(1)}) custom-call(bf16[16,16,256]{2,1,0:T(8,128)(2,1)} %slip_hbm.1, s32[1,128]{1,0:T(1,128)} %bitcast.5, bf16[32,2,1024]{2,1,0:T(2,128)(2,1)} %bitcast.4), custom_call_target="tpu_custom_call" | custom-call | tf_op jit(solution)/shard_map/arrange_own/pallas_call | solution.py:98
  1.7 0.0 collective-permute-done.other_ref.green_ref
  1.7 0.8 %route_tiles.1 = (bf16[32,1024]{1,0:T(8,128)(2,1)S(1)}, bf16[32,1024]{1,0:T(8,128)(2,1)S(1)}, bf16[16,1024]{1,0:T(8,128)(2,1)S(1)}) custom-call(bf16[64,64]{1,0:T(8,128)(2,1)S(1)} %get-tuple-element.17.send_ref, bf16[32,2,1024]{2,1,0:T(2,128)(2,1)S(1)} %get-tuple-element.18.own_ref, bf16[32,2,1024]{2,1,0:T(2,128)(2,1)S(1)} %collective-permute-done.other_ref.green_ref), custom_call_target="tpu_custom_call" | custom-call | tf_op jit(solution)/shard_map/route_tiles/pallas_call | solution.py:204
  2.6 3.0 %collective-permute-start.1 = (bf16[32,1024]{1,0:T(8,128)(2,1)S(1)}, bf16[32,1024]{1,0:T(8,128)(2,1)S(1)}, u32[]{:S(2)}, u32[]{:S(2)}) collective-permute-start(bf16[32,1024]{1,0:T(8,128)(2,1)S(1)} %get-tuple-element.20), channel_id=1, source_target_pairs={{0,2},{1,5},{2,0},{3,7},{4,6},{5,1},{6,4},{7,3},{8,10},{9,13},{10,... | collective-permute-start | bytes 196616 | tf_op jit(solution)/shard_map/ppermute | solution.py:414
  5.6 0.0 collective-permute-done.5.slip_ref
  5.6 0.2 arrange_other.1.refs_0_
  5.8 2.7 %collective-permute-start.6 = (bf16[128,512]{1,0:T(8,128)(2,1)S(1)}, bf16[128,512]{1,0:T(8,128)(2,1)S(1)}, u32[]{:S(2)}, u32[]{:S(2)}) collective-permute-start(bf16[128,512]{1,0:T(8,128)(2,1)S(1)} %arrange_other.1.refs_0_), channel_id=1, source_target_pairs={{0,16},{8,24},{16,0},{24,8},{1,17},{9,25},{17,1},{25,9},{2,18},{10... | collective-permute-start | bytes 393224 | tf_op jit(solution)/shard_map/ppermute | solution.py:425
  8.4 1.5 %collective-permute-start.3 = (bf16[16,1024]{1,0:T(8,128)(2,1)S(1)}, bf16[16,1024]{1,0:T(8,128)(2,1)S(1)}, u32[]{:S(2)}, u32[]{:S(2)}) collective-permute-start(bf16[16,1024]{1,0:T(8,128)(2,1)S(1)} %get-tuple-element.21), channel_id=1, source_target_pairs={{0,6},{1,7},{2,4},{3,5},{4,2},{5,3},{6,0},{7,1},{8,14},{9,15},{10,... | collective-permute-start | bytes 98312 | tf_op jit(solution)/shard_map/ppermute | solution.py:414
  9.9 0.0 collective-permute-done.1.refs_1_
  9.9 0.0 collective-permute-start.2
  9.9 3.3 %collective-permute-done.3.refs_3_ = bf16[16,1024]{1,0:T(8,128)(2,1)S(1)} collective-permute-done((bf16[16,1024]{1,0:T(8,128)(2,1)S(1)}, bf16[16,1024]{1,0:T(8,128)(2,1)S(1)}, u32[]{:S(2)}, u32[]{:S(2)}) %collective-permute-start.3) | collective-permute-done | bytes 32800 | tf_op jit(solution)/shard_map/ppermute | solution.py:414
  13.3 0.0 collective-permute-start.4
  13.3 1.6 %collective-permute-start.8 = (bf16[128,512]{1,0:T(8,128)(2,1)S(1)}, bf16[128,512]{1,0:T(8,128)(2,1)S(1)}, u32[]{:S(2)}, u32[]{:S(2)}) collective-permute-start(bf16[128,512]{1,0:T(8,128)(2,1)S(1)} %arrange_other.1.refs_0_), channel_id=1, source_target_pairs={{0,8},{8,0},{16,24},{24,16},{1,9},{9,1},{17,25},{25,17},{2,10},{10... | collective-permute-start | bytes 393224 | tf_op jit(solution)/shard_map/ppermute | solution.py:425
  14.8 0.0 collective-permute-done.4.refs_4_
  14.8 0.0 collective-permute-done.2.refs_2_
  14.8 0.0 collective-permute-done.6.refs_0_
  14.9 1.2 %collective-permute-start.7 = (bf16[128,512]{1,0:T(8,128)(2,1)S(1)}, bf16[128,512]{1,0:T(8,128)(2,1)S(1)}, u32[]{:S(2)}, u32[]{:S(2)}) collective-permute-start(bf16[128,512]{1,0:T(8,128)(2,1)S(1)} %pass_on.1.refs_2_), channel_id=1, source_target_pairs={{0,8},{8,0},{16,24},{24,16},{1,9},{9,1},{17,25},{25,17},{2,10},{10... | collective-permute-start | bytes 393224 | tf_op jit(solution)/shard_map/ppermute | solution.py:425
  16.1 0.8 %shift_tiles.1.shifted_ref = bf16[512,2304]{1,0:T(8,128)(2,1)S(1)} custom-call(bf16[64,32]{1,0:T(8,128)(2,1)S(1)} %get-tuple-element.16.pick_ref, bf16[32,1024]{1,0:T(8,128)(2,1)S(1)} %get-tuple-element.19.refs_0_, bf16[32,1024]{1,0:T(8,128)(2,1)S(1)} %collective-permute-done.1.refs_1_, bf16[32,1024]{1,0:T(8,128)(2,1)S(1)} %collective-permute-done.2.refs_2_, ...), custom_call_target="tpu_custom_call" | custom-call | tf_op jit(solution)/shard_map/shift_tiles/pallas_call | solution.py:256
  16.9 2.6 %collective-permute-done.8.refs_1_ = bf16[128,512]{1,0:T(8,128)(2,1)S(1)} collective-permute-done((bf16[128,512]{1,0:T(8,128)(2,1)S(1)}, bf16[128,512]{1,0:T(8,128)(2,1)S(1)}, u32[]{:S(2)}, u32[]{:S(2)}) %collective-permute-start.8) | collective-permute-done | bytes 131104 | tf_op jit(solution)/shard_map/ppermute | solution.py:425
  19.6 1.3 %convolve_first.1.first_ref = f32[3,16,1280]{2,1,0:T(8,128)S(1)} custom-call(bf16[512,2304]{1,0:T(8,128)(2,1)S(1)} %shift_tiles.1.shifted_ref, bf16[128,512]{1,0:T(8,128)(2,1)S(1)} %arrange_other.1.refs_0_, bf16[128,512]{1,0:T(8,128)(2,1)S(1)} %collective-permute-done.8.refs_1_, bf16[128,512]{1,0:T(8,128)(2,1)S(1)} %pass_on.1.refs_2_), custom_call_target="tpu_custom_call" | custom-call | tf_op jit(solution)/shard_map/convolve_first/pallas_call | solution.py:310
  20.8 1.2 %collective-permute-done.7.slip_ref = bf16[128,512]{1,0:T(8,128)(2,1)S(1)} collective-permute-done((bf16[128,512]{1,0:T(8,128)(2,1)S(1)}, bf16[128,512]{1,0:T(8,128)(2,1)S(1)}, u32[]{:S(2)}, u32[]{:S(2)}) %collective-permute-start.7) | collective-permute-done | bytes 131104 | tf_op jit(solution)/shard_map/ppermute | solution.py:425
  22.0 0.7 %convolve_last.1 = (f32[16,1280]{1,0:T(8,128)S(1)}, s16[16,1408]{1,0:T(8,128)(2,1)S(1)}, s16[16,1408]{1,0:T(8,128)(2,1)S(1)}, s16[16,1408]{1,0:T(8,128)(2,1)S(1)}) custom-call(bf16[512,2304]{1,0:T(8,128)(2,1)S(1)} %shift_tiles.1.shifted_ref, bf16[128,512]{1,0:T(8,128)(2,1)S(1)} %collective-permute-done.7.slip_ref, f32[3,16,1280]{2,1,0:T(8,128)S(1)} %convolve_first.1.first_ref), custom_call_target="tpu_custom_call" | custom-call | tf_op jit(solution)/shard_map/convolve_last/pallas_call | solution.py:350
  22.7 1.6 %collective-permute-start.10 = (s16[16,1408]{1,0:T(8,128)(2,1)S(1)}, s16[16,1408]{1,0:T(8,128)(2,1)S(1)}, u32[]{:S(2)}, u32[]{:S(2)}) collective-permute-start(s16[16,1408]{1,0:T(8,128)(2,1)S(1)} %get-tuple-element.25), channel_id=1, source_target_pairs={{0,6},{1,7},{2,4},{3,5},{4,2},{5,3},{6,0},{7,1},{8,14},{9,15},{10,... | collective-permute-start | bytes 135176 | tf_op jit(solution)/shard_map/ppermute | solution.py:393
  24.3 0.5 %collective-permute-start.11 = (s16[16,1408]{1,0:T(8,128)(2,1)S(1)}, s16[16,1408]{1,0:T(8,128)(2,1)S(1)}, u32[]{:S(2)}, u32[]{:S(2)}) collective-permute-start(s16[16,1408]{1,0:T(8,128)(2,1)S(1)} %get-tuple-element.26), channel_id=1, source_target_pairs={{0,4},{1,5},{2,6},{3,7},{4,0},{5,1},{6,2},{7,3},{8,12},{9,13},{10,... | collective-permute-start | bytes 135176 | tf_op jit(solution)/shard_map/ppermute | solution.py:393
  24.8 1.5 %collective-permute-start.9 = (s16[16,1408]{1,0:T(8,128)(2,1)S(1)}, s16[16,1408]{1,0:T(8,128)(2,1)S(1)}, u32[]{:S(2)}, u32[]{:S(2)}) collective-permute-start(s16[16,1408]{1,0:T(8,128)(2,1)S(1)} %get-tuple-element.24), channel_id=1, source_target_pairs={{0,2},{1,3},{2,0},{3,1},{4,6},{5,7},{6,4},{7,5},{8,10},{9,11},{10,... | collective-permute-start | bytes 135176 | tf_op jit(solution)/shard_map/ppermute | solution.py:393
  26.3 1.7 %collective-permute-done.10.refs_1_ = s16[16,1408]{1,0:T(8,128)(2,1)S(1)} collective-permute-done((s16[16,1408]{1,0:T(8,128)(2,1)S(1)}, s16[16,1408]{1,0:T(8,128)(2,1)S(1)}, u32[]{:S(2)}, u32[]{:S(2)}) %collective-permute-start.10) | collective-permute-done | bytes 45088 | tf_op jit(solution)/shard_map/ppermute | solution.py:393
  27.9 0.4 %collective-permute-done.11.refs_2_ = s16[16,1408]{1,0:T(8,128)(2,1)S(1)} collective-permute-done((s16[16,1408]{1,0:T(8,128)(2,1)S(1)}, s16[16,1408]{1,0:T(8,128)(2,1)S(1)}, u32[]{:S(2)}, u32[]{:S(2)}) %collective-permute-start.11) | collective-permute-done | bytes 45088 | tf_op jit(solution)/shard_map/ppermute | solution.py:393
  28.4 0.4 %collective-permute-done.9.refs_0_ = s16[16,1408]{1,0:T(8,128)(2,1)S(1)} collective-permute-done((s16[16,1408]{1,0:T(8,128)(2,1)S(1)}, s16[16,1408]{1,0:T(8,128)(2,1)S(1)}, u32[]{:S(2)}, u32[]{:S(2)}) %collective-permute-start.9) | collective-permute-done | bytes 45088 | tf_op jit(solution)/shard_map/ppermute | solution.py:393
  28.8 0.7 %add_up.1 = f32[8,2,1280]{2,1,0:T(2,128)} custom-call(f32[16,1280]{1,0:T(8,128)S(1)} %get-tuple-element.23.own_ref, s16[16,1408]{1,0:T(8,128)(2,1)S(1)} %collective-permute-done.9.refs_0_, s16[16,1408]{1,0:T(8,128)(2,1)S(1)} %collective-permute-done.10.refs_1_, s16[16,1408]{1,0:T(8,128)(2,1)S(1)} %collective-permute-done.11.refs_2_), custom_call_target="tpu_custom_call" | custom-call | tf_op jit(solution)/shard_map/add_up/pallas_call | solution.py:373
  (1 shorter events, 0.0 us)
Async XLA Ops:
  0.0 1.7 %collective-permute-start = (bf16[32,2,1024]{2,1,0:T(2,128)(2,1)}, bf16[32,2,1024]{2,1,0:T(2,128)(2,1)S(1)}, u32[]{:S(2)}, u32[]{:S(2)}) collective-permute-start(bf16[32,2,1024]{2,1,0:T(2,128)(2,1)} %bitcast.3), channel_id=1, source_target_pairs={{0,1},{1,0},{2,3},{3,2},{4,5},{5,4},{6,7},{7,6},{8,9},{9,8},{10,11... | collective-permute-start | bytes 393224 | tf_op jit(solution)/shard_map/ppermute | solution.py:393
  0.5 5.1 %collective-permute-start.5 = (bf16[16,16,256]{2,1,0:T(8,128)(2,1)}, bf16[16,16,256]{2,1,0:T(8,128)(2,1)S(1)}, u32[]{:S(2)}, u32[]{:S(2)}) collective-permute-start(bf16[16,16,256]{2,1,0:T(8,128)(2,1)} %slip_hbm.1), channel_id=1, source_target_pairs={{0,1},{1,0},{2,3},{3,2},{4,5},{5,4},{6,7},{7,6},{8,9},{9,8},{10,11... | collective-permute-start | bytes 393224 | tf_op jit(solution)/shard_map/ppermute | solution.py:393
  2.6 7.4 %collective-permute-start.1 = (bf16[32,1024]{1,0:T(8,128)(2,1)S(1)}, bf16[32,1024]{1,0:T(8,128)(2,1)S(1)}, u32[]{:S(2)}, u32[]{:S(2)}) collective-permute-start(bf16[32,1024]{1,0:T(8,128)(2,1)S(1)} %get-tuple-element.20), channel_id=1, source_target_pairs={{0,2},{1,5},{2,0},{3,7},{4,6},{5,1},{6,4},{7,3},{8,10},{9,13},{10,... | collective-permute-start | bytes 196616 | tf_op jit(solution)/shard_map/ppermute | solution.py:414
  5.8 9.1 %collective-permute-start.6 = (bf16[128,512]{1,0:T(8,128)(2,1)S(1)}, bf16[128,512]{1,0:T(8,128)(2,1)S(1)}, u32[]{:S(2)}, u32[]{:S(2)}) collective-permute-start(bf16[128,512]{1,0:T(8,128)(2,1)S(1)} %arrange_other.1.refs_0_), channel_id=1, source_target_pairs={{0,16},{8,24},{16,0},{24,8},{1,17},{9,25},{17,1},{25,9},{2,18},{10... | collective-permute-start | bytes 393224 | tf_op jit(solution)/shard_map/ppermute | solution.py:425
  8.4 4.8 %collective-permute-start.3 = (bf16[16,1024]{1,0:T(8,128)(2,1)S(1)}, bf16[16,1024]{1,0:T(8,128)(2,1)S(1)}, u32[]{:S(2)}, u32[]{:S(2)}) collective-permute-start(bf16[16,1024]{1,0:T(8,128)(2,1)S(1)} %get-tuple-element.21), channel_id=1, source_target_pairs={{0,6},{1,7},{2,4},{3,5},{4,2},{5,3},{6,0},{7,1},{8,14},{9,15},{10,... | collective-permute-start | bytes 98312 | tf_op jit(solution)/shard_map/ppermute | solution.py:414
  9.9 4.9 %collective-permute-start.2 = (bf16[32,1024]{1,0:T(8,128)(2,1)S(1)}, bf16[32,1024]{1,0:T(8,128)(2,1)S(1)}, u32[]{:S(2)}, u32[]{:S(2)}) collective-permute-start(bf16[32,1024]{1,0:T(8,128)(2,1)S(1)} %collective-permute-done.1.refs_1_), channel_id=1, source_target_pairs={{0,1},{1,0},{2,3},{3,2},{4,5},{5,4},{6,7},{7,6},{8,9},{9,8},{10,11... | collective-permute-start | bytes 196616 | tf_op jit(solution)/shard_map/ppermute | solution.py:393
  13.3 1.6 %collective-permute-start.4 = (bf16[16,1024]{1,0:T(8,128)(2,1)S(1)}, bf16[16,1024]{1,0:T(8,128)(2,1)S(1)}, u32[]{:S(2)}, u32[]{:S(2)}) collective-permute-start(bf16[16,1024]{1,0:T(8,128)(2,1)S(1)} %collective-permute-done.3.refs_3_), channel_id=1, source_target_pairs={{0,1},{1,0},{2,3},{3,2},{4,5},{5,4},{6,7},{7,6},{8,9},{9,8},{10,11... | collective-permute-start | bytes 98312 | tf_op jit(solution)/shard_map/ppermute | solution.py:393
  13.3 6.3 %collective-permute-start.8 = (bf16[128,512]{1,0:T(8,128)(2,1)S(1)}, bf16[128,512]{1,0:T(8,128)(2,1)S(1)}, u32[]{:S(2)}, u32[]{:S(2)}) collective-permute-start(bf16[128,512]{1,0:T(8,128)(2,1)S(1)} %arrange_other.1.refs_0_), channel_id=1, source_target_pairs={{0,8},{8,0},{16,24},{24,16},{1,9},{9,1},{17,25},{25,17},{2,10},{10... | collective-permute-start | bytes 393224 | tf_op jit(solution)/shard_map/ppermute | solution.py:425
  14.9 7.1 %collective-permute-start.7 = (bf16[128,512]{1,0:T(8,128)(2,1)S(1)}, bf16[128,512]{1,0:T(8,128)(2,1)S(1)}, u32[]{:S(2)}, u32[]{:S(2)}) collective-permute-start(bf16[128,512]{1,0:T(8,128)(2,1)S(1)} %pass_on.1.refs_2_), channel_id=1, source_target_pairs={{0,8},{8,0},{16,24},{24,16},{1,9},{9,1},{17,25},{25,17},{2,10},{10... | collective-permute-start | bytes 393224 | tf_op jit(solution)/shard_map/ppermute | solution.py:425
  22.7 5.2 %collective-permute-start.10 = (s16[16,1408]{1,0:T(8,128)(2,1)S(1)}, s16[16,1408]{1,0:T(8,128)(2,1)S(1)}, u32[]{:S(2)}, u32[]{:S(2)}) collective-permute-start(s16[16,1408]{1,0:T(8,128)(2,1)S(1)} %get-tuple-element.25), channel_id=1, source_target_pairs={{0,6},{1,7},{2,4},{3,5},{4,2},{5,3},{6,0},{7,1},{8,14},{9,15},{10,... | collective-permute-start | bytes 135176 | tf_op jit(solution)/shard_map/ppermute | solution.py:393
  24.3 4.1 %collective-permute-start.11 = (s16[16,1408]{1,0:T(8,128)(2,1)S(1)}, s16[16,1408]{1,0:T(8,128)(2,1)S(1)}, u32[]{:S(2)}, u32[]{:S(2)}) collective-permute-start(s16[16,1408]{1,0:T(8,128)(2,1)S(1)} %get-tuple-element.26), channel_id=1, source_target_pairs={{0,4},{1,5},{2,6},{3,7},{4,0},{5,1},{6,2},{7,3},{8,12},{9,13},{10,... | collective-permute-start | bytes 135176 | tf_op jit(solution)/shard_map/ppermute | solution.py:393
  24.8 4.0 %collective-permute-start.9 = (s16[16,1408]{1,0:T(8,128)(2,1)S(1)}, s16[16,1408]{1,0:T(8,128)(2,1)S(1)}, u32[]{:S(2)}, u32[]{:S(2)}) collective-permute-start(s16[16,1408]{1,0:T(8,128)(2,1)S(1)} %get-tuple-element.24), channel_id=1, source_target_pairs={{0,2},{1,3},{2,0},{3,1},{4,6},{5,7},{6,4},{7,5},{8,10},{9,11},{10,... | collective-permute-start | bytes 135176 | tf_op jit(solution)/shard_map/ppermute | solution.py:393

commit v2 on v1

--- a/solution.py
+++ b/solution.py
@@ -176,7 +176,7 @@
     pick_ref[...] = one_hot(lax.broadcasted_iota(jnp.int32, pick_ref.shape, 0) == code)
 
 
-def route_kernel(chips, send_ref, own_ref, other_ref, *out_refs):
+def route_kernel(chips, send_ref, own_ref, other_ref, after_ref, *out_refs):
     capacity = send_ref.shape[0] // chips
     half = capacity // 2
     core = lax.rem(lax.axis_index("patch"), 2)
@@ -196,17 +196,19 @@
         out_ref[...] = jnp.concatenate(values, axis=0).astype(jnp.bfloat16)
 
 
-def route_tiles(send, own, other, chips):
+def route_tiles(send, own, other, after, chips):
     components, lags = own.shape[1:]
     rows = components * send.shape[0] // chips
     shape = jax.ShapeDtypeStruct((rows, lags), jnp.bfloat16)
     part = jax.ShapeDtypeStruct((rows // 2, lags), jnp.bfloat16)
     return pl.pallas_call(
         functools.partial(route_kernel, chips),
+        in_specs=[pl.BlockSpec(memory_space=pltpu.VMEM)] * 3
+        + [pl.BlockSpec(memory_space=pl.ANY)],
         out_shape=(shape,) * (chips // 2) + (part,),
         compiler_params=params(),
         name="route_tiles",
-    )(send, own, other)
+    )(send, own, other, after)
 
 
 def pass_on(value, *others):
@@ -406,7 +408,7 @@
     )
     block = arrange_other(other, other_tiles, block)
 
-    pieces = list(route_tiles(send, greens, other_tiles, chips))
+    pieces = list(route_tiles(send, greens, other_tiles, block, chips))
     arrived = []
     for index, piece in enumerate(pieces[1:]):
         hops = [(2 * index + 1, 2 * index + 2), (chips - 1, chips - 1)][index == len(pieces) - 2]
@@ -426,7 +428,7 @@
                 blocks[step - low], "site", [(i, i ^ low) for i in range(sites)]
             )
             if step == sites // 2:
-                blocks[step] = pass_on(blocks[step], *pieces[1:])
+                blocks[step] = pass_on(blocks[step], *arrived)
     shifted = shift_tiles(pick, pieces, components)
 
     slips = [blocks[step] for step in range(sites)]

time: 29.7 us -> 27 us (0.909)
  waiting for transfers between devices: 9.66 us -> 6.31 us
  starting transfers between devices: 14 us -> 14.7 us
    ppermute x3, waiting for transfers between devices: 3.77 us -> 0.07 us  [local(): lax.ppermute(blocks[step - low], 'site', [(i, i ^ low) for i in range(sit...]
    ppermute x7, waiting for transfers between devices: 2.57 us -> 4.49 us  [over_patch(): lax.ppermute(value, 'patch', [(i, i ^ offset) for i in range(devices)])]
    ppermute x3, starting transfers between devices: 5.48 us -> 7.06 us  [local(): lax.ppermute(blocks[step - low], 'site', [(i, i ^ low) for i in range(sit...]
    ppermute x2, waiting for transfers between devices: 3.32 us -> 1.75 us  [local(): lax.ppermute(piece, 'patch', [(i, i ^ 2 * hops[i % 2]) for i in range(dev...]
    ppermute x2, starting transfers between devices: 4.49 us -> 3.05 us  [local(): lax.ppermute(piece, 'patch', [(i, i ^ 2 * hops[i % 2]) for i in range(dev...]
    ppermute x7, starting transfers between devices: 4.07 us -> 4.57 us  [over_patch(): lax.ppermute(value, 'patch', [(i, i ^ offset) for i in range(devices)])]
  transfers between devices with their start and end apart: 12 -> 12, of which waited for: 6 -> 7; matrix products, arithmetic and copies ran while one was open for 0% -> 0% of each run, Pallas kernels for 15% -> 15%
where the time goes in v2:
time: 27 us; the launch traced here: 26.8 us
  starting transfers between devices  14.7 us (54%)
  waiting for transfers between devices  6.31 us (23%)
  Pallas kernels  5.79 us (21%)
    ppermute x3, starting transfers between devices, local(): lax.ppermute(blocks[step - low], 'site', [(i, i ^ low) for i in range(sit...  7.06 us
    ppermute x7, starting transfers between devices, over_patch(): lax.ppermute(value, 'patch', [(i, i ^ offset) for i in range(devices)])  4.57 us
    ppermute x7, waiting for transfers between devices, over_patch(): lax.ppermute(value, 'patch', [(i, i ^ offset) for i in range(devices)])  4.49 us
    ppermute x2, starting transfers between devices, local(): lax.ppermute(piece, 'patch', [(i, i ^ 2 * hops[i % 2]) for i in range(dev...  3.05 us
    ppermute x2, waiting for transfers between devices, local(): lax.ppermute(piece, 'patch', [(i, i ^ 2 * hops[i % 2]) for i in range(dev...  1.75 us
    pallas_call x1, Pallas kernels, convolve_first(): pl.pallas_call(functools.partial(convolve_first_kernel, rows), out_shape=...  1.27 us
    pallas_call x1, Pallas kernels, arrange_own(): pl.pallas_call(functools.partial(arrange_own_kernel, chips, per_chip, cap...  1.21 us
    pallas_call x1, Pallas kernels, route_tiles(): pl.pallas_call(functools.partial(route_kernel, chips), in_specs=[pl.Block...  0.84 us
  transfers between devices with their start and end apart: 12, of which 7 were waited for; matrix products, arithmetic and copies ran while one was open for 0% of the time, Pallas kernels for 15%

profile of v2, /device:TPU:0, one launch (start us, length us, event | category | flops | bytes accessed | tf_op | source)
XLA Modules:
  0.0 26.8 jit_solution(9899344562711542918)
XLA Ops:
  0.0 0.5 %collective-permute-start = (bf16[32,2,1024]{2,1,0:T(2,128)(2,1)}, bf16[32,2,1024]{2,1,0:T(2,128)(2,1)S(1)}, u32[]{:S(2)}, u32[]{:S(2)}) collective-permute-start(bf16[32,2,1024]{2,1,0:T(2,128)(2,1)} %bitcast.3), channel_id=1, source_target_pairs={{0,1},{1,0},{2,3},{3,2},{4,5},{5,4},{6,7},{7,6},{8,9},{9,8},{10,11... | collective-permute-start | bytes 393224 | tf_op jit(solution)/shard_map/ppermute | solution.py:395
  0.5 0.1 collective-permute-start.1
  0.5 1.2 %arrange_own.1 = (bf16[128,512]{1,0:T(8,128)(2,1)S(1)}, bf16[64,64]{1,0:T(8,128)(2,1)S(1)}, bf16[64,32]{1,0:T(8,128)(2,1)S(1)}, bf16[32,2,1024]{2,1,0:T(2,128)(2,1)S(1)}) custom-call(bf16[16,16,256]{2,1,0:T(8,128)(2,1)} %slip_hbm.1, s32[1,128]{1,0:T(1,128)} %bitcast.5, bf16[32,2,1024]{2,1,0:T(2,128)(2,1)} %bitcast.4), custom_call_target="tpu_custom_call" | custom-call | tf_op jit(solution)/shard_map/arrange_own/pallas_call | solution.py:98
  1.7 0.0 collective-permute-done.green_ref.other_ref
  1.7 0.3 %collective-permute-done.1.slip_ref = bf16[16,16,256]{2,1,0:T(8,128)(2,1)S(1)} collective-permute-done((bf16[16,16,256]{2,1,0:T(8,128)(2,1)}, bf16[16,16,256]{2,1,0:T(8,128)(2,1)S(1)}, u32[]{:S(2)}, u32[]{:S(2)}) %collective-permute-start.1) | collective-permute-done | bytes 131104 | tf_op jit(solution)/shard_map/ppermute | solution.py:395
  2.0 0.2 arrange_other.1.after_ref.refs_0_
  2.2 3.8 %collective-permute-start.6 = (bf16[128,512]{1,0:T(8,128)(2,1)S(1)}, bf16[128,512]{1,0:T(8,128)(2,1)S(1)}, u32[]{:S(2)}, u32[]{:S(2)}) collective-permute-start(bf16[128,512]{1,0:T(8,128)(2,1)S(1)} %arrange_other.1.after_ref.refs_0_), channel_id=1, source_target_pairs={{0,16},{8,24},{16,0},{24,8},{1,17},{9,25},{17,1},{25,9},{2,18},{10... | collective-permute-start | bytes 393224 | tf_op jit(solution)/shard_map/ppermute | solution.py:427
  6.1 0.8 %route_tiles.1 = (bf16[32,1024]{1,0:T(8,128)(2,1)S(1)}, bf16[32,1024]{1,0:T(8,128)(2,1)S(1)}, bf16[16,1024]{1,0:T(8,128)(2,1)S(1)}) custom-call(bf16[64,64]{1,0:T(8,128)(2,1)S(1)} %get-tuple-element.17.send_ref, bf16[32,2,1024]{2,1,0:T(2,128)(2,1)S(1)} %get-tuple-element.18.own_ref, bf16[32,2,1024]{2,1,0:T(2,128)(2,1)S(1)} %collective-permute-done.green_ref.other_ref, ...), custom_call_target="tpu_custom_call" | custom-call | tf_op jit(solution)/shard_map/route_tiles/pallas_call | solution.py:204
  6.9 1.6 %collective-permute-start.2 = (bf16[32,1024]{1,0:T(8,128)(2,1)S(1)}, bf16[32,1024]{1,0:T(8,128)(2,1)S(1)}, u32[]{:S(2)}, u32[]{:S(2)}) collective-permute-start(bf16[32,1024]{1,0:T(8,128)(2,1)S(1)} %get-tuple-element.21), channel_id=1, source_target_pairs={{0,2},{1,5},{2,0},{3,7},{4,6},{5,1},{6,4},{7,3},{8,10},{9,13},{10,... | collective-permute-start | bytes 196616 | tf_op jit(solution)/shard_map/ppermute | solution.py:416
  8.5 1.5 %collective-permute-start.4 = (bf16[16,1024]{1,0:T(8,128)(2,1)S(1)}, bf16[16,1024]{1,0:T(8,128)(2,1)S(1)}, u32[]{:S(2)}, u32[]{:S(2)}) collective-permute-start(bf16[16,1024]{1,0:T(8,128)(2,1)S(1)} %get-tuple-element.22), channel_id=1, source_target_pairs={{0,6},{1,7},{2,4},{3,5},{4,2},{5,3},{6,0},{7,1},{8,14},{9,15},{10,... | collective-permute-start | bytes 98312 | tf_op jit(solution)/shard_map/ppermute | solution.py:416
  9.9 1.6 %collective-permute-start.8 = (bf16[128,512]{1,0:T(8,128)(2,1)S(1)}, bf16[128,512]{1,0:T(8,128)(2,1)S(1)}, u32[]{:S(2)}, u32[]{:S(2)}) collective-permute-start(bf16[128,512]{1,0:T(8,128)(2,1)S(1)} %arrange_other.1.after_ref.refs_0_), channel_id=1, source_target_pairs={{0,8},{8,0},{16,24},{24,16},{1,9},{9,1},{17,25},{25,17},{2,10},{10... | collective-permute-start | bytes 393224 | tf_op jit(solution)/shard_map/ppermute | solution.py:427
  11.5 1.7 %collective-permute-done.4.refs_3_.refs_2_ = bf16[16,1024]{1,0:T(8,128)(2,1)S(1)} collective-permute-done((bf16[16,1024]{1,0:T(8,128)(2,1)S(1)}, bf16[16,1024]{1,0:T(8,128)(2,1)S(1)}, u32[]{:S(2)}, u32[]{:S(2)}) %collective-permute-start.4) | collective-permute-done | bytes 32800 | tf_op jit(solution)/shard_map/ppermute | solution.py:416
  13.3 0.0 collective-permute-done.2.refs_1_
  13.3 0.0 collective-permute-done.6.refs_0_
  13.3 1.6 %collective-permute-start.7 = (bf16[128,512]{1,0:T(8,128)(2,1)S(1)}, bf16[128,512]{1,0:T(8,128)(2,1)S(1)}, u32[]{:S(2)}, u32[]{:S(2)}) collective-permute-start(bf16[128,512]{1,0:T(8,128)(2,1)S(1)} %pass_on.1.refs_2_), channel_id=1, source_target_pairs={{0,8},{8,0},{16,24},{24,16},{1,9},{9,1},{17,25},{25,17},{2,10},{10... | collective-permute-start | bytes 393224 | tf_op jit(solution)/shard_map/ppermute | solution.py:427
  14.9 0.0 collective-permute-start.3
  14.9 0.5 %collective-permute-start.5 = (bf16[16,1024]{1,0:T(8,128)(2,1)S(1)}, bf16[16,1024]{1,0:T(8,128)(2,1)S(1)}, u32[]{:S(2)}, u32[]{:S(2)}) collective-permute-start(bf16[16,1024]{1,0:T(8,128)(2,1)S(1)} %collective-permute-done.4.refs_3_.refs_2_), channel_id=1, source_target_pairs={{0,1},{1,0},{2,3},{3,2},{4,5},{5,4},{6,7},{7,6},{8,9},{9,8},{10,11... | collective-permute-start | bytes 98312 | tf_op jit(solution)/shard_map/ppermute | solution.py:395
  15.4 0.9 %collective-permute-done.5.refs_4_ = bf16[16,1024]{1,0:T(8,128)(2,1)S(1)} collective-permute-done((bf16[16,1024]{1,0:T(8,128)(2,1)S(1)}, bf16[16,1024]{1,0:T(8,128)(2,1)S(1)}, u32[]{:S(2)}, u32[]{:S(2)}) %collective-permute-start.5) | collective-permute-done | bytes 32800 | tf_op jit(solution)/shard_map/ppermute | solution.py:395
  16.3 0.0 collective-permute-done.3.refs_2_
  16.3 0.8 %shift_tiles.1.shifted_ref = bf16[512,2304]{1,0:T(8,128)(2,1)S(1)} custom-call(bf16[64,32]{1,0:T(8,128)(2,1)S(1)} %get-tuple-element.16.pick_ref, bf16[32,1024]{1,0:T(8,128)(2,1)S(1)} %get-tuple-element.20.refs_0_, bf16[32,1024]{1,0:T(8,128)(2,1)S(1)} %collective-permute-done.2.refs_1_, bf16[32,1024]{1,0:T(8,128)(2,1)S(1)} %collective-permute-done.3.refs_2_, ...), custom_call_target="tpu_custom_call" | custom-call | tf_op jit(solution)/shard_map/shift_tiles/pallas_call | solution.py:258
  17.1 0.0 collective-permute-done.8.refs_1_
  17.1 1.3 %convolve_first.1.first_ref = f32[3,16,1280]{2,1,0:T(8,128)S(1)} custom-call(bf16[512,2304]{1,0:T(8,128)(2,1)S(1)} %shift_tiles.1.shifted_ref, bf16[128,512]{1,0:T(8,128)(2,1)S(1)} %arrange_other.1.after_ref.refs_0_, bf16[128,512]{1,0:T(8,128)(2,1)S(1)} %collective-permute-done.8.refs_1_, bf16[128,512]{1,0:T(8,128)(2,1)S(1)} %pass_on.1.refs_2_), custom_call_target="tpu_custom_call" | custom-call | tf_op jit(solution)/shard_map/convolve_first/pallas_call | solution.py:312
  18.4 0.1 collective-permute-done.7.slip_ref
  18.5 0.7 %convolve_last.1 = (f32[16,1280]{1,0:T(8,128)S(1)}, s16[16,1408]{1,0:T(8,128)(2,1)S(1)}, s16[16,1408]{1,0:T(8,128)(2,1)S(1)}, s16[16,1408]{1,0:T(8,128)(2,1)S(1)}) custom-call(bf16[512,2304]{1,0:T(8,128)(2,1)S(1)} %shift_tiles.1.shifted_ref, bf16[128,512]{1,0:T(8,128)(2,1)S(1)} %collective-permute-done.7.slip_ref, f32[3,16,1280]{2,1,0:T(8,128)S(1)} %convolve_first.1.first_ref), custom_call_target="tpu_custom_call" | custom-call | tf_op jit(solution)/shard_map/convolve_last/pallas_call | solution.py:352
  19.2 2.4 %collective-permute-start.10 = (s16[16,1408]{1,0:T(8,128)(2,1)S(1)}, s16[16,1408]{1,0:T(8,128)(2,1)S(1)}, u32[]{:S(2)}, u32[]{:S(2)}) collective-permute-start(s16[16,1408]{1,0:T(8,128)(2,1)S(1)} %get-tuple-element.25), channel_id=1, source_target_pairs={{0,6},{1,7},{2,4},{3,5},{4,2},{5,3},{6,0},{7,1},{8,14},{9,15},{10,... | collective-permute-start | bytes 135176 | tf_op jit(solution)/shard_map/ppermute | solution.py:395
  21.6 0.5 %collective-permute-start.11 = (s16[16,1408]{1,0:T(8,128)(2,1)S(1)}, s16[16,1408]{1,0:T(8,128)(2,1)S(1)}, u32[]{:S(2)}, u32[]{:S(2)}) collective-permute-start(s16[16,1408]{1,0:T(8,128)(2,1)S(1)} %get-tuple-element.26), channel_id=1, source_target_pairs={{0,4},{1,5},{2,6},{3,7},{4,0},{5,1},{6,2},{7,3},{8,12},{9,13},{10,... | collective-permute-start | bytes 135176 | tf_op jit(solution)/shard_map/ppermute | solution.py:395
  22.0 0.7 %collective-permute-start.9 = (s16[16,1408]{1,0:T(8,128)(2,1)S(1)}, s16[16,1408]{1,0:T(8,128)(2,1)S(1)}, u32[]{:S(2)}, u32[]{:S(2)}) collective-permute-start(s16[16,1408]{1,0:T(8,128)(2,1)S(1)} %get-tuple-element.24), channel_id=1, source_target_pairs={{0,2},{1,3},{2,0},{3,1},{4,6},{5,7},{6,4},{7,5},{8,10},{9,11},{10,... | collective-permute-start | bytes 135176 | tf_op jit(solution)/shard_map/ppermute | solution.py:395
  22.7 1.5 %collective-permute-done.10.refs_1_ = s16[16,1408]{1,0:T(8,128)(2,1)S(1)} collective-permute-done((s16[16,1408]{1,0:T(8,128)(2,1)S(1)}, s16[16,1408]{1,0:T(8,128)(2,1)S(1)}, u32[]{:S(2)}, u32[]{:S(2)}) %collective-permute-start.10) | collective-permute-done | bytes 45088 | tf_op jit(solution)/shard_map/ppermute | solution.py:395
  24.3 1.3 %collective-permute-done.11.refs_2_ = s16[16,1408]{1,0:T(8,128)(2,1)S(1)} collective-permute-done((s16[16,1408]{1,0:T(8,128)(2,1)S(1)}, s16[16,1408]{1,0:T(8,128)(2,1)S(1)}, u32[]{:S(2)}, u32[]{:S(2)}) %collective-permute-start.11) | collective-permute-done | bytes 45088 | tf_op jit(solution)/shard_map/ppermute | solution.py:395
  25.6 0.5 %collective-permute-done.9.refs_0_ = s16[16,1408]{1,0:T(8,128)(2,1)S(1)} collective-permute-done((s16[16,1408]{1,0:T(8,128)(2,1)S(1)}, s16[16,1408]{1,0:T(8,128)(2,1)S(1)}, u32[]{:S(2)}, u32[]{:S(2)}) %collective-permute-start.9) | collective-permute-done | bytes 45088 | tf_op jit(solution)/shard_map/ppermute | solution.py:395
  26.1 0.7 %add_up.1 = f32[8,2,1280]{2,1,0:T(2,128)} custom-call(f32[16,1280]{1,0:T(8,128)S(1)} %get-tuple-element.23.own_ref, s16[16,1408]{1,0:T(8,128)(2,1)S(1)} %collective-permute-done.9.refs_0_, s16[16,1408]{1,0:T(8,128)(2,1)S(1)} %collective-permute-done.10.refs_1_, s16[16,1408]{1,0:T(8,128)(2,1)S(1)} %collective-permute-done.11.refs_2_), custom_call_target="tpu_custom_call" | custom-call | tf_op jit(solution)/shard_map/add_up/pallas_call | solution.py:375
  (1 shorter events, 0.0 us)
Async XLA Ops:
  0.0 1.7 %collective-permute-start = (bf16[32,2,1024]{2,1,0:T(2,128)(2,1)}, bf16[32,2,1024]{2,1,0:T(2,128)(2,1)S(1)}, u32[]{:S(2)}, u32[]{:S(2)}) collective-permute-start(bf16[32,2,1024]{2,1,0:T(2,128)(2,1)} %bitcast.3), channel_id=1, source_target_pairs={{0,1},{1,0},{2,3},{3,2},{4,5},{5,4},{6,7},{7,6},{8,9},{9,8},{10,11... | collective-permute-start | bytes 393224 | tf_op jit(solution)/shard_map/ppermute | solution.py:395
  0.5 1.6 %collective-permute-start.1 = (bf16[16,16,256]{2,1,0:T(8,128)(2,1)}, bf16[16,16,256]{2,1,0:T(8,128)(2,1)S(1)}, u32[]{:S(2)}, u32[]{:S(2)}) collective-permute-start(bf16[16,16,256]{2,1,0:T(8,128)(2,1)} %slip_hbm.1), channel_id=1, source_target_pairs={{0,1},{1,0},{2,3},{3,2},{4,5},{5,4},{6,7},{7,6},{8,9},{9,8},{10,11... | collective-permute-start | bytes 393224 | tf_op jit(solution)/shard_map/ppermute | solution.py:395
  2.2 11.1 %collective-permute-start.6 = (bf16[128,512]{1,0:T(8,128)(2,1)S(1)}, bf16[128,512]{1,0:T(8,128)(2,1)S(1)}, u32[]{:S(2)}, u32[]{:S(2)}) collective-permute-start(bf16[128,512]{1,0:T(8,128)(2,1)S(1)} %arrange_other.1.after_ref.refs_0_), channel_id=1, source_target_pairs={{0,16},{8,24},{16,0},{24,8},{1,17},{9,25},{17,1},{25,9},{2,18},{10... | collective-permute-start | bytes 393224 | tf_op jit(solution)/shard_map/ppermute | solution.py:427
  6.9 6.4 %collective-permute-start.2 = (bf16[32,1024]{1,0:T(8,128)(2,1)S(1)}, bf16[32,1024]{1,0:T(8,128)(2,1)S(1)}, u32[]{:S(2)}, u32[]{:S(2)}) collective-permute-start(bf16[32,1024]{1,0:T(8,128)(2,1)S(1)} %get-tuple-element.21), channel_id=1, source_target_pairs={{0,2},{1,5},{2,0},{3,7},{4,6},{5,1},{6,4},{7,3},{8,10},{9,13},{10,... | collective-permute-start | bytes 196616 | tf_op jit(solution)/shard_map/ppermute | solution.py:416
  8.5 4.8 %collective-permute-start.4 = (bf16[16,1024]{1,0:T(8,128)(2,1)S(1)}, bf16[16,1024]{1,0:T(8,128)(2,1)S(1)}, u32[]{:S(2)}, u32[]{:S(2)}) collective-permute-start(bf16[16,1024]{1,0:T(8,128)(2,1)S(1)} %get-tuple-element.22), channel_id=1, source_target_pairs={{0,6},{1,7},{2,4},{3,5},{4,2},{5,3},{6,0},{7,1},{8,14},{9,15},{10,... | collective-permute-start | bytes 98312 | tf_op jit(solution)/shard_map/ppermute | solution.py:416
  9.9 7.2 %collective-permute-start.8 = (bf16[128,512]{1,0:T(8,128)(2,1)S(1)}, bf16[128,512]{1,0:T(8,128)(2,1)S(1)}, u32[]{:S(2)}, u32[]{:S(2)}) collective-permute-start(bf16[128,512]{1,0:T(8,128)(2,1)S(1)} %arrange_other.1.after_ref.refs_0_), channel_id=1, source_target_pairs={{0,8},{8,0},{16,24},{24,16},{1,9},{9,1},{17,25},{25,17},{2,10},{10... | collective-permute-start | bytes 393224 | tf_op jit(solution)/shard_map/ppermute | solution.py:427
  13.3 5.2 %collective-permute-start.7 = (bf16[128,512]{1,0:T(8,128)(2,1)S(1)}, bf16[128,512]{1,0:T(8,128)(2,1)S(1)}, u32[]{:S(2)}, u32[]{:S(2)}) collective-permute-start(bf16[128,512]{1,0:T(8,128)(2,1)S(1)} %pass_on.1.refs_2_), channel_id=1, source_target_pairs={{0,8},{8,0},{16,24},{24,16},{1,9},{9,1},{17,25},{25,17},{2,10},{10... | collective-permute-start | bytes 393224 | tf_op jit(solution)/shard_map/ppermute | solution.py:427
  14.9 1.4 %collective-permute-start.3 = (bf16[32,1024]{1,0:T(8,128)(2,1)S(1)}, bf16[32,1024]{1,0:T(8,128)(2,1)S(1)}, u32[]{:S(2)}, u32[]{:S(2)}) collective-permute-start(bf16[32,1024]{1,0:T(8,128)(2,1)S(1)} %collective-permute-done.2.refs_1_), channel_id=1, source_target_pairs={{0,1},{1,0},{2,3},{3,2},{4,5},{5,4},{6,7},{7,6},{8,9},{9,8},{10,11... | collective-permute-start | bytes 196616 | tf_op jit(solution)/shard_map/ppermute | solution.py:395
  14.9 1.4 %collective-permute-start.5 = (bf16[16,1024]{1,0:T(8,128)(2,1)S(1)}, bf16[16,1024]{1,0:T(8,128)(2,1)S(1)}, u32[]{:S(2)}, u32[]{:S(2)}) collective-permute-start(bf16[16,1024]{1,0:T(8,128)(2,1)S(1)} %collective-permute-done.4.refs_3_.refs_2_), channel_id=1, source_target_pairs={{0,1},{1,0},{2,3},{3,2},{4,5},{5,4},{6,7},{7,6},{8,9},{9,8},{10,11... | collective-permute-start | bytes 98312 | tf_op jit(solution)/shard_map/ppermute | solution.py:395
  19.2 5.1 %collective-permute-start.10 = (s16[16,1408]{1,0:T(8,128)(2,1)S(1)}, s16[16,1408]{1,0:T(8,128)(2,1)S(1)}, u32[]{:S(2)}, u32[]{:S(2)}) collective-permute-start(s16[16,1408]{1,0:T(8,128)(2,1)S(1)} %get-tuple-element.25), channel_id=1, source_target_pairs={{0,6},{1,7},{2,4},{3,5},{4,2},{5,3},{6,0},{7,1},{8,14},{9,15},{10,... | collective-permute-start | bytes 135176 | tf_op jit(solution)/shard_map/ppermute | solution.py:395
  21.6 4.0 %collective-permute-start.11 = (s16[16,1408]{1,0:T(8,128)(2,1)S(1)}, s16[16,1408]{1,0:T(8,128)(2,1)S(1)}, u32[]{:S(2)}, u32[]{:S(2)}) collective-permute-start(s16[16,1408]{1,0:T(8,128)(2,1)S(1)} %get-tuple-element.26), channel_id=1, source_target_pairs={{0,4},{1,5},{2,6},{3,7},{4,0},{5,1},{6,2},{7,3},{8,12},{9,13},{10,... | collective-permute-start | bytes 135176 | tf_op jit(solution)/shard_map/ppermute | solution.py:395
  22.0 4.0 %collective-permute-start.9 = (s16[16,1408]{1,0:T(8,128)(2,1)S(1)}, s16[16,1408]{1,0:T(8,128)(2,1)S(1)}, u32[]{:S(2)}, u32[]{:S(2)}) collective-permute-start(s16[16,1408]{1,0:T(8,128)(2,1)S(1)} %get-tuple-element.24), channel_id=1, source_target_pairs={{0,2},{1,3},{2,0},{3,1},{4,6},{5,7},{6,4},{7,5},{8,10},{9,11},{10,... | collective-permute-start | bytes 135176 | tf_op jit(solution)/shard_map/ppermute | solution.py:395

commit v3 on v2

--- a/solution.py
+++ b/solution.py
@@ -101,7 +101,7 @@
         out_shape=(
             block,
             jax.ShapeDtypeStruct((chips * capacity, 2 * width), jnp.bfloat16),
-            jax.ShapeDtypeStruct((chips * capacity, per_chip), jnp.bfloat16),
+            jax.ShapeDtypeStruct(((chips + 1) * capacity, per_chip), jnp.bfloat16),
             jax.ShapeDtypeStruct(greens.shape, greens.dtype),
         ),
         scratch_shapes=[
@@ -140,7 +140,6 @@
 
 
 def mark_tiles(chips, per_chip, capacity, width, slots_ref, send_ref, pick_ref):
-    half = capacity // 2
     count = slots_ref.shape[1]
     own = lax.axis_index("patch")
     chip, core = own // 2, lax.rem(own, 2)
@@ -165,20 +164,21 @@
         one_hot(marks), earlier_in_chip(per_chip, per_chip), preferred_element_type=jnp.float32
     )
     rank = jnp.sum(jnp.where(marks, rank, 0.0), axis=0, keepdims=True).astype(jnp.int32)
-    from_other = jnp.where(owner == chips - 1, rank // half, 1 - owner % 2) != core
-    base = (owner - jnp.where(owner == chips - 1, 0, 1 - owner % 2)) * capacity
-    code = base + jnp.where(
-        owner == chips - 1,
-        jnp.where(from_other, half, 0) + rank % half,
-        jnp.where(from_other, capacity, 0) + rank,
-    )
-    code = jnp.where(owner == 0, rank, code)
+    by_first = (owner % 2 == 1) & (owner < chips - 1)
+    index = jnp.where(owner == chips - 1, 0, owner // 2)
+    place = 1 + 2 * index + jnp.where(by_first == (core == 0), 0, 1)
+    code = jnp.where(owner == 0, 0, place) * capacity + rank
     pick_ref[...] = one_hot(lax.broadcasted_iota(jnp.int32, pick_ref.shape, 0) == code)
+
+
+def send_rounds(chips):
+    firsts = list(range(1, chips - 1, 2)) + [0]
+    seconds = [chips - 1] + list(range(2, chips - 1, 2))
+    return list(zip(firsts, seconds))
 
 
 def route_kernel(chips, send_ref, own_ref, other_ref, after_ref, *out_refs):
     capacity = send_ref.shape[0] // chips
-    half = capacity // 2
     core = lax.rem(lax.axis_index("patch"), 2)
     tiles = jnp.concatenate([own_ref[...], other_ref[...]], axis=0).astype(jnp.float32)
     by_comp = []
@@ -186,11 +186,9 @@
         both = tiles[:, comp, :].astype(jnp.bfloat16)
         chosen = jnp.dot(send_ref[...], both, preferred_element_type=jnp.float32)
         chosen = [chosen[step * capacity : (step + 1) * capacity] for step in range(chips)]
-        last = chosen[-1]
         sent = [chosen[0]]
-        for step in range(1, chips - 1, 2):
-            sent.append(jnp.where(core == 0, chosen[step], chosen[step + 1]))
-        sent.append(jnp.where(core == 0, last[:half], last[half:]))
+        for first, second in send_rounds(chips):
+            sent.append(jnp.where(core == 0, chosen[first], chosen[second]))
         by_comp.append(sent)
     for values, out_ref in zip(zip(*by_comp), out_refs):
         out_ref[...] = jnp.concatenate(values, axis=0).astype(jnp.bfloat16)
@@ -200,12 +198,11 @@
     components, lags = own.shape[1:]
     rows = components * send.shape[0] // chips
     shape = jax.ShapeDtypeStruct((rows, lags), jnp.bfloat16)
-    part = jax.ShapeDtypeStruct((rows // 2, lags), jnp.bfloat16)
     return pl.pallas_call(
         functools.partial(route_kernel, chips),
         in_specs=[pl.BlockSpec(memory_space=pltpu.VMEM)] * 3
         + [pl.BlockSpec(memory_space=pl.ANY)],
-        out_shape=(shape,) * (chips // 2) + (part,),
+        out_shape=(shape,) * (1 + chips // 2),
         compiler_params=params(),
         name="route_tiles",
     )(send, own, other, after)
@@ -229,16 +226,15 @@
 def shift_kernel(pick_ref, *refs):
     pieces, out_ref = refs[:-1], refs[-1]
     count = pick_ref.shape[1]
-    components = sum(piece.shape[0] for piece in pieces) // pick_ref.shape[0]
+    capacity = pick_ref.shape[0] // len(pieces)
+    components = pieces[0].shape[0] // capacity
     lags = pieces[0].shape[1]
     span = out_ref.shape[1] // components
     tail = jnp.zeros((BLOCK, span - lags), jnp.float32)
     for comp in range(components):
-        arrived = []
-        for piece in pieces:
-            size = piece.shape[0] // components
-            arrived.append(piece[...].astype(jnp.float32)[comp * size : (comp + 1) * size])
-        arrived = jnp.concatenate(arrived, axis=0).astype(jnp.bfloat16)
+        arrived = jnp.concatenate(
+            [piece[comp * capacity : (comp + 1) * capacity, :] for piece in pieces], axis=0
+        )
         tiles = lax.dot_general(
             pick_ref[...], arrived, (((0,), (0,)), ((), ())), preferred_element_type=jnp.float32
         )
@@ -410,12 +406,10 @@
 
     pieces = list(route_tiles(send, greens, other_tiles, block, chips))
     arrived = []
-    for index, piece in enumerate(pieces[1:]):
-        hops = [(2 * index + 1, 2 * index + 2), (chips - 1, chips - 1)][index == len(pieces) - 2]
+    for piece, hops in zip(pieces[1:], send_rounds(chips)):
         arrived.append(
             lax.ppermute(piece, "patch", [(i, i ^ (2 * hops[i % 2])) for i in range(devices)])
         )
-
     pieces = pieces[:1]
     for piece in arrived:
         pieces += [piece, over_patch(piece, 1)]

time: 27 us -> 27.6 us (1.022)
  waiting for transfers between devices: 6.31 us -> 6.93 us
    ppermute x7, starting transfers between devices: 4.57 us -> 6.16 us  [over_patch(): lax.ppermute(value, 'patch', [(i, i ^ offset) for i in range(devices)])]
    ppermute x3, waiting for transfers between devices: 0.07 us -> 0.95 us  [local(): lax.ppermute(blocks[step - low], 'site', [(i, i ^ low) for i in range(sit...]
    ppermute x2, starting transfers between devices: 3.05 us -> 2.21 us  [local(): lax.ppermute(piece, 'patch', [(i, i ^ 2 * hops[i % 2]) for i in range(dev...]
    ppermute x3, starting transfers between devices: 7.06 us -> 6.27 us  [local(): lax.ppermute(blocks[step - low], 'site', [(i, i ^ low) for i in range(sit...]
    ppermute x2, waiting for transfers between devices: 1.75 us -> 1.15 us  [local(): lax.ppermute(piece, 'patch', [(i, i ^ 2 * hops[i % 2]) for i in range(dev...]
    ppermute x7, waiting for transfers between devices: 4.49 us -> 4.83 us  [over_patch(): lax.ppermute(value, 'patch', [(i, i ^ offset) for i in range(devices)])]
  transfers between devices with their start and end apart: 12 -> 12, of which waited for: 7 -> 8; matrix products, arithmetic and copies ran while one was open for 0% -> 0% of each run, Pallas kernels for 15% -> 15%
where the time goes in v3:
time: 27.6 us; the launch traced here: 27.4 us
  starting transfers between devices  14.6 us (53%)
  waiting for transfers between devices  6.93 us (25%)
  Pallas kernels  5.81 us (21%)
    ppermute x3, starting transfers between devices, local(): lax.ppermute(blocks[step - low], 'site', [(i, i ^ low) for i in range(sit...  6.27 us
    ppermute x7, starting transfers between devices, over_patch(): lax.ppermute(value, 'patch', [(i, i ^ offset) for i in range(devices)])  6.16 us
    ppermute x7, waiting for transfers between devices, over_patch(): lax.ppermute(value, 'patch', [(i, i ^ offset) for i in range(devices)])  4.83 us
    ppermute x2, starting transfers between devices, local(): lax.ppermute(piece, 'patch', [(i, i ^ 2 * hops[i % 2]) for i in range(dev...  2.21 us
    pallas_call x1, Pallas kernels, convolve_first(): pl.pallas_call(functools.partial(convolve_first_kernel, rows), out_shape=...  1.27 us
    pallas_call x1, Pallas kernels, arrange_own(): pl.pallas_call(functools.partial(arrange_own_kernel, chips, per_chip, cap...  1.21 us
    ppermute x2, waiting for transfers between devices, local(): lax.ppermute(piece, 'patch', [(i, i ^ 2 * hops[i % 2]) for i in range(dev...  1.15 us
    ppermute x3, waiting for transfers between devices, local(): lax.ppermute(blocks[step - low], 'site', [(i, i ^ low) for i in range(sit...  0.95 us
  transfers between devices with their start and end apart: 12, of which 8 were waited for; matrix products, arithmetic and copies ran while one was open for 0% of the time, Pallas kernels for 15%

profile of v3, /device:TPU:0, one launch (start us, length us, event | category | flops | bytes accessed | tf_op | source)
XLA Modules:
  0.0 27.4 jit_solution(3549690370614081470)
XLA Ops:
  0.0 0.5 %collective-permute-start = (bf16[32,2,1024]{2,1,0:T(2,128)(2,1)}, bf16[32,2,1024]{2,1,0:T(2,128)(2,1)S(1)}, u32[]{:S(2)}, u32[]{:S(2)}) collective-permute-start(bf16[32,2,1024]{2,1,0:T(2,128)(2,1)} %bitcast.3), channel_id=1, source_target_pairs={{0,1},{1,0},{2,3},{3,2},{4,5},{5,4},{6,7},{7,6},{8,9},{9,8},{10,11... | collective-permute-start | bytes 393224 | tf_op jit(solution)/shard_map/ppermute | solution.py:391
  0.5 0.1 collective-permute-start.1
  0.5 1.2 %arrange_own.1 = (bf16[128,512]{1,0:T(8,128)(2,1)S(1)}, bf16[64,64]{1,0:T(8,128)(2,1)S(1)}, bf16[80,32]{1,0:T(8,128)(2,1)S(1)}, bf16[32,2,1024]{2,1,0:T(2,128)(2,1)S(1)}) custom-call(bf16[16,16,256]{2,1,0:T(8,128)(2,1)} %slip_hbm.1, s32[1,128]{1,0:T(1,128)} %bitcast.5, bf16[32,2,1024]{2,1,0:T(2,128)(2,1)} %bitcast.4), custom_call_target="tpu_custom_call" | custom-call | tf_op jit(solution)/shard_map/arrange_own/pallas_call | solution.py:98
  1.7 0.0 collective-permute-done.green_ref.other_ref
  1.7 0.3 %collective-permute-done.1.slip_ref = bf16[16,16,256]{2,1,0:T(8,128)(2,1)S(1)} collective-permute-done((bf16[16,16,256]{2,1,0:T(8,128)(2,1)}, bf16[16,16,256]{2,1,0:T(8,128)(2,1)S(1)}, u32[]{:S(2)}, u32[]{:S(2)}) %collective-permute-start.1) | collective-permute-done | bytes 131104 | tf_op jit(solution)/shard_map/ppermute | solution.py:391
  2.0 0.2 arrange_other.1.after_ref.refs_0_
  2.2 3.8 %collective-permute-start.6 = (bf16[128,512]{1,0:T(8,128)(2,1)S(1)}, bf16[128,512]{1,0:T(8,128)(2,1)S(1)}, u32[]{:S(2)}, u32[]{:S(2)}) collective-permute-start(bf16[128,512]{1,0:T(8,128)(2,1)S(1)} %arrange_other.1.after_ref.refs_0_), channel_id=1, source_target_pairs={{0,16},{8,24},{16,0},{24,8},{1,17},{9,25},{17,1},{25,9},{2,18},{10... | collective-permute-start | bytes 393224 | tf_op jit(solution)/shard_map/ppermute | solution.py:421
  6.1 0.8 %route_tiles.1 = (bf16[32,1024]{1,0:T(8,128)(2,1)S(1)}, bf16[32,1024]{1,0:T(8,128)(2,1)S(1)}, bf16[32,1024]{1,0:T(8,128)(2,1)S(1)}) custom-call(bf16[64,64]{1,0:T(8,128)(2,1)S(1)} %get-tuple-element.17.send_ref, bf16[32,2,1024]{2,1,0:T(2,128)(2,1)S(1)} %get-tuple-element.18.own_ref, bf16[32,2,1024]{2,1,0:T(2,128)(2,1)S(1)} %collective-permute-done.green_ref.other_ref, ...), custom_call_target="tpu_custom_call" | custom-call | tf_op jit(solution)/shard_map/route_tiles/pallas_call | solution.py:201
  6.9 1.6 %collective-permute-start.2 = (bf16[32,1024]{1,0:T(8,128)(2,1)S(1)}, bf16[32,1024]{1,0:T(8,128)(2,1)S(1)}, u32[]{:S(2)}, u32[]{:S(2)}) collective-permute-start(bf16[32,1024]{1,0:T(8,128)(2,1)S(1)} %get-tuple-element.21), channel_id=1, source_target_pairs={{0,2},{1,7},{2,0},{3,5},{4,6},{5,3},{6,4},{7,1},{8,10},{9,15},{10,... | collective-permute-start | bytes 196616 | tf_op jit(solution)/shard_map/ppermute | solution.py:411
  8.4 0.7 %collective-permute-start.4 = (bf16[32,1024]{1,0:T(8,128)(2,1)S(1)}, bf16[32,1024]{1,0:T(8,128)(2,1)S(1)}, u32[]{:S(2)}, u32[]{:S(2)}) collective-permute-start(bf16[32,1024]{1,0:T(8,128)(2,1)S(1)} %get-tuple-element.22), channel_id=1, source_target_pairs={{0,0},{1,5},{2,2},{3,7},{4,4},{5,1},{6,6},{7,3},{8,8},{9,13},{10,1... | collective-permute-start | bytes 196616 | tf_op jit(solution)/shard_map/ppermute | solution.py:411
  9.1 1.6 %collective-permute-start.8 = (bf16[128,512]{1,0:T(8,128)(2,1)S(1)}, bf16[128,512]{1,0:T(8,128)(2,1)S(1)}, u32[]{:S(2)}, u32[]{:S(2)}) collective-permute-start(bf16[128,512]{1,0:T(8,128)(2,1)S(1)} %arrange_other.1.after_ref.refs_0_), channel_id=1, source_target_pairs={{0,8},{8,0},{16,24},{24,16},{1,9},{9,1},{17,25},{25,17},{2,10},{10... | collective-permute-start | bytes 393224 | tf_op jit(solution)/shard_map/ppermute | solution.py:421
  10.8 1.1 %collective-permute-done.2.refs_1_ = bf16[32,1024]{1,0:T(8,128)(2,1)S(1)} collective-permute-done((bf16[32,1024]{1,0:T(8,128)(2,1)S(1)}, bf16[32,1024]{1,0:T(8,128)(2,1)S(1)}, u32[]{:S(2)}, u32[]{:S(2)}) %collective-permute-start.2) | collective-permute-done | bytes 65568 | tf_op jit(solution)/shard_map/ppermute | solution.py:411
  11.9 0.0 collective-permute-done.4.refs_3_.refs_2_
  11.9 0.9 %collective-permute-done.6.refs_0_ = bf16[128,512]{1,0:T(8,128)(2,1)S(1)} collective-permute-done((bf16[128,512]{1,0:T(8,128)(2,1)S(1)}, bf16[128,512]{1,0:T(8,128)(2,1)S(1)}, u32[]{:S(2)}, u32[]{:S(2)}) %collective-permute-start.6) | collective-permute-done | bytes 131104 | tf_op jit(solution)/shard_map/ppermute | solution.py:421
  12.8 0.8 %collective-permute-start.7 = (bf16[128,512]{1,0:T(8,128)(2,1)S(1)}, bf16[128,512]{1,0:T(8,128)(2,1)S(1)}, u32[]{:S(2)}, u32[]{:S(2)}) collective-permute-start(bf16[128,512]{1,0:T(8,128)(2,1)S(1)} %pass_on.1.refs_2_), channel_id=1, source_target_pairs={{0,8},{8,0},{16,24},{24,16},{1,9},{9,1},{17,25},{25,17},{2,10},{10... | collective-permute-start | bytes 393224 | tf_op jit(solution)/shard_map/ppermute | solution.py:421
  13.6 2.1 %collective-permute-start.3 = (bf16[32,1024]{1,0:T(8,128)(2,1)S(1)}, bf16[32,1024]{1,0:T(8,128)(2,1)S(1)}, u32[]{:S(2)}, u32[]{:S(2)}) collective-permute-start(bf16[32,1024]{1,0:T(8,128)(2,1)S(1)} %collective-permute-done.2.refs_1_), channel_id=1, source_target_pairs={{0,1},{1,0},{2,3},{3,2},{4,5},{5,4},{6,7},{7,6},{8,9},{9,8},{10,11... | collective-permute-start | bytes 196616 | tf_op jit(solution)/shard_map/ppermute | solution.py:391
  15.7 0.0 collective-permute-start.5
  15.7 0.9 %collective-permute-done.3.refs_2_ = bf16[32,1024]{1,0:T(8,128)(2,1)S(1)} collective-permute-done((bf16[32,1024]{1,0:T(8,128)(2,1)S(1)}, bf16[32,1024]{1,0:T(8,128)(2,1)S(1)}, u32[]{:S(2)}, u32[]{:S(2)}) %collective-permute-start.3) | collective-permute-done | bytes 65568 | tf_op jit(solution)/shard_map/ppermute | solution.py:391
  16.6 0.4 %collective-permute-done.5.refs_4_ = bf16[32,1024]{1,0:T(8,128)(2,1)S(1)} collective-permute-done((bf16[32,1024]{1,0:T(8,128)(2,1)S(1)}, bf16[32,1024]{1,0:T(8,128)(2,1)S(1)}, u32[]{:S(2)}, u32[]{:S(2)}) %collective-permute-start.5) | collective-permute-done | bytes 65568 | tf_op jit(solution)/shard_map/ppermute | solution.py:391
  17.0 0.8 %shift_tiles.1.shifted_ref = bf16[512,2304]{1,0:T(8,128)(2,1)S(1)} custom-call(bf16[80,32]{1,0:T(8,128)(2,1)S(1)} %get-tuple-element.16.pick_ref, bf16[32,1024]{1,0:T(8,128)(2,1)S(1)} %get-tuple-element.20.refs_0_, bf16[32,1024]{1,0:T(8,128)(2,1)S(1)} %collective-permute-done.2.refs_1_, bf16[32,1024]{1,0:T(8,128)(2,1)S(1)} %collective-permute-done.3.refs_2_, ...), custom_call_target="tpu_custom_call" | custom-call | tf_op jit(solution)/shard_map/shift_tiles/pallas_call | solution.py:254
  17.8 0.0 collective-permute-done.8.refs_1_
  17.8 1.3 %convolve_first.1.first_ref = f32[3,16,1280]{2,1,0:T(8,128)S(1)} custom-call(bf16[512,2304]{1,0:T(8,128)(2,1)S(1)} %shift_tiles.1.shifted_ref, bf16[128,512]{1,0:T(8,128)(2,1)S(1)} %arrange_other.1.after_ref.refs_0_, bf16[128,512]{1,0:T(8,128)(2,1)S(1)} %collective-permute-done.8.refs_1_, bf16[128,512]{1,0:T(8,128)(2,1)S(1)} %pass_on.1.refs_2_), custom_call_target="tpu_custom_call" | custom-call | tf_op jit(solution)/shard_map/convolve_first/pallas_call | solution.py:308
  19.1 0.0 collective-permute-done.7.slip_ref
  19.1 0.7 %convolve_last.1 = (f32[16,1280]{1,0:T(8,128)S(1)}, s16[16,1408]{1,0:T(8,128)(2,1)S(1)}, s16[16,1408]{1,0:T(8,128)(2,1)S(1)}, s16[16,1408]{1,0:T(8,128)(2,1)S(1)}) custom-call(bf16[512,2304]{1,0:T(8,128)(2,1)S(1)} %shift_tiles.1.shifted_ref, bf16[128,512]{1,0:T(8,128)(2,1)S(1)} %collective-permute-done.7.slip_ref, f32[3,16,1280]{2,1,0:T(8,128)S(1)} %convolve_first.1.first_ref), custom_call_target="tpu_custom_call" | custom-call | tf_op jit(solution)/shard_map/convolve_last/pallas_call | solution.py:348
  19.8 1.9 %collective-permute-start.10 = (s16[16,1408]{1,0:T(8,128)(2,1)S(1)}, s16[16,1408]{1,0:T(8,128)(2,1)S(1)}, u32[]{:S(2)}, u32[]{:S(2)}) collective-permute-start(s16[16,1408]{1,0:T(8,128)(2,1)S(1)} %get-tuple-element.25), channel_id=1, source_target_pairs={{0,6},{1,7},{2,4},{3,5},{4,2},{5,3},{6,0},{7,1},{8,14},{9,15},{10,... | collective-permute-start | bytes 135176 | tf_op jit(solution)/shard_map/ppermute | solution.py:391
  21.7 0.9 %collective-permute-start.11 = (s16[16,1408]{1,0:T(8,128)(2,1)S(1)}, s16[16,1408]{1,0:T(8,128)(2,1)S(1)}, u32[]{:S(2)}, u32[]{:S(2)}) collective-permute-start(s16[16,1408]{1,0:T(8,128)(2,1)S(1)} %get-tuple-element.26), channel_id=1, source_target_pairs={{0,4},{1,5},{2,6},{3,7},{4,0},{5,1},{6,2},{7,3},{8,12},{9,13},{10,... | collective-permute-start | bytes 135176 | tf_op jit(solution)/shard_map/ppermute | solution.py:391
  22.7 0.7 %collective-permute-start.9 = (s16[16,1408]{1,0:T(8,128)(2,1)S(1)}, s16[16,1408]{1,0:T(8,128)(2,1)S(1)}, u32[]{:S(2)}, u32[]{:S(2)}) collective-permute-start(s16[16,1408]{1,0:T(8,128)(2,1)S(1)} %get-tuple-element.24), channel_id=1, source_target_pairs={{0,2},{1,3},{2,0},{3,1},{4,6},{5,7},{6,4},{7,5},{8,10},{9,11},{10,... | collective-permute-start | bytes 135176 | tf_op jit(solution)/shard_map/ppermute | solution.py:391
  23.4 1.9 %collective-permute-done.10.refs_1_ = s16[16,1408]{1,0:T(8,128)(2,1)S(1)} collective-permute-done((s16[16,1408]{1,0:T(8,128)(2,1)S(1)}, s16[16,1408]{1,0:T(8,128)(2,1)S(1)}, u32[]{:S(2)}, u32[]{:S(2)}) %collective-permute-start.10) | collective-permute-done | bytes 45088 | tf_op jit(solution)/shard_map/ppermute | solution.py:391
  25.3 0.5 %collective-permute-done.11.refs_2_ = s16[16,1408]{1,0:T(8,128)(2,1)S(1)} collective-permute-done((s16[16,1408]{1,0:T(8,128)(2,1)S(1)}, s16[16,1408]{1,0:T(8,128)(2,1)S(1)}, u32[]{:S(2)}, u32[]{:S(2)}) %collective-permute-start.11) | collective-permute-done | bytes 45088 | tf_op jit(solution)/shard_map/ppermute | solution.py:391
  25.8 0.9 %collective-permute-done.9.refs_0_ = s16[16,1408]{1,0:T(8,128)(2,1)S(1)} collective-permute-done((s16[16,1408]{1,0:T(8,128)(2,1)S(1)}, s16[16,1408]{1,0:T(8,128)(2,1)S(1)}, u32[]{:S(2)}, u32[]{:S(2)}) %collective-permute-start.9) | collective-permute-done | bytes 45088 | tf_op jit(solution)/shard_map/ppermute | solution.py:391
  26.7 0.7 %add_up.1 = f32[8,2,1280]{2,1,0:T(2,128)} custom-call(f32[16,1280]{1,0:T(8,128)S(1)} %get-tuple-element.23.own_ref, s16[16,1408]{1,0:T(8,128)(2,1)S(1)} %collective-permute-done.9.refs_0_, s16[16,1408]{1,0:T(8,128)(2,1)S(1)} %collective-permute-done.10.refs_1_, s16[16,1408]{1,0:T(8,128)(2,1)S(1)} %collective-permute-done.11.refs_2_), custom_call_target="tpu_custom_call" | custom-call | tf_op jit(solution)/shard_map/add_up/pallas_call | solution.py:371
  (1 shorter events, 0.0 us)
Async XLA Ops:
  0.0 1.7 %collective-permute-start = (bf16[32,2,1024]{2,1,0:T(2,128)(2,1)}, bf16[32,2,1024]{2,1,0:T(2,128)(2,1)S(1)}, u32[]{:S(2)}, u32[]{:S(2)}) collective-permute-start(bf16[32,2,1024]{2,1,0:T(2,128)(2,1)} %bitcast.3), channel_id=1, source_target_pairs={{0,1},{1,0},{2,3},{3,2},{4,5},{5,4},{6,7},{7,6},{8,9},{9,8},{10,11... | collective-permute-start | bytes 393224 | tf_op jit(solution)/shard_map/ppermute | solution.py:391
  0.5 1.6 %collective-permute-start.1 = (bf16[16,16,256]{2,1,0:T(8,128)(2,1)}, bf16[16,16,256]{2,1,0:T(8,128)(2,1)S(1)}, u32[]{:S(2)}, u32[]{:S(2)}) collective-permute-start(bf16[16,16,256]{2,1,0:T(8,128)(2,1)} %slip_hbm.1), channel_id=1, source_target_pairs={{0,1},{1,0},{2,3},{3,2},{4,5},{5,4},{6,7},{7,6},{8,9},{9,8},{10,11... | collective-permute-start | bytes 393224 | tf_op jit(solution)/shard_map/ppermute | solution.py:391
  2.2 10.6 %collective-permute-start.6 = (bf16[128,512]{1,0:T(8,128)(2,1)S(1)}, bf16[128,512]{1,0:T(8,128)(2,1)S(1)}, u32[]{:S(2)}, u32[]{:S(2)}) collective-permute-start(bf16[128,512]{1,0:T(8,128)(2,1)S(1)} %arrange_other.1.after_ref.refs_0_), channel_id=1, source_target_pairs={{0,16},{8,24},{16,0},{24,8},{1,17},{9,25},{17,1},{25,9},{2,18},{10... | collective-permute-start | bytes 393224 | tf_op jit(solution)/shard_map/ppermute | solution.py:421
  6.9 5.0 %collective-permute-start.2 = (bf16[32,1024]{1,0:T(8,128)(2,1)S(1)}, bf16[32,1024]{1,0:T(8,128)(2,1)S(1)}, u32[]{:S(2)}, u32[]{:S(2)}) collective-permute-start(bf16[32,1024]{1,0:T(8,128)(2,1)S(1)} %get-tuple-element.21), channel_id=1, source_target_pairs={{0,2},{1,7},{2,0},{3,5},{4,6},{5,3},{6,4},{7,1},{8,10},{9,15},{10,... | collective-permute-start | bytes 196616 | tf_op jit(solution)/shard_map/ppermute | solution.py:411
  8.4 3.5 %collective-permute-start.4 = (bf16[32,1024]{1,0:T(8,128)(2,1)S(1)}, bf16[32,1024]{1,0:T(8,128)(2,1)S(1)}, u32[]{:S(2)}, u32[]{:S(2)}) collective-permute-start(bf16[32,1024]{1,0:T(8,128)(2,1)S(1)} %get-tuple-element.22), channel_id=1, source_target_pairs={{0,0},{1,5},{2,2},{3,7},{4,4},{5,1},{6,6},{7,3},{8,8},{9,13},{10,1... | collective-permute-start | bytes 196616 | tf_op jit(solution)/shard_map/ppermute | solution.py:411
  9.1 8.7 %collective-permute-start.8 = (bf16[128,512]{1,0:T(8,128)(2,1)S(1)}, bf16[128,512]{1,0:T(8,128)(2,1)S(1)}, u32[]{:S(2)}, u32[]{:S(2)}) collective-permute-start(bf16[128,512]{1,0:T(8,128)(2,1)S(1)} %arrange_other.1.after_ref.refs_0_), channel_id=1, source_target_pairs={{0,8},{8,0},{16,24},{24,16},{1,9},{9,1},{17,25},{25,17},{2,10},{10... | collective-permute-start | bytes 393224 | tf_op jit(solution)/shard_map/ppermute | solution.py:421
  12.8 6.3 %collective-permute-start.7 = (bf16[128,512]{1,0:T(8,128)(2,1)S(1)}, bf16[128,512]{1,0:T(8,128)(2,1)S(1)}, u32[]{:S(2)}, u32[]{:S(2)}) collective-permute-start(bf16[128,512]{1,0:T(8,128)(2,1)S(1)} %pass_on.1.refs_2_), channel_id=1, source_target_pairs={{0,8},{8,0},{16,24},{24,16},{1,9},{9,1},{17,25},{25,17},{2,10},{10... | collective-permute-start | bytes 393224 | tf_op jit(solution)/shard_map/ppermute | solution.py:421
  13.6 3.0 %collective-permute-start.3 = (bf16[32,1024]{1,0:T(8,128)(2,1)S(1)}, bf16[32,1024]{1,0:T(8,128)(2,1)S(1)}, u32[]{:S(2)}, u32[]{:S(2)}) collective-permute-start(bf16[32,1024]{1,0:T(8,128)(2,1)S(1)} %collective-permute-done.2.refs_1_), channel_id=1, source_target_pairs={{0,1},{1,0},{2,3},{3,2},{4,5},{5,4},{6,7},{7,6},{8,9},{9,8},{10,11... | collective-permute-start | bytes 196616 | tf_op jit(solution)/shard_map/ppermute | solution.py:391
  15.7 1.3 %collective-permute-start.5 = (bf16[32,1024]{1,0:T(8,128)(2,1)S(1)}, bf16[32,1024]{1,0:T(8,128)(2,1)S(1)}, u32[]{:S(2)}, u32[]{:S(2)}) collective-permute-start(bf16[32,1024]{1,0:T(8,128)(2,1)S(1)} %collective-permute-done.4.refs_3_.refs_2_), channel_id=1, source_target_pairs={{0,1},{1,0},{2,3},{3,2},{4,5},{5,4},{6,7},{7,6},{8,9},{9,8},{10,11... | collective-permute-start | bytes 196616 | tf_op jit(solution)/shard_map/ppermute | solution.py:391
  19.8 5.4 %collective-permute-start.10 = (s16[16,1408]{1,0:T(8,128)(2,1)S(1)}, s16[16,1408]{1,0:T(8,128)(2,1)S(1)}, u32[]{:S(2)}, u32[]{:S(2)}) collective-permute-start(s16[16,1408]{1,0:T(8,128)(2,1)S(1)} %get-tuple-element.25), channel_id=1, source_target_pairs={{0,6},{1,7},{2,4},{3,5},{4,2},{5,3},{6,0},{7,1},{8,14},{9,15},{10,... | collective-permute-start | bytes 135176 | tf_op jit(solution)/shard_map/ppermute | solution.py:391
  21.7 4.0 %collective-permute-start.11 = (s16[16,1408]{1,0:T(8,128)(2,1)S(1)}, s16[16,1408]{1,0:T(8,128)(2,1)S(1)}, u32[]{:S(2)}, u32[]{:S(2)}) collective-permute-start(s16[16,1408]{1,0:T(8,128)(2,1)S(1)} %get-tuple-element.26), channel_id=1, source_target_pairs={{0,4},{1,5},{2,6},{3,7},{4,0},{5,1},{6,2},{7,3},{8,12},{9,13},{10,... | collective-permute-start | bytes 135176 | tf_op jit(solution)/shard_map/ppermute | solution.py:391
  22.7 4.0 %collective-permute-start.9 = (s16[16,1408]{1,0:T(8,128)(2,1)S(1)}, s16[16,1408]{1,0:T(8,128)(2,1)S(1)}, u32[]{:S(2)}, u32[]{:S(2)}) collective-permute-start(s16[16,1408]{1,0:T(8,128)(2,1)S(1)} %get-tuple-element.24), channel_id=1, source_target_pairs={{0,2},{1,3},{2,0},{3,1},{4,6},{5,7},{6,4},{7,5},{8,10},{9,11},{10,... | collective-permute-start | bytes 135176 | tf_op jit(solution)/shard_map/ppermute | solution.py:391

commit v4 on v2

--- a/solution.py
+++ b/solution.py
@@ -55,29 +55,21 @@
     chips,
     per_chip,
     capacity,
-    slip_hbm,
-    slots_hbm,
-    green_hbm,
+    slip_ref,
+    slots_ref,
+    green_ref,
     out_ref,
     send_ref,
     pick_ref,
-    green_ref,
-    slip_ref,
-    slots_ref,
-    sems,
+    tiles_ref,
 ):
-    fetch_slips = pltpu.make_async_copy(slip_hbm, slip_ref, sems.at[0])
-    fetch_slots = pltpu.make_async_copy(slots_hbm, slots_ref, sems.at[1])
-    fetch_greens = pltpu.make_async_copy(green_hbm, green_ref, sems.at[2])
-    fetch_slips.start()
-    fetch_slots.start()
-    fetch_greens.start()
-    fetch_slots.wait()
-    mark_tiles(chips, per_chip, capacity, green_hbm.shape[0], slots_ref, send_ref, pick_ref)
-    fetch_slips.wait()
+    width = green_ref.shape[0]
+    mark_tiles(chips, per_chip, capacity, width, slots_ref, send_ref, pick_ref)
     core = lax.rem(lax.axis_index("patch"), 2)
     arrange_half(slip_ref, out_ref, core, core)
-    fetch_greens.wait()
+    tiles = green_ref[...].astype(jnp.float32)
+    for comp in range(green_ref.shape[1]):
+        tiles_ref[comp * width : (comp + 1) * width, :] = tiles[:, comp, :].astype(jnp.bfloat16)
 
 
 def arrange_other_kernel(slip_ref, green_ref, block_ref, out_ref):
@@ -85,33 +77,23 @@
     arrange_half(slip_ref, out_ref, core, 1 - core)
 
 
-def in_hbm(*values):
-    return [pltpu.with_memory_space_constraint(value, pltpu.HBM) for value in values]
-
-
 def arrange_own(slips, slots, greens, chips, per_chip, capacity):
     patches, both, samples = slips.shape
-    width = greens.shape[0]
+    width, components, lags = greens.shape
     block = jax.ShapeDtypeStruct(
         (samples // BLOCK * both // 2, 2 * patches * BLOCK), jnp.bfloat16
     )
     return pl.pallas_call(
         functools.partial(arrange_own_kernel, chips, per_chip, capacity),
-        in_specs=[pl.BlockSpec(memory_space=pltpu.HBM)] * 3,
         out_shape=(
             block,
             jax.ShapeDtypeStruct((chips * capacity, 2 * width), jnp.bfloat16),
             jax.ShapeDtypeStruct((chips * capacity, per_chip), jnp.bfloat16),
-            jax.ShapeDtypeStruct(greens.shape, greens.dtype),
+            jax.ShapeDtypeStruct((components * width, lags), jnp.bfloat16),
         ),
-        scratch_shapes=[
-            pltpu.VMEM(slips.shape, slips.dtype),
-            pltpu.VMEM(slots.shape, slots.dtype),
-            pltpu.SemaphoreType.DMA((3,)),
-        ],
         compiler_params=params(),
         name="arrange_own",
-    )(*in_hbm(slips, slots, greens))
+    )(slips, slots, greens)
 
 
 def arrange_other(slips, greens, block):
@@ -180,10 +162,14 @@
     capacity = send_ref.shape[0] // chips
     half = capacity // 2
     core = lax.rem(lax.axis_index("patch"), 2)
-    tiles = jnp.concatenate([own_ref[...], other_ref[...]], axis=0).astype(jnp.float32)
+    width, components, _ = other_ref.shape
+    tiles = other_ref[...].astype(jnp.float32)
     by_comp = []
-    for comp in range(own_ref.shape[1]):
-        both = tiles[:, comp, :].astype(jnp.bfloat16)
+    for comp in range(components):
+        both = jnp.concatenate(
+            [own_ref[comp * width : (comp + 1) * width, :], tiles[:, comp, :].astype(jnp.bfloat16)],
+            axis=0,
+        )
         chosen = jnp.dot(send_ref[...], both, preferred_element_type=jnp.float32)
         chosen = [chosen[step * capacity : (step + 1) * capacity] for step in range(chips)]
         last = chosen[-1]
@@ -197,7 +183,7 @@
 
 
 def route_tiles(send, own, other, after, chips):
-    components, lags = own.shape[1:]
+    components, lags = other.shape[1:]
     rows = components * send.shape[0] // chips
     shape = jax.ShapeDtypeStruct((rows, lags), jnp.bfloat16)
     part = jax.ShapeDtypeStruct((rows // 2, lags), jnp.bfloat16)
@@ -295,9 +281,23 @@
             out_ref[step, comp * rows : (comp + 1) * rows, :] = total
 
 
+def unit_of(exponent):
+    return jnp.exp2(exponent.astype(jnp.float32) * (1.0 / STEPS)) * (1.0 / LARGEST)
+
+
+def as_sent(total, lanes):
+    peak = jnp.maximum(jnp.max(jnp.abs(total), axis=1, keepdims=True), SMALLEST)
+    exponent = jnp.ceil(jnp.log2(peak) * STEPS).astype(jnp.int32)
+    whole = jnp.clip(jnp.round(total * (1.0 / unit_of(exponent))), -LARGEST, LARGEST)
+    rest = jnp.broadcast_to(exponent, (total.shape[0], lanes - total.shape[1]))
+    return jnp.concatenate([whole.astype(jnp.int32), rest], axis=1).astype(jnp.int16)
+
+
 def convolve_first_kernel(rows, shifted_ref, *refs):
-    slip_refs, (out_ref, stack_ref, product_ref) = refs[:-3], refs[-3:]
+    slip_refs, (out_ref, sent_ref, stack_ref, product_ref) = refs[:-4], refs[-4:]
     convolve_blocks(shifted_ref, slip_refs, stack_ref, product_ref, out_ref, rows)
+    for step in range(out_ref.shape[0]):
+        sent_ref[step] = as_sent(out_ref[step], sent_ref.shape[2])
 
 
 def convolve_scratch(shifted, count, height, depth, components):
@@ -308,47 +308,44 @@
 
 
 def convolve_first(shifted, slips, rows, components, length):
-    shape = jax.ShapeDtypeStruct((len(slips), components * rows, length), jnp.float32)
+    size = (len(slips), components * rows)
+    lanes = round_up(length, LANES) + LANES
     return pl.pallas_call(
         functools.partial(convolve_first_kernel, rows),
-        out_shape=shape,
+        out_shape=(
+            jax.ShapeDtypeStruct(size + (length,), jnp.float32),
+            jax.ShapeDtypeStruct(size + (lanes,), jnp.int16),
+        ),
         scratch_shapes=convolve_scratch(shifted, len(slips), *slips[0].shape, components),
         compiler_params=params(),
         name="convolve_first",
     )(shifted, *slips)
 
 
-def unit_of(exponent):
-    return jnp.exp2(exponent.astype(jnp.float32) * (1.0 / STEPS)) * (1.0 / LARGEST)
-
-
-def convolve_last_kernel(rows, shifted_ref, slip_ref, first_ref, *refs):
+def convolve_last_kernel(rows, shifted_ref, slip_ref, first_ref, early_ref, *refs):
     out_refs, (stack_ref, product_ref, last_ref) = refs[:-3], refs[-3:]
     convolve_blocks(shifted_ref, [slip_ref], stack_ref, product_ref, last_ref, rows)
     count = first_ref.shape[0]
-    length = first_ref.shape[2]
     turn = lax.axis_index("site") ^ (lax.axis_index("patch") // 2)
     last = last_ref[0]
+    late = as_sent(last, early_ref.shape[2])
     for step, ref in enumerate(out_refs):
         source = step ^ turn
-        total = jnp.where(source == count, last, first_ref[jnp.minimum(source, count - 1)])
-        if step == 0:
-            ref[...] = total
-            continue
-        peak = jnp.maximum(jnp.max(jnp.abs(total), axis=1, keepdims=True), SMALLEST)
-        exponent = jnp.ceil(jnp.log2(peak) * STEPS).astype(jnp.int32)
-        scaled = jnp.round(total * (1.0 / unit_of(exponent)))
-        whole = jnp.clip(scaled, -LARGEST, LARGEST).astype(jnp.int32)
-        ref[:, :length] = whole.astype(jnp.int16)
-        ref[:, length:] = jnp.broadcast_to(
-            exponent, (exponent.shape[0], ref.shape[1] - length)
-        ).astype(jnp.int16)
-
-
-def convolve_last(shifted, slip, first, rows, components):
+        before = jnp.minimum(source, count - 1)
+
+        @pl.when(source == count)
+        def _():
+            ref[...] = late if step else last
+
+        @pl.when(source < count)
+        def _():
+            ref[...] = early_ref[before] if step else first_ref[before]
+
+
+def convolve_last(shifted, slip, first, early, rows, components):
     count, height, length = first.shape
     own = jax.ShapeDtypeStruct((height, length), jnp.float32)
-    sent = jax.ShapeDtypeStruct((height, round_up(length, LANES) + LANES), jnp.int16)
+    sent = jax.ShapeDtypeStruct(early.shape[1:], jnp.int16)
     return pl.pallas_call(
         functools.partial(convolve_last_kernel, rows),
         out_shape=(own,) + (sent,) * count,
@@ -356,7 +353,7 @@
         + [pltpu.VMEM((1, height, length), jnp.float32)],
         compiler_params=params(),
         name="convolve_last",
-    )(shifted, slip, first)
+    )(shifted, slip, first, early)
 
 
 def add_kernel(own_ref, *refs):
@@ -400,22 +397,22 @@
         slips = jnp.pad(slips, ((0, 0), (0, 0), (0, rows - part), (0, 0)))
         slips = slips.reshape(patches, 2 * rows, samples)
     greens = green_tiles[0]
-    other, other_tiles = over_patch(slips, 1), over_patch(greens, 1)
+    other_tiles, other = over_patch(greens, 1), over_patch(slips, 1)
     share = 2 * max(1, patches // devices)
     capacity = round_up(4 * share, 16)
-    block, send, pick, greens = arrange_own(
-        slips, patch_slot.reshape(1, -1), greens, chips, 2 * patches, capacity
+    own_slips, own_tiles = over_patch(slips, 0), over_patch(greens, 0)
+    block, send, pick, own_tiles = arrange_own(
+        own_slips, patch_slot.reshape(1, -1), own_tiles, chips, 2 * patches, capacity
     )
     block = arrange_other(other, other_tiles, block)
 
-    pieces = list(route_tiles(send, greens, other_tiles, block, chips))
-    arrived = []
-    for index, piece in enumerate(pieces[1:]):
-        hops = [(2 * index + 1, 2 * index + 2), (chips - 1, chips - 1)][index == len(pieces) - 2]
-        arrived.append(
-            lax.ppermute(piece, "patch", [(i, i ^ (2 * hops[i % 2])) for i in range(devices)])
+    pieces = list(route_tiles(send, own_tiles, other_tiles, block, chips))
+    arrived = [None] * (len(pieces) - 1)
+    for index in reversed(range(len(arrived))):
+        hops = [(2 * index + 1, 2 * index + 2), (chips - 1, chips - 1)][index == len(arrived) - 1]
+        arrived[index] = lax.ppermute(
+            pieces[1 + index], "patch", [(i, i ^ (2 * hops[i % 2])) for i in range(devices)]
         )
-
     pieces = pieces[:1]
     for piece in arrived:
         pieces += [piece, over_patch(piece, 1)]
@@ -432,8 +429,8 @@
     shifted = shift_tiles(pick, pieces, components)
 
     slips = [blocks[step] for step in range(sites)]
-    first = convolve_first(shifted, slips[:-1], rows, components, length)
-    sums = convolve_last(shifted, slips[-1], first, rows, components)
+    first, early = convolve_first(shifted, slips[:-1], rows, components, length)
+    sums = convolve_last(shifted, slips[-1], first, early, rows, components)
     order = [1, chips - 1] + list(range(2, chips - 1))
     sent = [over_patch(sums[step], 2 * step) for step in order]
     return add_up(sums[0], sent, part, components)[None]

time: 27 us -> 29.1 us (1.078)
  starting transfers between devices: 14.7 us -> 16.6 us
  Pallas kernels: 5.79 us -> 5.03 us
  local copies, waits for them, and re-layouts: 0 us -> 0.65 us
    ppermute x7 -> x9, starting transfers between devices: 4.57 us -> 6.38 us  [over_patch(): lax.ppermute(value, 'patch', [(i, i ^ offset) for i in range(devices)])]
    unnamed x0 -> x2, local copies, waits for them, and re-layouts: none -> 0.65 us
    pallas_call x1, Pallas kernels: 1.21 us -> 0.65 us  [arrange_own(): pl.pallas_call(functools.partial(arrange_own_kernel, chips, per_chip, cap...]
    pallas_call x1, Pallas kernels: 0.84 us -> 0.5 us  [route_tiles(): pl.pallas_call(functools.partial(route_kernel, chips), in_specs=[pl.Block...]
    ppermute x7 -> x9, waiting for transfers between devices: 4.49 us -> 4.63 us  [over_patch(): lax.ppermute(value, 'patch', [(i, i ^ offset) for i in range(devices)])]
  transfers between devices with their start and end apart: 12 -> 14, of which waited for: 7 -> 7; matrix products, arithmetic and copies ran while one was open for 0% -> 0% of each run, Pallas kernels for 15% -> 12%
where the time goes in v4:
time: 29.1 us; the launch traced here: 28.9 us
  starting transfers between devices  16.6 us (57%)
  waiting for transfers between devices  6.56 us (23%)
  Pallas kernels  5.03 us (17%)
  local copies, waits for them, and re-layouts  0.65 us (2%)
    ppermute x3, starting transfers between devices, local(): lax.ppermute(blocks[step - low], 'site', [(i, i ^ low) for i in range(sit...  7.16 us
    ppermute x9, starting transfers between devices, over_patch(): lax.ppermute(value, 'patch', [(i, i ^ offset) for i in range(devices)])  6.38 us
    ppermute x9, waiting for transfers between devices, over_patch(): lax.ppermute(value, 'patch', [(i, i ^ offset) for i in range(devices)])  4.63 us
    ppermute x2, starting transfers between devices, local(): lax.ppermute(pieces[1 + index], 'patch', [(i, i ^ 2 * hops[i % 2]) for i...  3.05 us
    ppermute x2, waiting for transfers between devices, local(): lax.ppermute(pieces[1 + index], 'patch', [(i, i ^ 2 * hops[i % 2]) for i...  1.75 us
    pallas_call x1, Pallas kernels, convolve_first(): pl.pallas_call(functools.partial(convolve_first_kernel, rows), out_shape=...  1.38 us
    pallas_call x1, Pallas kernels, shift_tiles(): pl.pallas_call(shift_kernel, out_shape=shape, compiler_params=params(), n...  0.82 us
    pallas_call x1, Pallas kernels, add_up(): pl.pallas_call(add_kernel, out_shape=jax.ShapeDtypeStruct((part, componen...  0.75 us
  transfers between devices with their start and end apart: 14, of which 7 were waited for; matrix products, arithmetic and copies ran while one was open for 0% of the time, Pallas kernels for 12%

profile of v4, /device:TPU:0, one launch (start us, length us, event | category | flops | bytes accessed | tf_op | source)
XLA Modules:
  0.0 28.9 jit_solution(1536154675183283310)
XLA Ops:
  0.0 0.9 %collective-permute-start.1 = (bf16[32,2,1024]{2,1,0:T(2,128)(2,1)}, bf16[32,2,1024]{2,1,0:T(2,128)(2,1)S(1)}, u32[]{:S(2)}, u32[]{:S(2)}) collective-permute-start(bf16[32,2,1024]{2,1,0:T(2,128)(2,1)} %bitcast.4), channel_id=1, source_target_pairs={{0,0},{1,1},{2,2},{3,3},{4,4},{5,5},{6,6},{7,7},{8,8},{9,9},{10,10... | collective-permute-start | bytes 393224 | tf_op jit(solution)/shard_map/ppermute | solution.py:392
  0.9 0.9 %collective-permute-start = (bf16[16,16,256]{2,1,0:T(8,128)(2,1)}, bf16[16,16,256]{2,1,0:T(8,128)(2,1)S(1)}, u32[]{:S(2)}, u32[]{:S(2)}) collective-permute-start(bf16[16,16,256]{2,1,0:T(8,128)(2,1)} %param.3), channel_id=1, source_target_pairs={{0,0},{1,1},{2,2},{3,3},{4,4},{5,5},{6,6},{7,7},{8,8},{9,9},{10,10... | collective-permute-start | bytes 393224 | tf_op jit(solution)/shard_map/ppermute | solution.py:392
  1.8 0.5 %collective-permute-start.2 = (bf16[32,2,1024]{2,1,0:T(2,128)(2,1)}, bf16[32,2,1024]{2,1,0:T(2,128)(2,1)S(1)}, u32[]{:S(2)}, u32[]{:S(2)}) collective-permute-start(bf16[32,2,1024]{2,1,0:T(2,128)(2,1)} %bitcast.5), channel_id=1, source_target_pairs={{0,1},{1,0},{2,3},{3,2},{4,5},{5,4},{6,7},{7,6},{8,9},{9,8},{10,11... | collective-permute-start | bytes 393224 | tf_op jit(solution)/shard_map/ppermute | solution.py:392
  2.3 0.1 collective-permute-start.3
  2.3 0.0 collective-permute-done.1.green_ref
  2.3 0.0 collective-permute-done.slip_ref
  2.3 0.7 %copy-done = s32[128]{0:T(128)S(1)} copy-done((s32[128]{0:T(128)S(1)}, s32[128]{0:T(128)}, u32[]{:S(2)}) %copy-start) | copy-done | bytes 536
  3.0 0.7 %arrange_own.1 = (bf16[128,512]{1,0:T(8,128)(2,1)S(1)}, bf16[64,64]{1,0:T(8,128)(2,1)S(1)}, bf16[64,32]{1,0:T(8,128)(2,1)S(1)}, bf16[64,1024]{1,0:T(8,128)(2,1)S(1)}) custom-call(bf16[16,16,256]{2,1,0:T(8,128)(2,1)S(1)} %collective-permute-done.slip_ref, s32[1,128]{1,0:T(1,128)S(1)} %bitcast.3, bf16[32,2,1024]{2,1,0:T(2,128)(2,1)S(1)} %collective-permute-done.1.green_ref), custom_call_target="tpu_custom_call" | custom-call | tf_op jit(solution)/shard_map/arrange_own/pallas_call | solution.py:86
  3.6 0.0 collective-permute-done.2.green_ref.other_ref
  3.7 0.2 collective-permute-done.3.slip_ref
  3.8 0.2 arrange_other.1.after_ref.refs_0_
  4.0 4.0 %collective-permute-start.8 = (bf16[128,512]{1,0:T(8,128)(2,1)S(1)}, bf16[128,512]{1,0:T(8,128)(2,1)S(1)}, u32[]{:S(2)}, u32[]{:S(2)}) collective-permute-start(bf16[128,512]{1,0:T(8,128)(2,1)S(1)} %arrange_other.1.after_ref.refs_0_), channel_id=1, source_target_pairs={{0,16},{8,24},{16,0},{24,8},{1,17},{9,25},{17,1},{25,9},{2,18},{10... | collective-permute-start | bytes 393224 | tf_op jit(solution)/shard_map/ppermute | solution.py:424
  8.0 0.5 %route_tiles.1 = (bf16[32,1024]{1,0:T(8,128)(2,1)S(1)}, bf16[32,1024]{1,0:T(8,128)(2,1)S(1)}, bf16[16,1024]{1,0:T(8,128)(2,1)S(1)}) custom-call(bf16[64,64]{1,0:T(8,128)(2,1)S(1)} %get-tuple-element.19.send_ref, bf16[64,1024]{1,0:T(8,128)(2,1)S(1)} %get-tuple-element.20.own_ref, bf16[32,2,1024]{2,1,0:T(2,128)(2,1)S(1)} %collective-permute-done.2.green_ref.other_ref, ...), custom_call_target="tpu_custom_call" | custom-call | tf_op jit(solution)/shard_map/route_tiles/pallas_call | solution.py:190
  8.5 1.6 %collective-permute-start.4 = (bf16[32,1024]{1,0:T(8,128)(2,1)S(1)}, bf16[32,1024]{1,0:T(8,128)(2,1)S(1)}, u32[]{:S(2)}, u32[]{:S(2)}) collective-permute-start(bf16[32,1024]{1,0:T(8,128)(2,1)S(1)} %get-tuple-element.23), channel_id=1, source_target_pairs={{0,2},{1,5},{2,0},{3,7},{4,6},{5,1},{6,4},{7,3},{8,10},{9,13},{10,... | collective-permute-start | bytes 196616 | tf_op jit(solution)/shard_map/ppermute | solution.py:413
  10.0 1.5 %collective-permute-start.6 = (bf16[16,1024]{1,0:T(8,128)(2,1)S(1)}, bf16[16,1024]{1,0:T(8,128)(2,1)S(1)}, u32[]{:S(2)}, u32[]{:S(2)}) collective-permute-start(bf16[16,1024]{1,0:T(8,128)(2,1)S(1)} %get-tuple-element.24), channel_id=1, source_target_pairs={{0,6},{1,7},{2,4},{3,5},{4,2},{5,3},{6,0},{7,1},{8,14},{9,15},{10,... | collective-permute-start | bytes 98312 | tf_op jit(solution)/shard_map/ppermute | solution.py:413
  11.5 1.6 %collective-permute-start.10 = (bf16[128,512]{1,0:T(8,128)(2,1)S(1)}, bf16[128,512]{1,0:T(8,128)(2,1)S(1)}, u32[]{:S(2)}, u32[]{:S(2)}) collective-permute-start(bf16[128,512]{1,0:T(8,128)(2,1)S(1)} %arrange_other.1.after_ref.refs_0_), channel_id=1, source_target_pairs={{0,8},{8,0},{16,24},{24,16},{1,9},{9,1},{17,25},{25,17},{2,10},{10... | collective-permute-start | bytes 393224 | tf_op jit(solution)/shard_map/ppermute | solution.py:424
  13.1 1.7 %collective-permute-done.6.refs_3_.refs_2_ = bf16[16,1024]{1,0:T(8,128)(2,1)S(1)} collective-permute-done((bf16[16,1024]{1,0:T(8,128)(2,1)S(1)}, bf16[16,1024]{1,0:T(8,128)(2,1)S(1)}, u32[]{:S(2)}, u32[]{:S(2)}) %collective-permute-start.6) | collective-permute-done | bytes 32800 | tf_op jit(solution)/shard_map/ppermute | solution.py:413
  14.9 0.0 collective-permute-done.4.refs_1_
  14.9 1.6 %collective-permute-start.9 = (bf16[128,512]{1,0:T(8,128)(2,1)S(1)}, bf16[128,512]{1,0:T(8,128)(2,1)S(1)}, u32[]{:S(2)}, u32[]{:S(2)}) collective-permute-start(bf16[128,512]{1,0:T(8,128)(2,1)S(1)} %pass_on.1.refs_2_), channel_id=1, source_target_pairs={{0,8},{8,0},{16,24},{24,16},{1,9},{9,1},{17,25},{25,17},{2,10},{10... | collective-permute-start | bytes 393224 | tf_op jit(solution)/shard_map/ppermute | solution.py:424
  16.5 0.5 %collective-permute-start.7 = (bf16[16,1024]{1,0:T(8,128)(2,1)S(1)}, bf16[16,1024]{1,0:T(8,128)(2,1)S(1)}, u32[]{:S(2)}, u32[]{:S(2)}) collective-permute-start(bf16[16,1024]{1,0:T(8,128)(2,1)S(1)} %collective-permute-done.6.refs_3_.refs_2_), channel_id=1, source_target_pairs={{0,1},{1,0},{2,3},{3,2},{4,5},{5,4},{6,7},{7,6},{8,9},{9,8},{10,11... | collective-permute-start | bytes 98312 | tf_op jit(solution)/shard_map/ppermute | solution.py:392
  17.0 0.9 %collective-permute-done.7.refs_4_ = bf16[16,1024]{1,0:T(8,128)(2,1)S(1)} collective-permute-done((bf16[16,1024]{1,0:T(8,128)(2,1)S(1)}, bf16[16,1024]{1,0:T(8,128)(2,1)S(1)}, u32[]{:S(2)}, u32[]{:S(2)}) %collective-permute-start.7) | collective-permute-done | bytes 32800 | tf_op jit(solution)/shard_map/ppermute | solution.py:392
  17.9 0.8 %shift_tiles.1.shifted_ref = bf16[512,2304]{1,0:T(8,128)(2,1)S(1)} custom-call(bf16[64,32]{1,0:T(8,128)(2,1)S(1)} %get-tuple-element.18.pick_ref, bf16[32,1024]{1,0:T(8,128)(2,1)S(1)} %get-tuple-element.22.refs_0_, bf16[32,1024]{1,0:T(8,128)(2,1)S(1)} %collective-permute-done.4.refs_1_, bf16[32,1024]{1,0:T(8,128)(2,1)S(1)} %collective-permute-done.5.refs_2_, ...), custom_call_target="tpu_custom_call" | custom-call | tf_op jit(solution)/shard_map/shift_tiles/pallas_call | solution.py:244
  18.7 1.4 %convolve_first.1 = (f32[3,16,1280]{2,1,0:T(8,128)S(1)}, s16[3,16,1408]{2,1,0:T(8,128)(2,1)S(1)}) custom-call(bf16[512,2304]{1,0:T(8,128)(2,1)S(1)} %shift_tiles.1.shifted_ref, bf16[128,512]{1,0:T(8,128)(2,1)S(1)} %arrange_other.1.after_ref.refs_0_, bf16[128,512]{1,0:T(8,128)(2,1)S(1)} %collective-permute-done.10.refs_1_, bf16[128,512]{1,0:T(8,128)(2,1)S(1)} %pass_on.1.refs_2_), custom_call_target="tpu_custom_call" | custom-call | tf_op jit(solution)/shard_map/convolve_first/pallas_call | solution.py:313
  20.1 0.2 collective-permute-done.9.slip_ref
  20.3 0.7 %convolve_last.1 = (f32[16,1280]{1,0:T(8,128)S(1)}, s16[16,1408]{1,0:T(8,128)(2,1)S(1)}, s16[16,1408]{1,0:T(8,128)(2,1)S(1)}, s16[16,1408]{1,0:T(8,128)(2,1)S(1)}) custom-call(bf16[512,2304]{1,0:T(8,128)(2,1)S(1)} %shift_tiles.1.shifted_ref, bf16[128,512]{1,0:T(8,128)(2,1)S(1)} %collective-permute-done.9.slip_ref, ...), custom_call_target="tpu_custom_call" | custom-call | tf_op jit(solution)/shard_map/convolve_last/pallas_call | solution.py:349
  21.0 1.1 %collective-permute-start.11 = (s16[16,1408]{1,0:T(8,128)(2,1)S(1)}, s16[16,1408]{1,0:T(8,128)(2,1)S(1)}, u32[]{:S(2)}, u32[]{:S(2)}) collective-permute-start(s16[16,1408]{1,0:T(8,128)(2,1)S(1)} %get-tuple-element.28), channel_id=1, source_target_pairs={{0,2},{1,3},{2,0},{3,1},{4,6},{5,7},{6,4},{7,5},{8,10},{9,11},{10,... | collective-permute-start | bytes 135176 | tf_op jit(solution)/shard_map/ppermute | solution.py:392
  22.1 2.0 %collective-permute-start.12 = (s16[16,1408]{1,0:T(8,128)(2,1)S(1)}, s16[16,1408]{1,0:T(8,128)(2,1)S(1)}, u32[]{:S(2)}, u32[]{:S(2)}) collective-permute-start(s16[16,1408]{1,0:T(8,128)(2,1)S(1)} %get-tuple-element.29), channel_id=1, source_target_pairs={{0,6},{1,7},{2,4},{3,5},{4,2},{5,3},{6,0},{7,1},{8,14},{9,15},{10,... | collective-permute-start | bytes 135176 | tf_op jit(solution)/shard_map/ppermute | solution.py:392
  24.1 0.5 %collective-permute-start.13 = (s16[16,1408]{1,0:T(8,128)(2,1)S(1)}, s16[16,1408]{1,0:T(8,128)(2,1)S(1)}, u32[]{:S(2)}, u32[]{:S(2)}) collective-permute-start(s16[16,1408]{1,0:T(8,128)(2,1)S(1)} %get-tuple-element.30), channel_id=1, source_target_pairs={{0,4},{1,5},{2,6},{3,7},{4,0},{5,1},{6,2},{7,3},{8,12},{9,13},{10,... | collective-permute-start | bytes 135176 | tf_op jit(solution)/shard_map/ppermute | solution.py:392
  24.6 0.7 %collective-permute-done.11.refs_0_ = s16[16,1408]{1,0:T(8,128)(2,1)S(1)} collective-permute-done((s16[16,1408]{1,0:T(8,128)(2,1)S(1)}, s16[16,1408]{1,0:T(8,128)(2,1)S(1)}, u32[]{:S(2)}, u32[]{:S(2)}) %collective-permute-start.11) | collective-permute-done | bytes 45088 | tf_op jit(solution)/shard_map/ppermute | solution.py:392
  25.3 1.9 %collective-permute-done.12.refs_1_ = s16[16,1408]{1,0:T(8,128)(2,1)S(1)} collective-permute-done((s16[16,1408]{1,0:T(8,128)(2,1)S(1)}, s16[16,1408]{1,0:T(8,128)(2,1)S(1)}, u32[]{:S(2)}, u32[]{:S(2)}) %collective-permute-start.12) | collective-permute-done | bytes 45088 | tf_op jit(solution)/shard_map/ppermute | solution.py:392
  27.1 1.0 %collective-permute-done.13.refs_2_ = s16[16,1408]{1,0:T(8,128)(2,1)S(1)} collective-permute-done((s16[16,1408]{1,0:T(8,128)(2,1)S(1)}, s16[16,1408]{1,0:T(8,128)(2,1)S(1)}, u32[]{:S(2)}, u32[]{:S(2)}) %collective-permute-start.13) | collective-permute-done | bytes 45088 | tf_op jit(solution)/shard_map/ppermute | solution.py:392
  28.2 0.7 %add_up.1 = f32[8,2,1280]{2,1,0:T(2,128)} custom-call(f32[16,1280]{1,0:T(8,128)S(1)} %get-tuple-element.27.own_ref, s16[16,1408]{1,0:T(8,128)(2,1)S(1)} %collective-permute-done.11.refs_0_, s16[16,1408]{1,0:T(8,128)(2,1)S(1)} %collective-permute-done.12.refs_1_, s16[16,1408]{1,0:T(8,128)(2,1)S(1)} %collective-permute-done.13.refs_2_), custom_call_target="tpu_custom_call" | custom-call | tf_op jit(solution)/shard_map/add_up/pallas_call | solution.py:372
  (6 shorter events, 0.0 us)
Async XLA Ops:
  0.0 2.3 %collective-permute-start.1 = (bf16[32,2,1024]{2,1,0:T(2,128)(2,1)}, bf16[32,2,1024]{2,1,0:T(2,128)(2,1)S(1)}, u32[]{:S(2)}, u32[]{:S(2)}) collective-permute-start(bf16[32,2,1024]{2,1,0:T(2,128)(2,1)} %bitcast.4), channel_id=1, source_target_pairs={{0,0},{1,1},{2,2},{3,3},{4,4},{5,5},{6,6},{7,7},{8,8},{9,9},{10,10... | collective-permute-start | bytes 393224 | tf_op jit(solution)/shard_map/ppermute | solution.py:392
  0.9 1.4 %collective-permute-start = (bf16[16,16,256]{2,1,0:T(8,128)(2,1)}, bf16[16,16,256]{2,1,0:T(8,128)(2,1)S(1)}, u32[]{:S(2)}, u32[]{:S(2)}) collective-permute-start(bf16[16,16,256]{2,1,0:T(8,128)(2,1)} %param.3), channel_id=1, source_target_pairs={{0,0},{1,1},{2,2},{3,3},{4,4},{5,5},{6,6},{7,7},{8,8},{9,9},{10,10... | collective-permute-start | bytes 393224 | tf_op jit(solution)/shard_map/ppermute | solution.py:392
  1.8 1.8 %collective-permute-start.2 = (bf16[32,2,1024]{2,1,0:T(2,128)(2,1)}, bf16[32,2,1024]{2,1,0:T(2,128)(2,1)S(1)}, u32[]{:S(2)}, u32[]{:S(2)}) collective-permute-start(bf16[32,2,1024]{2,1,0:T(2,128)(2,1)} %bitcast.5), channel_id=1, source_target_pairs={{0,1},{1,0},{2,3},{3,2},{4,5},{5,4},{6,7},{7,6},{8,9},{9,8},{10,11... | collective-permute-start | bytes 393224 | tf_op jit(solution)/shard_map/ppermute | solution.py:392
  2.3 1.6 %collective-permute-start.3 = (bf16[16,16,256]{2,1,0:T(8,128)(2,1)}, bf16[16,16,256]{2,1,0:T(8,128)(2,1)S(1)}, u32[]{:S(2)}, u32[]{:S(2)}) collective-permute-start(bf16[16,16,256]{2,1,0:T(8,128)(2,1)} %param.3), channel_id=1, source_target_pairs={{0,1},{1,0},{2,3},{3,2},{4,5},{5,4},{6,7},{7,6},{8,9},{9,8},{10,11... | collective-permute-start | bytes 393224 | tf_op jit(solution)/shard_map/ppermute | solution.py:392
  2.3 0.7 %copy-start = (s32[128]{0:T(128)S(1)}, s32[128]{0:T(128)}, u32[]{:S(2)}) copy-start(s32[128]{0:T(128)} %param.5) | copy-start | bytes 1540
  4.0 10.8 %collective-permute-start.8 = (bf16[128,512]{1,0:T(8,128)(2,1)S(1)}, bf16[128,512]{1,0:T(8,128)(2,1)S(1)}, u32[]{:S(2)}, u32[]{:S(2)}) collective-permute-start(bf16[128,512]{1,0:T(8,128)(2,1)S(1)} %arrange_other.1.after_ref.refs_0_), channel_id=1, source_target_pairs={{0,16},{8,24},{16,0},{24,8},{1,17},{9,25},{17,1},{25,9},{2,18},{10... | collective-permute-start | bytes 393224 | tf_op jit(solution)/shard_map/ppermute | solution.py:424
  8.5 6.4 %collective-permute-start.4 = (bf16[32,1024]{1,0:T(8,128)(2,1)S(1)}, bf16[32,1024]{1,0:T(8,128)(2,1)S(1)}, u32[]{:S(2)}, u32[]{:S(2)}) collective-permute-start(bf16[32,1024]{1,0:T(8,128)(2,1)S(1)} %get-tuple-element.23), channel_id=1, source_target_pairs={{0,2},{1,5},{2,0},{3,7},{4,6},{5,1},{6,4},{7,3},{8,10},{9,13},{10,... | collective-permute-start | bytes 196616 | tf_op jit(solution)/shard_map/ppermute | solution.py:413
  10.0 4.8 %collective-permute-start.6 = (bf16[16,1024]{1,0:T(8,128)(2,1)S(1)}, bf16[16,1024]{1,0:T(8,128)(2,1)S(1)}, u32[]{:S(2)}, u32[]{:S(2)}) collective-permute-start(bf16[16,1024]{1,0:T(8,128)(2,1)S(1)} %get-tuple-element.24), channel_id=1, source_target_pairs={{0,6},{1,7},{2,4},{3,5},{4,2},{5,3},{6,0},{7,1},{8,14},{9,15},{10,... | collective-permute-start | bytes 98312 | tf_op jit(solution)/shard_map/ppermute | solution.py:413
  11.5 7.2 %collective-permute-start.10 = (bf16[128,512]{1,0:T(8,128)(2,1)S(1)}, bf16[128,512]{1,0:T(8,128)(2,1)S(1)}, u32[]{:S(2)}, u32[]{:S(2)}) collective-permute-start(bf16[128,512]{1,0:T(8,128)(2,1)S(1)} %arrange_other.1.after_ref.refs_0_), channel_id=1, source_target_pairs={{0,8},{8,0},{16,24},{24,16},{1,9},{9,1},{17,25},{25,17},{2,10},{10... | collective-permute-start | bytes 393224 | tf_op jit(solution)/shard_map/ppermute | solution.py:424
  14.9 5.4 %collective-permute-start.9 = (bf16[128,512]{1,0:T(8,128)(2,1)S(1)}, bf16[128,512]{1,0:T(8,128)(2,1)S(1)}, u32[]{:S(2)}, u32[]{:S(2)}) collective-permute-start(bf16[128,512]{1,0:T(8,128)(2,1)S(1)} %pass_on.1.refs_2_), channel_id=1, source_target_pairs={{0,8},{8,0},{16,24},{24,16},{1,9},{9,1},{17,25},{25,17},{2,10},{10... | collective-permute-start | bytes 393224 | tf_op jit(solution)/shard_map/ppermute | solution.py:424
  16.5 1.4 %collective-permute-start.5 = (bf16[32,1024]{1,0:T(8,128)(2,1)S(1)}, bf16[32,1024]{1,0:T(8,128)(2,1)S(1)}, u32[]{:S(2)}, u32[]{:S(2)}) collective-permute-start(bf16[32,1024]{1,0:T(8,128)(2,1)S(1)} %collective-permute-done.4.refs_1_), channel_id=1, source_target_pairs={{0,1},{1,0},{2,3},{3,2},{4,5},{5,4},{6,7},{7,6},{8,9},{9,8},{10,11... | collective-permute-start | bytes 196616 | tf_op jit(solution)/shard_map/ppermute | solution.py:392
  16.5 1.4 %collective-permute-start.7 = (bf16[16,1024]{1,0:T(8,128)(2,1)S(1)}, bf16[16,1024]{1,0:T(8,128)(2,1)S(1)}, u32[]{:S(2)}, u32[]{:S(2)}) collective-permute-start(bf16[16,1024]{1,0:T(8,128)(2,1)S(1)} %collective-permute-done.6.refs_3_.refs_2_), channel_id=1, source_target_pairs={{0,1},{1,0},{2,3},{3,2},{4,5},{5,4},{6,7},{7,6},{8,9},{9,8},{10,11... | collective-permute-start | bytes 98312 | tf_op jit(solution)/shard_map/ppermute | solution.py:392
  21.0 4.3 %collective-permute-start.11 = (s16[16,1408]{1,0:T(8,128)(2,1)S(1)}, s16[16,1408]{1,0:T(8,128)(2,1)S(1)}, u32[]{:S(2)}, u32[]{:S(2)}) collective-permute-start(s16[16,1408]{1,0:T(8,128)(2,1)S(1)} %get-tuple-element.28), channel_id=1, source_target_pairs={{0,2},{1,3},{2,0},{3,1},{4,6},{5,7},{6,4},{7,5},{8,10},{9,11},{10,... | collective-permute-start | bytes 135176 | tf_op jit(solution)/shard_map/ppermute | solution.py:392
  22.1 5.1 %collective-permute-start.12 = (s16[16,1408]{1,0:T(8,128)(2,1)S(1)}, s16[16,1408]{1,0:T(8,128)(2,1)S(1)}, u32[]{:S(2)}, u32[]{:S(2)}) collective-permute-start(s16[16,1408]{1,0:T(8,128)(2,1)S(1)} %get-tuple-element.29), channel_id=1, source_target_pairs={{0,6},{1,7},{2,4},{3,5},{4,2},{5,3},{6,0},{7,1},{8,14},{9,15},{10,... | collective-permute-start | bytes 135176 | tf_op jit(solution)/shard_map/ppermute | solution.py:392
  24.1 4.0 %collective-permute-start.13 = (s16[16,1408]{1,0:T(8,128)(2,1)S(1)}, s16[16,1408]{1,0:T(8,128)(2,1)S(1)}, u32[]{:S(2)}, u32[]{:S(2)}) collective-permute-start(s16[16,1408]{1,0:T(8,128)(2,1)S(1)} %get-tuple-element.30), channel_id=1, source_target_pairs={{0,4},{1,5},{2,6},{3,7},{4,0},{5,1},{6,2},{7,3},{8,12},{9,13},{10,... | collective-permute-start | bytes 135176 | tf_op jit(solution)/shard_map/ppermute | solution.py:392

commit v5 on v4

--- a/solution.py
+++ b/solution.py
@@ -55,18 +55,31 @@
     chips,
     per_chip,
     capacity,
-    slip_ref,
-    slots_ref,
-    green_ref,
+    slip_hbm,
+    slots_hbm,
+    green_hbm,
     out_ref,
     send_ref,
     pick_ref,
     tiles_ref,
+    slip_ref,
+    slots_ref,
+    green_ref,
+    sems,
 ):
     width = green_ref.shape[0]
+    fetch_slips = pltpu.make_async_copy(slip_hbm, slip_ref, sems.at[0])
+    fetch_slots = pltpu.make_async_copy(slots_hbm, slots_ref, sems.at[1])
+    fetch_greens = pltpu.make_async_copy(green_hbm, green_ref, sems.at[2])
+    fetch_slots.start()
+    fetch_slips.start()
+    fetch_greens.start()
+    fetch_slots.wait()
     mark_tiles(chips, per_chip, capacity, width, slots_ref, send_ref, pick_ref)
+    fetch_slips.wait()
     core = lax.rem(lax.axis_index("patch"), 2)
     arrange_half(slip_ref, out_ref, core, core)
+    fetch_greens.wait()
     tiles = green_ref[...].astype(jnp.float32)
     for comp in range(green_ref.shape[1]):
         tiles_ref[comp * width : (comp + 1) * width, :] = tiles[:, comp, :].astype(jnp.bfloat16)
@@ -75,6 +88,10 @@
 def arrange_other_kernel(slip_ref, green_ref, block_ref, out_ref):
     core = lax.rem(lax.axis_index("patch"), 2)
     arrange_half(slip_ref, out_ref, core, 1 - core)
+
+
+def in_hbm(*values):
+    return [pltpu.with_memory_space_constraint(value, pltpu.HBM) for value in values]
 
 
 def arrange_own(slips, slots, greens, chips, per_chip, capacity):
@@ -85,15 +102,22 @@
     )
     return pl.pallas_call(
         functools.partial(arrange_own_kernel, chips, per_chip, capacity),
+        in_specs=[pl.BlockSpec(memory_space=pltpu.HBM)] * 3,
         out_shape=(
             block,
             jax.ShapeDtypeStruct((chips * capacity, 2 * width), jnp.bfloat16),
             jax.ShapeDtypeStruct((chips * capacity, per_chip), jnp.bfloat16),
             jax.ShapeDtypeStruct((components * width, lags), jnp.bfloat16),
         ),
+        scratch_shapes=[
+            pltpu.VMEM(slips.shape, slips.dtype),
+            pltpu.VMEM(slots.shape, slots.dtype),
+            pltpu.VMEM(greens.shape, greens.dtype),
+            pltpu.SemaphoreType.DMA((3,)),
+        ],
         compiler_params=params(),
         name="arrange_own",
-    )(slips, slots, greens)
+    )(*in_hbm(slips, slots, greens))
 
 
 def arrange_other(slips, greens, block):
@@ -400,9 +424,8 @@
     other_tiles, other = over_patch(greens, 1), over_patch(slips, 1)
     share = 2 * max(1, patches // devices)
     capacity = round_up(4 * share, 16)
-    own_slips, own_tiles = over_patch(slips, 0), over_patch(greens, 0)
     block, send, pick, own_tiles = arrange_own(
-        own_slips, patch_slot.reshape(1, -1), own_tiles, chips, 2 * patches, capacity
+        slips, patch_slot.reshape(1, -1), greens, chips, 2 * patches, capacity
     )
     block = arrange_other(other, other_tiles, block)
 

time: 29.1 us -> 26.8 us (0.921)
  starting transfers between devices: 16.6 us -> 14.9 us
  Pallas kernels: 5.03 us -> 5.87 us
  waiting for transfers between devices: 6.56 us -> 5.73 us
  local copies, waits for them, and re-layouts: 0.65 us -> 0 us
    ppermute x9 -> x7, starting transfers between devices: 6.38 us -> 4.57 us  [over_patch(): lax.ppermute(value, 'patch', [(i, i ^ offset) for i in range(devices)])]
    pallas_call x1, Pallas kernels: 0.65 us -> 1.48 us  [arrange_own(): pl.pallas_call(functools.partial(arrange_own_kernel, chips, per_chip, cap...]
    ppermute x9 -> x7, waiting for transfers between devices: 4.63 us -> 3.96 us  [over_patch(): lax.ppermute(value, 'patch', [(i, i ^ offset) for i in range(devices)])]
    unnamed x2 -> x0, local copies, waits for them, and re-layouts: 0.65 us -> none
  transfers between devices with their start and end apart: 14 -> 12, of which waited for: 7 -> 5; matrix products, arithmetic and copies ran while one was open for 0% -> 0% of each run, Pallas kernels for 12% -> 16%
where the time goes in v5:
time: 26.8 us; the launch traced here: 26.6 us
  starting transfers between devices  14.9 us (56%)
  Pallas kernels  5.87 us (22%)
  waiting for transfers between devices  5.73 us (21%)
    ppermute x3, starting transfers between devices, local(): lax.ppermute(blocks[step - low], 'site', [(i, i ^ low) for i in range(sit...  7.31 us
    ppermute x7, starting transfers between devices, over_patch(): lax.ppermute(value, 'patch', [(i, i ^ offset) for i in range(devices)])  4.57 us
    ppermute x7, waiting for transfers between devices, over_patch(): lax.ppermute(value, 'patch', [(i, i ^ offset) for i in range(devices)])  3.96 us
    ppermute x2, starting transfers between devices, local(): lax.ppermute(pieces[1 + index], 'patch', [(i, i ^ 2 * hops[i % 2]) for i...  3.05 us
    ppermute x2, waiting for transfers between devices, local(): lax.ppermute(pieces[1 + index], 'patch', [(i, i ^ 2 * hops[i % 2]) for i...  1.75 us
    pallas_call x1, Pallas kernels, arrange_own(): pl.pallas_call(functools.partial(arrange_own_kernel, chips, per_chip, cap...  1.48 us
    pallas_call x1, Pallas kernels, convolve_first(): pl.pallas_call(functools.partial(convolve_first_kernel, rows), out_shape=...  1.38 us
    pallas_call x1, Pallas kernels, shift_tiles(): pl.pallas_call(shift_kernel, out_shape=shape, compiler_params=params(), n...  0.81 us
  transfers between devices with their start and end apart: 12, of which 5 were waited for; matrix products, arithmetic and copies ran while one was open for 0% of the time, Pallas kernels for 16%

profile of v5, /device:TPU:0, one launch (start us, length us, event | category | flops | bytes accessed | tf_op | source)
XLA Modules:
  0.0 26.6 jit_solution(2710356289134291165)
XLA Ops:
  0.0 0.5 %collective-permute-start = (bf16[32,2,1024]{2,1,0:T(2,128)(2,1)}, bf16[32,2,1024]{2,1,0:T(2,128)(2,1)S(1)}, u32[]{:S(2)}, u32[]{:S(2)}) collective-permute-start(bf16[32,2,1024]{2,1,0:T(2,128)(2,1)} %bitcast.3), channel_id=1, source_target_pairs={{0,1},{1,0},{2,3},{3,2},{4,5},{5,4},{6,7},{7,6},{8,9},{9,8},{10,11... | collective-permute-start | bytes 393224 | tf_op jit(solution)/shard_map/ppermute | solution.py:416
  0.5 0.1 collective-permute-start.1
  0.5 1.5 %arrange_own.1 = (bf16[128,512]{1,0:T(8,128)(2,1)S(1)}, bf16[64,64]{1,0:T(8,128)(2,1)S(1)}, bf16[64,32]{1,0:T(8,128)(2,1)S(1)}, bf16[64,1024]{1,0:T(8,128)(2,1)S(1)}) custom-call(bf16[16,16,256]{2,1,0:T(8,128)(2,1)} %slip_hbm.1, s32[1,128]{1,0:T(1,128)} %bitcast.5, bf16[32,2,1024]{2,1,0:T(2,128)(2,1)} %bitcast.4), custom_call_target="tpu_custom_call" | custom-call | tf_op jit(solution)/shard_map/arrange_own/pallas_call | solution.py:103
  2.0 0.0 collective-permute-done.green_ref.other_ref
  2.0 0.0 collective-permute-done.1.slip_ref
  2.0 0.2 arrange_other.1.after_ref.refs_0_
  2.2 4.1 %collective-permute-start.6 = (bf16[128,512]{1,0:T(8,128)(2,1)S(1)}, bf16[128,512]{1,0:T(8,128)(2,1)S(1)}, u32[]{:S(2)}, u32[]{:S(2)}) collective-permute-start(bf16[128,512]{1,0:T(8,128)(2,1)S(1)} %arrange_other.1.after_ref.refs_0_), channel_id=1, source_target_pairs={{0,16},{8,24},{16,0},{24,8},{1,17},{9,25},{17,1},{25,9},{2,18},{10... | collective-permute-start | bytes 393224 | tf_op jit(solution)/shard_map/ppermute | solution.py:447
  6.3 0.5 %route_tiles.1 = (bf16[32,1024]{1,0:T(8,128)(2,1)S(1)}, bf16[32,1024]{1,0:T(8,128)(2,1)S(1)}, bf16[16,1024]{1,0:T(8,128)(2,1)S(1)}) custom-call(bf16[64,64]{1,0:T(8,128)(2,1)S(1)} %get-tuple-element.19.send_ref, bf16[64,1024]{1,0:T(8,128)(2,1)S(1)} %get-tuple-element.20.own_ref, bf16[32,2,1024]{2,1,0:T(2,128)(2,1)S(1)} %collective-permute-done.green_ref.other_ref, ...), custom_call_target="tpu_custom_call" | custom-call | tf_op jit(solution)/shard_map/route_tiles/pallas_call | solution.py:214
  6.8 1.6 %collective-permute-start.2 = (bf16[32,1024]{1,0:T(8,128)(2,1)S(1)}, bf16[32,1024]{1,0:T(8,128)(2,1)S(1)}, u32[]{:S(2)}, u32[]{:S(2)}) collective-permute-start(bf16[32,1024]{1,0:T(8,128)(2,1)S(1)} %get-tuple-element.23), channel_id=1, source_target_pairs={{0,2},{1,5},{2,0},{3,7},{4,6},{5,1},{6,4},{7,3},{8,10},{9,13},{10,... | collective-permute-start | bytes 196616 | tf_op jit(solution)/shard_map/ppermute | solution.py:436
  8.4 1.5 %collective-permute-start.4 = (bf16[16,1024]{1,0:T(8,128)(2,1)S(1)}, bf16[16,1024]{1,0:T(8,128)(2,1)S(1)}, u32[]{:S(2)}, u32[]{:S(2)}) collective-permute-start(bf16[16,1024]{1,0:T(8,128)(2,1)S(1)} %get-tuple-element.24), channel_id=1, source_target_pairs={{0,6},{1,7},{2,4},{3,5},{4,2},{5,3},{6,0},{7,1},{8,14},{9,15},{10,... | collective-permute-start | bytes 98312 | tf_op jit(solution)/shard_map/ppermute | solution.py:436
  9.9 1.6 %collective-permute-start.8 = (bf16[128,512]{1,0:T(8,128)(2,1)S(1)}, bf16[128,512]{1,0:T(8,128)(2,1)S(1)}, u32[]{:S(2)}, u32[]{:S(2)}) collective-permute-start(bf16[128,512]{1,0:T(8,128)(2,1)S(1)} %arrange_other.1.after_ref.refs_0_), channel_id=1, source_target_pairs={{0,8},{8,0},{16,24},{24,16},{1,9},{9,1},{17,25},{25,17},{2,10},{10... | collective-permute-start | bytes 393224 | tf_op jit(solution)/shard_map/ppermute | solution.py:447
  11.5 1.7 %collective-permute-done.4.refs_3_.refs_2_ = bf16[16,1024]{1,0:T(8,128)(2,1)S(1)} collective-permute-done((bf16[16,1024]{1,0:T(8,128)(2,1)S(1)}, bf16[16,1024]{1,0:T(8,128)(2,1)S(1)}, u32[]{:S(2)}, u32[]{:S(2)}) %collective-permute-start.4) | collective-permute-done | bytes 32800 | tf_op jit(solution)/shard_map/ppermute | solution.py:436
  13.2 0.0 collective-permute-done.2.refs_1_
  13.2 0.0 collective-permute-done.6.refs_0_
  13.2 1.6 %collective-permute-start.7 = (bf16[128,512]{1,0:T(8,128)(2,1)S(1)}, bf16[128,512]{1,0:T(8,128)(2,1)S(1)}, u32[]{:S(2)}, u32[]{:S(2)}) collective-permute-start(bf16[128,512]{1,0:T(8,128)(2,1)S(1)} %pass_on.1.refs_2_), channel_id=1, source_target_pairs={{0,8},{8,0},{16,24},{24,16},{1,9},{9,1},{17,25},{25,17},{2,10},{10... | collective-permute-start | bytes 393224 | tf_op jit(solution)/shard_map/ppermute | solution.py:447
  14.9 0.0 collective-permute-start.3
  14.9 0.5 %collective-permute-start.5 = (bf16[16,1024]{1,0:T(8,128)(2,1)S(1)}, bf16[16,1024]{1,0:T(8,128)(2,1)S(1)}, u32[]{:S(2)}, u32[]{:S(2)}) collective-permute-start(bf16[16,1024]{1,0:T(8,128)(2,1)S(1)} %collective-permute-done.4.refs_3_.refs_2_), channel_id=1, source_target_pairs={{0,1},{1,0},{2,3},{3,2},{4,5},{5,4},{6,7},{7,6},{8,9},{9,8},{10,11... | collective-permute-start | bytes 98312 | tf_op jit(solution)/shard_map/ppermute | solution.py:416
  15.4 0.9 %collective-permute-done.5.refs_4_ = bf16[16,1024]{1,0:T(8,128)(2,1)S(1)} collective-permute-done((bf16[16,1024]{1,0:T(8,128)(2,1)S(1)}, bf16[16,1024]{1,0:T(8,128)(2,1)S(1)}, u32[]{:S(2)}, u32[]{:S(2)}) %collective-permute-start.5) | collective-permute-done | bytes 32800 | tf_op jit(solution)/shard_map/ppermute | solution.py:416
  16.2 0.0 collective-permute-done.3.refs_2_
  16.2 0.8 %shift_tiles.1.shifted_ref = bf16[512,2304]{1,0:T(8,128)(2,1)S(1)} custom-call(bf16[64,32]{1,0:T(8,128)(2,1)S(1)} %get-tuple-element.18.pick_ref, bf16[32,1024]{1,0:T(8,128)(2,1)S(1)} %get-tuple-element.22.refs_0_, bf16[32,1024]{1,0:T(8,128)(2,1)S(1)} %collective-permute-done.2.refs_1_, bf16[32,1024]{1,0:T(8,128)(2,1)S(1)} %collective-permute-done.3.refs_2_, ...), custom_call_target="tpu_custom_call" | custom-call | tf_op jit(solution)/shard_map/shift_tiles/pallas_call | solution.py:268
  17.0 0.0 collective-permute-done.8.refs_1_
  17.1 1.4 %convolve_first.1 = (f32[3,16,1280]{2,1,0:T(8,128)S(1)}, s16[3,16,1408]{2,1,0:T(8,128)(2,1)S(1)}) custom-call(bf16[512,2304]{1,0:T(8,128)(2,1)S(1)} %shift_tiles.1.shifted_ref, bf16[128,512]{1,0:T(8,128)(2,1)S(1)} %arrange_other.1.after_ref.refs_0_, bf16[128,512]{1,0:T(8,128)(2,1)S(1)} %collective-permute-done.8.refs_1_, bf16[128,512]{1,0:T(8,128)(2,1)S(1)} %pass_on.1.refs_2_), custom_call_target="tpu_custom_call" | custom-call | tf_op jit(solution)/shard_map/convolve_first/pallas_call | solution.py:337
  18.4 0.0 collective-permute-done.7.slip_ref
  18.5 0.7 %convolve_last.1 = (f32[16,1280]{1,0:T(8,128)S(1)}, s16[16,1408]{1,0:T(8,128)(2,1)S(1)}, s16[16,1408]{1,0:T(8,128)(2,1)S(1)}, s16[16,1408]{1,0:T(8,128)(2,1)S(1)}) custom-call(bf16[512,2304]{1,0:T(8,128)(2,1)S(1)} %shift_tiles.1.shifted_ref, bf16[128,512]{1,0:T(8,128)(2,1)S(1)} %collective-permute-done.7.slip_ref, ...), custom_call_target="tpu_custom_call" | custom-call | tf_op jit(solution)/shard_map/convolve_last/pallas_call | solution.py:373
  19.2 2.0 %collective-permute-start.10 = (s16[16,1408]{1,0:T(8,128)(2,1)S(1)}, s16[16,1408]{1,0:T(8,128)(2,1)S(1)}, u32[]{:S(2)}, u32[]{:S(2)}) collective-permute-start(s16[16,1408]{1,0:T(8,128)(2,1)S(1)} %get-tuple-element.29), channel_id=1, source_target_pairs={{0,6},{1,7},{2,4},{3,5},{4,2},{5,3},{6,0},{7,1},{8,14},{9,15},{10,... | collective-permute-start | bytes 135176 | tf_op jit(solution)/shard_map/ppermute | solution.py:416
  21.2 0.6 %collective-permute-start.11 = (s16[16,1408]{1,0:T(8,128)(2,1)S(1)}, s16[16,1408]{1,0:T(8,128)(2,1)S(1)}, u32[]{:S(2)}, u32[]{:S(2)}) collective-permute-start(s16[16,1408]{1,0:T(8,128)(2,1)S(1)} %get-tuple-element.30), channel_id=1, source_target_pairs={{0,4},{1,5},{2,6},{3,7},{4,0},{5,1},{6,2},{7,3},{8,12},{9,13},{10,... | collective-permute-start | bytes 135176 | tf_op jit(solution)/shard_map/ppermute | solution.py:416
  21.8 0.9 %collective-permute-start.9 = (s16[16,1408]{1,0:T(8,128)(2,1)S(1)}, s16[16,1408]{1,0:T(8,128)(2,1)S(1)}, u32[]{:S(2)}, u32[]{:S(2)}) collective-permute-start(s16[16,1408]{1,0:T(8,128)(2,1)S(1)} %get-tuple-element.28), channel_id=1, source_target_pairs={{0,2},{1,3},{2,0},{3,1},{4,6},{5,7},{6,4},{7,5},{8,10},{9,11},{10,... | collective-permute-start | bytes 135176 | tf_op jit(solution)/shard_map/ppermute | solution.py:416
  22.8 1.5 %collective-permute-done.10.refs_1_ = s16[16,1408]{1,0:T(8,128)(2,1)S(1)} collective-permute-done((s16[16,1408]{1,0:T(8,128)(2,1)S(1)}, s16[16,1408]{1,0:T(8,128)(2,1)S(1)}, u32[]{:S(2)}, u32[]{:S(2)}) %collective-permute-start.10) | collective-permute-done | bytes 45088 | tf_op jit(solution)/shard_map/ppermute | solution.py:416
  24.3 1.0 %collective-permute-done.11.refs_2_ = s16[16,1408]{1,0:T(8,128)(2,1)S(1)} collective-permute-done((s16[16,1408]{1,0:T(8,128)(2,1)S(1)}, s16[16,1408]{1,0:T(8,128)(2,1)S(1)}, u32[]{:S(2)}, u32[]{:S(2)}) %collective-permute-start.11) | collective-permute-done | bytes 45088 | tf_op jit(solution)/shard_map/ppermute | solution.py:416
  25.3 0.6 %collective-permute-done.9.refs_0_ = s16[16,1408]{1,0:T(8,128)(2,1)S(1)} collective-permute-done((s16[16,1408]{1,0:T(8,128)(2,1)S(1)}, s16[16,1408]{1,0:T(8,128)(2,1)S(1)}, u32[]{:S(2)}, u32[]{:S(2)}) %collective-permute-start.9) | collective-permute-done | bytes 45088 | tf_op jit(solution)/shard_map/ppermute | solution.py:416
  25.9 0.7 %add_up.1 = f32[8,2,1280]{2,1,0:T(2,128)} custom-call(f32[16,1280]{1,0:T(8,128)S(1)} %get-tuple-element.27.own_ref, s16[16,1408]{1,0:T(8,128)(2,1)S(1)} %collective-permute-done.9.refs_0_, s16[16,1408]{1,0:T(8,128)(2,1)S(1)} %collective-permute-done.10.refs_1_, s16[16,1408]{1,0:T(8,128)(2,1)S(1)} %collective-permute-done.11.refs_2_), custom_call_target="tpu_custom_call" | custom-call | tf_op jit(solution)/shard_map/add_up/pallas_call | solution.py:396
  (1 shorter events, 0.0 us)
Async XLA Ops:
  0.0 2.0 %collective-permute-start = (bf16[32,2,1024]{2,1,0:T(2,128)(2,1)}, bf16[32,2,1024]{2,1,0:T(2,128)(2,1)S(1)}, u32[]{:S(2)}, u32[]{:S(2)}) collective-permute-start(bf16[32,2,1024]{2,1,0:T(2,128)(2,1)} %bitcast.3), channel_id=1, source_target_pairs={{0,1},{1,0},{2,3},{3,2},{4,5},{5,4},{6,7},{7,6},{8,9},{9,8},{10,11... | collective-permute-start | bytes 393224 | tf_op jit(solution)/shard_map/ppermute | solution.py:416
  0.5 1.6 %collective-permute-start.1 = (bf16[16,16,256]{2,1,0:T(8,128)(2,1)}, bf16[16,16,256]{2,1,0:T(8,128)(2,1)S(1)}, u32[]{:S(2)}, u32[]{:S(2)}) collective-permute-start(bf16[16,16,256]{2,1,0:T(8,128)(2,1)} %slip_hbm.1), channel_id=1, source_target_pairs={{0,1},{1,0},{2,3},{3,2},{4,5},{5,4},{6,7},{7,6},{8,9},{9,8},{10,11... | collective-permute-start | bytes 393224 | tf_op jit(solution)/shard_map/ppermute | solution.py:416
  2.2 11.0 %collective-permute-start.6 = (bf16[128,512]{1,0:T(8,128)(2,1)S(1)}, bf16[128,512]{1,0:T(8,128)(2,1)S(1)}, u32[]{:S(2)}, u32[]{:S(2)}) collective-permute-start(bf16[128,512]{1,0:T(8,128)(2,1)S(1)} %arrange_other.1.after_ref.refs_0_), channel_id=1, source_target_pairs={{0,16},{8,24},{16,0},{24,8},{1,17},{9,25},{17,1},{25,9},{2,18},{10... | collective-permute-start | bytes 393224 | tf_op jit(solution)/shard_map/ppermute | solution.py:447
  6.8 6.4 %collective-permute-start.2 = (bf16[32,1024]{1,0:T(8,128)(2,1)S(1)}, bf16[32,1024]{1,0:T(8,128)(2,1)S(1)}, u32[]{:S(2)}, u32[]{:S(2)}) collective-permute-start(bf16[32,1024]{1,0:T(8,128)(2,1)S(1)} %get-tuple-element.23), channel_id=1, source_target_pairs={{0,2},{1,5},{2,0},{3,7},{4,6},{5,1},{6,4},{7,3},{8,10},{9,13},{10,... | collective-permute-start | bytes 196616 | tf_op jit(solution)/shard_map/ppermute | solution.py:436
  8.4 4.8 %collective-permute-start.4 = (bf16[16,1024]{1,0:T(8,128)(2,1)S(1)}, bf16[16,1024]{1,0:T(8,128)(2,1)S(1)}, u32[]{:S(2)}, u32[]{:S(2)}) collective-permute-start(bf16[16,1024]{1,0:T(8,128)(2,1)S(1)} %get-tuple-element.24), channel_id=1, source_target_pairs={{0,6},{1,7},{2,4},{3,5},{4,2},{5,3},{6,0},{7,1},{8,14},{9,15},{10,... | collective-permute-start | bytes 98312 | tf_op jit(solution)/shard_map/ppermute | solution.py:436
  9.9 7.2 %collective-permute-start.8 = (bf16[128,512]{1,0:T(8,128)(2,1)S(1)}, bf16[128,512]{1,0:T(8,128)(2,1)S(1)}, u32[]{:S(2)}, u32[]{:S(2)}) collective-permute-start(bf16[128,512]{1,0:T(8,128)(2,1)S(1)} %arrange_other.1.after_ref.refs_0_), channel_id=1, source_target_pairs={{0,8},{8,0},{16,24},{24,16},{1,9},{9,1},{17,25},{25,17},{2,10},{10... | collective-permute-start | bytes 393224 | tf_op jit(solution)/shard_map/ppermute | solution.py:447
  13.2 5.2 %collective-permute-start.7 = (bf16[128,512]{1,0:T(8,128)(2,1)S(1)}, bf16[128,512]{1,0:T(8,128)(2,1)S(1)}, u32[]{:S(2)}, u32[]{:S(2)}) collective-permute-start(bf16[128,512]{1,0:T(8,128)(2,1)S(1)} %pass_on.1.refs_2_), channel_id=1, source_target_pairs={{0,8},{8,0},{16,24},{24,16},{1,9},{9,1},{17,25},{25,17},{2,10},{10... | collective-permute-start | bytes 393224 | tf_op jit(solution)/shard_map/ppermute | solution.py:447
  14.9 1.4 %collective-permute-start.3 = (bf16[32,1024]{1,0:T(8,128)(2,1)S(1)}, bf16[32,1024]{1,0:T(8,128)(2,1)S(1)}, u32[]{:S(2)}, u32[]{:S(2)}) collective-permute-start(bf16[32,1024]{1,0:T(8,128)(2,1)S(1)} %collective-permute-done.2.refs_1_), channel_id=1, source_target_pairs={{0,1},{1,0},{2,3},{3,2},{4,5},{5,4},{6,7},{7,6},{8,9},{9,8},{10,11... | collective-permute-start | bytes 196616 | tf_op jit(solution)/shard_map/ppermute | solution.py:416
  14.9 1.4 %collective-permute-start.5 = (bf16[16,1024]{1,0:T(8,128)(2,1)S(1)}, bf16[16,1024]{1,0:T(8,128)(2,1)S(1)}, u32[]{:S(2)}, u32[]{:S(2)}) collective-permute-start(bf16[16,1024]{1,0:T(8,128)(2,1)S(1)} %collective-permute-done.4.refs_3_.refs_2_), channel_id=1, source_target_pairs={{0,1},{1,0},{2,3},{3,2},{4,5},{5,4},{6,7},{7,6},{8,9},{9,8},{10,11... | collective-permute-start | bytes 98312 | tf_op jit(solution)/shard_map/ppermute | solution.py:416
  19.2 5.1 %collective-permute-start.10 = (s16[16,1408]{1,0:T(8,128)(2,1)S(1)}, s16[16,1408]{1,0:T(8,128)(2,1)S(1)}, u32[]{:S(2)}, u32[]{:S(2)}) collective-permute-start(s16[16,1408]{1,0:T(8,128)(2,1)S(1)} %get-tuple-element.29), channel_id=1, source_target_pairs={{0,6},{1,7},{2,4},{3,5},{4,2},{5,3},{6,0},{7,1},{8,14},{9,15},{10,... | collective-permute-start | bytes 135176 | tf_op jit(solution)/shard_map/ppermute | solution.py:416
  21.2 4.0 %collective-permute-start.11 = (s16[16,1408]{1,0:T(8,128)(2,1)S(1)}, s16[16,1408]{1,0:T(8,128)(2,1)S(1)}, u32[]{:S(2)}, u32[]{:S(2)}) collective-permute-start(s16[16,1408]{1,0:T(8,128)(2,1)S(1)} %get-tuple-element.30), channel_id=1, source_target_pairs={{0,4},{1,5},{2,6},{3,7},{4,0},{5,1},{6,2},{7,3},{8,12},{9,13},{10,... | collective-permute-start | bytes 135176 | tf_op jit(solution)/shard_map/ppermute | solution.py:416
  21.8 4.0 %collective-permute-start.9 = (s16[16,1408]{1,0:T(8,128)(2,1)S(1)}, s16[16,1408]{1,0:T(8,128)(2,1)S(1)}, u32[]{:S(2)}, u32[]{:S(2)}) collective-permute-start(s16[16,1408]{1,0:T(8,128)(2,1)S(1)} %get-tuple-element.28), channel_id=1, source_target_pairs={{0,2},{1,3},{2,0},{3,1},{4,6},{5,7},{6,4},{7,5},{8,10},{9,11},{10,... | collective-permute-start | bytes 135176 | tf_op jit(solution)/shard_map/ppermute | solution.py:416

commit v6 on v5

--- a/solution.py
+++ b/solution.py
@@ -24,7 +24,7 @@
     return pltpu.CompilerParams(vmem_limit_bytes=limit)
 
 
-def arrange_half(slip_ref, out_ref, core, owner):
+def arrange_half(slip_ref, out_ref, core, owner, fetches=()):
     patches, both, samples = slip_ref.shape
     rows = both // 2
     per_reg = LANES // BLOCK
@@ -33,6 +33,8 @@
     lane_block = lax.broadcasted_iota(jnp.int32, (rows, LANES), 1) // BLOCK
     for group in range(depth // LANES):
         done = {}
+        for fetch in fetches[group * len(fetches) * LANES // depth :][: len(fetches) * LANES // depth]:
+            fetch.wait()
         for place in range(per_reg):
             full = slip_ref[group * per_reg + place].astype(jnp.float32)
             source = jnp.where(core == 0, full[:rows], full[rows:])
@@ -68,17 +70,24 @@
     sems,
 ):
     width = green_ref.shape[0]
-    fetch_slips = pltpu.make_async_copy(slip_hbm, slip_ref, sems.at[0])
-    fetch_slots = pltpu.make_async_copy(slots_hbm, slots_ref, sems.at[1])
-    fetch_greens = pltpu.make_async_copy(green_hbm, green_ref, sems.at[2])
+    parts = sems.shape[0] - 2
+    size = slip_ref.shape[0] // parts
+    fetch_slots = pltpu.make_async_copy(slots_hbm, slots_ref, sems.at[parts])
+    fetch_greens = pltpu.make_async_copy(green_hbm, green_ref, sems.at[parts + 1])
+    fetch_slips = []
+    for part in range(parts):
+        some = pl.ds(part * size, size)
+        fetch_slips.append(
+            pltpu.make_async_copy(slip_hbm.at[some], slip_ref.at[some], sems.at[part])
+        )
     fetch_slots.start()
-    fetch_slips.start()
+    for fetch in fetch_slips:
+        fetch.start()
     fetch_greens.start()
     fetch_slots.wait()
     mark_tiles(chips, per_chip, capacity, width, slots_ref, send_ref, pick_ref)
-    fetch_slips.wait()
     core = lax.rem(lax.axis_index("patch"), 2)
-    arrange_half(slip_ref, out_ref, core, core)
+    arrange_half(slip_ref, out_ref, core, core, fetch_slips)
     fetch_greens.wait()
     tiles = green_ref[...].astype(jnp.float32)
     for comp in range(green_ref.shape[1]):
@@ -113,7 +122,7 @@
             pltpu.VMEM(slips.shape, slips.dtype),
             pltpu.VMEM(slots.shape, slots.dtype),
             pltpu.VMEM(greens.shape, greens.dtype),
-            pltpu.SemaphoreType.DMA((3,)),
+            pltpu.SemaphoreType.DMA((2 * patches * BLOCK // LANES + 2,)),
         ],
         compiler_params=params(),
         name="arrange_own",
@@ -380,14 +389,32 @@
     )(shifted, slip, first, early)
 
 
+def with_sent(total, sent_refs):
+    length = total.shape[1]
+    for ref in sent_refs:
+        unit = unit_of(ref[:, length:].astype(jnp.int32)[:, :1])
+        total = total + ref[:, :length].astype(jnp.int32).astype(jnp.float32) * unit
+    return total
+
+
+def add_early_kernel(own_ref, *refs):
+    refs[-1][...] = with_sent(own_ref[...], refs[:-1])
+
+
+def add_early(own, sent):
+    return pl.pallas_call(
+        add_early_kernel,
+        out_shape=jax.ShapeDtypeStruct(own.shape, own.dtype),
+        compiler_params=params(),
+        name="add_early",
+    )(own, *sent)
+
+
 def add_kernel(own_ref, *refs):
     sent_refs, out_ref = refs[:-1], refs[-1]
     part, components, length = out_ref.shape
     rows = own_ref.shape[0] // components
-    total = own_ref[...]
-    for ref in sent_refs:
-        unit = unit_of(ref[:, length:].astype(jnp.int32)[:, :1])
-        total = total + ref[:, :length].astype(jnp.int32).astype(jnp.float32) * unit
+    total = with_sent(own_ref[...], sent_refs)
     for comp in range(components):
         out_ref[:, comp, :] = total[comp * rows : comp * rows + part]
 
@@ -456,7 +483,8 @@
     sums = convolve_last(shifted, slips[-1], first, early, rows, components)
     order = [1, chips - 1] + list(range(2, chips - 1))
     sent = [over_patch(sums[step], 2 * step) for step in order]
-    return add_up(sums[0], sent, part, components)[None]
+    early = add_early(sums[0], sent[1:][::-1])
+    return add_up(early, sent[:1], part, components)[None]
 
 
 def solution(mesh):

time: 26.8 us -> 26.8 us (level)
  no operation moved by 1% of the time
where the time goes in v6:
time: 26.8 us; the launch traced here: 26.7 us
  starting transfers between devices  14.9 us (56%)
  Pallas kernels  6.06 us (23%)
  waiting for transfers between devices  5.6 us (21%)
    ppermute x3, starting transfers between devices, local(): lax.ppermute(blocks[step - low], 'site', [(i, i ^ low) for i in range(sit...  7.32 us
    ppermute x7, starting transfers between devices, over_patch(): lax.ppermute(value, 'patch', [(i, i ^ offset) for i in range(devices)])  4.57 us
    ppermute x7, waiting for transfers between devices, over_patch(): lax.ppermute(value, 'patch', [(i, i ^ offset) for i in range(devices)])  3.85 us
    ppermute x2, starting transfers between devices, local(): lax.ppermute(pieces[1 + index], 'patch', [(i, i ^ 2 * hops[i % 2]) for i...  3.05 us
    ppermute x2, waiting for transfers between devices, local(): lax.ppermute(pieces[1 + index], 'patch', [(i, i ^ 2 * hops[i % 2]) for i...  1.75 us
    pallas_call x1, Pallas kernels, arrange_own(): pl.pallas_call(functools.partial(arrange_own_kernel, chips, per_chip, cap...  1.59 us
    pallas_call x1, Pallas kernels, convolve_first(): pl.pallas_call(functools.partial(convolve_first_kernel, rows), out_shape=...  1.38 us
    pallas_call x1, Pallas kernels, shift_tiles(): pl.pallas_call(shift_kernel, out_shape=shape, compiler_params=params(), n...  0.81 us
  transfers between devices with their start and end apart: 12, of which 5 were waited for; matrix products, arithmetic and copies ran while one was open for 0% of the time, Pallas kernels for 16%

profile of v6, /device:TPU:0, one launch (start us, length us, event | category | flops | bytes accessed | tf_op | source)
XLA Modules:
  0.0 26.7 jit_solution(13741347810576691437)
XLA Ops:
  0.0 0.5 %collective-permute-start = (bf16[32,2,1024]{2,1,0:T(2,128)(2,1)}, bf16[32,2,1024]{2,1,0:T(2,128)(2,1)S(1)}, u32[]{:S(2)}, u32[]{:S(2)}) collective-permute-start(bf16[32,2,1024]{2,1,0:T(2,128)(2,1)} %bitcast.3), channel_id=1, source_target_pairs={{0,1},{1,0},{2,3},{3,2},{4,5},{5,4},{6,7},{7,6},{8,9},{9,8},{10,11... | collective-permute-start | bytes 393224 | tf_op jit(solution)/shard_map/ppermute | solution.py:443
  0.5 0.1 collective-permute-start.1
  0.5 1.6 %arrange_own.1 = (bf16[128,512]{1,0:T(8,128)(2,1)S(1)}, bf16[64,64]{1,0:T(8,128)(2,1)S(1)}, bf16[64,32]{1,0:T(8,128)(2,1)S(1)}, bf16[64,1024]{1,0:T(8,128)(2,1)S(1)}) custom-call(bf16[16,16,256]{2,1,0:T(8,128)(2,1)} %slip_hbm.1, s32[1,128]{1,0:T(1,128)} %bitcast.5, bf16[32,2,1024]{2,1,0:T(2,128)(2,1)} %bitcast.4), custom_call_target="tpu_custom_call" | custom-call | tf_op jit(solution)/shard_map/arrange_own/pallas_call | solution.py:112
  2.1 0.0 collective-permute-done.green_ref.other_ref
  2.1 0.0 collective-permute-done.1.slip_ref
  2.1 0.2 arrange_other.1.after_ref.refs_0_
  2.3 4.1 %collective-permute-start.6 = (bf16[128,512]{1,0:T(8,128)(2,1)S(1)}, bf16[128,512]{1,0:T(8,128)(2,1)S(1)}, u32[]{:S(2)}, u32[]{:S(2)}) collective-permute-start(bf16[128,512]{1,0:T(8,128)(2,1)S(1)} %arrange_other.1.after_ref.refs_0_), channel_id=1, source_target_pairs={{0,16},{8,24},{16,0},{24,8},{1,17},{9,25},{17,1},{25,9},{2,18},{10... | collective-permute-start | bytes 393224 | tf_op jit(solution)/shard_map/ppermute | solution.py:474
  6.4 0.5 %route_tiles.1 = (bf16[32,1024]{1,0:T(8,128)(2,1)S(1)}, bf16[32,1024]{1,0:T(8,128)(2,1)S(1)}, bf16[16,1024]{1,0:T(8,128)(2,1)S(1)}) custom-call(bf16[64,64]{1,0:T(8,128)(2,1)S(1)} %get-tuple-element.19.send_ref, bf16[64,1024]{1,0:T(8,128)(2,1)S(1)} %get-tuple-element.20.own_ref, bf16[32,2,1024]{2,1,0:T(2,128)(2,1)S(1)} %collective-permute-done.green_ref.other_ref, ...), custom_call_target="tpu_custom_call" | custom-call | tf_op jit(solution)/shard_map/route_tiles/pallas_call | solution.py:223
  6.9 1.6 %collective-permute-start.2 = (bf16[32,1024]{1,0:T(8,128)(2,1)S(1)}, bf16[32,1024]{1,0:T(8,128)(2,1)S(1)}, u32[]{:S(2)}, u32[]{:S(2)}) collective-permute-start(bf16[32,1024]{1,0:T(8,128)(2,1)S(1)} %get-tuple-element.23), channel_id=1, source_target_pairs={{0,2},{1,5},{2,0},{3,7},{4,6},{5,1},{6,4},{7,3},{8,10},{9,13},{10,... | collective-permute-start | bytes 196616 | tf_op jit(solution)/shard_map/ppermute | solution.py:463
  8.5 1.5 %collective-permute-start.4 = (bf16[16,1024]{1,0:T(8,128)(2,1)S(1)}, bf16[16,1024]{1,0:T(8,128)(2,1)S(1)}, u32[]{:S(2)}, u32[]{:S(2)}) collective-permute-start(bf16[16,1024]{1,0:T(8,128)(2,1)S(1)} %get-tuple-element.24), channel_id=1, source_target_pairs={{0,6},{1,7},{2,4},{3,5},{4,2},{5,3},{6,0},{7,1},{8,14},{9,15},{10,... | collective-permute-start | bytes 98312 | tf_op jit(solution)/shard_map/ppermute | solution.py:463
  10.0 1.6 %collective-permute-start.8 = (bf16[128,512]{1,0:T(8,128)(2,1)S(1)}, bf16[128,512]{1,0:T(8,128)(2,1)S(1)}, u32[]{:S(2)}, u32[]{:S(2)}) collective-permute-start(bf16[128,512]{1,0:T(8,128)(2,1)S(1)} %arrange_other.1.after_ref.refs_0_), channel_id=1, source_target_pairs={{0,8},{8,0},{16,24},{24,16},{1,9},{9,1},{17,25},{25,17},{2,10},{10... | collective-permute-start | bytes 393224 | tf_op jit(solution)/shard_map/ppermute | solution.py:474
  11.6 1.7 %collective-permute-done.4.refs_3_.refs_2_ = bf16[16,1024]{1,0:T(8,128)(2,1)S(1)} collective-permute-done((bf16[16,1024]{1,0:T(8,128)(2,1)S(1)}, bf16[16,1024]{1,0:T(8,128)(2,1)S(1)}, u32[]{:S(2)}, u32[]{:S(2)}) %collective-permute-start.4) | collective-permute-done | bytes 32800 | tf_op jit(solution)/shard_map/ppermute | solution.py:463
  13.3 0.0 collective-permute-done.2.refs_1_
  13.3 0.0 collective-permute-done.6.refs_0_
  13.3 1.6 %collective-permute-start.7 = (bf16[128,512]{1,0:T(8,128)(2,1)S(1)}, bf16[128,512]{1,0:T(8,128)(2,1)S(1)}, u32[]{:S(2)}, u32[]{:S(2)}) collective-permute-start(bf16[128,512]{1,0:T(8,128)(2,1)S(1)} %pass_on.1.refs_2_), channel_id=1, source_target_pairs={{0,8},{8,0},{16,24},{24,16},{1,9},{9,1},{17,25},{25,17},{2,10},{10... | collective-permute-start | bytes 393224 | tf_op jit(solution)/shard_map/ppermute | solution.py:474
  15.0 0.0 collective-permute-start.3
  15.0 0.5 %collective-permute-start.5 = (bf16[16,1024]{1,0:T(8,128)(2,1)S(1)}, bf16[16,1024]{1,0:T(8,128)(2,1)S(1)}, u32[]{:S(2)}, u32[]{:S(2)}) collective-permute-start(bf16[16,1024]{1,0:T(8,128)(2,1)S(1)} %collective-permute-done.4.refs_3_.refs_2_), channel_id=1, source_target_pairs={{0,1},{1,0},{2,3},{3,2},{4,5},{5,4},{6,7},{7,6},{8,9},{9,8},{10,11... | collective-permute-start | bytes 98312 | tf_op jit(solution)/shard_map/ppermute | solution.py:443
  15.5 0.9 %collective-permute-done.5.refs_4_ = bf16[16,1024]{1,0:T(8,128)(2,1)S(1)} collective-permute-done((bf16[16,1024]{1,0:T(8,128)(2,1)S(1)}, bf16[16,1024]{1,0:T(8,128)(2,1)S(1)}, u32[]{:S(2)}, u32[]{:S(2)}) %collective-permute-start.5) | collective-permute-done | bytes 32800 | tf_op jit(solution)/shard_map/ppermute | solution.py:443
  16.3 0.0 collective-permute-done.3.refs_2_
  16.3 0.8 %shift_tiles.1.shifted_ref = bf16[512,2304]{1,0:T(8,128)(2,1)S(1)} custom-call(bf16[64,32]{1,0:T(8,128)(2,1)S(1)} %get-tuple-element.18.pick_ref, bf16[32,1024]{1,0:T(8,128)(2,1)S(1)} %get-tuple-element.22.refs_0_, bf16[32,1024]{1,0:T(8,128)(2,1)S(1)} %collective-permute-done.2.refs_1_, bf16[32,1024]{1,0:T(8,128)(2,1)S(1)} %collective-permute-done.3.refs_2_, ...), custom_call_target="tpu_custom_call" | custom-call | tf_op jit(solution)/shard_map/shift_tiles/pallas_call | solution.py:277
  17.2 0.0 collective-permute-done.8.refs_1_
  17.2 1.4 %convolve_first.1 = (f32[3,16,1280]{2,1,0:T(8,128)S(1)}, s16[3,16,1408]{2,1,0:T(8,128)(2,1)S(1)}) custom-call(bf16[512,2304]{1,0:T(8,128)(2,1)S(1)} %shift_tiles.1.shifted_ref, bf16[128,512]{1,0:T(8,128)(2,1)S(1)} %arrange_other.1.after_ref.refs_0_, bf16[128,512]{1,0:T(8,128)(2,1)S(1)} %collective-permute-done.8.refs_1_, bf16[128,512]{1,0:T(8,128)(2,1)S(1)} %pass_on.1.refs_2_), custom_call_target="tpu_custom_call" | custom-call | tf_op jit(solution)/shard_map/convolve_first/pallas_call | solution.py:346
  18.6 0.0 collective-permute-done.7.slip_ref
  18.6 0.7 %convolve_last.1 = (f32[16,1280]{1,0:T(8,128)S(1)}, s16[16,1408]{1,0:T(8,128)(2,1)S(1)}, s16[16,1408]{1,0:T(8,128)(2,1)S(1)}, s16[16,1408]{1,0:T(8,128)(2,1)S(1)}) custom-call(bf16[512,2304]{1,0:T(8,128)(2,1)S(1)} %shift_tiles.1.shifted_ref, bf16[128,512]{1,0:T(8,128)(2,1)S(1)} %collective-permute-done.7.slip_ref, ...), custom_call_target="tpu_custom_call" | custom-call | tf_op jit(solution)/shard_map/convolve_last/pallas_call | solution.py:382
  19.3 2.0 %collective-permute-start.10 = (s16[16,1408]{1,0:T(8,128)(2,1)S(1)}, s16[16,1408]{1,0:T(8,128)(2,1)S(1)}, u32[]{:S(2)}, u32[]{:S(2)}) collective-permute-start(s16[16,1408]{1,0:T(8,128)(2,1)S(1)} %get-tuple-element.29), channel_id=1, source_target_pairs={{0,6},{1,7},{2,4},{3,5},{4,2},{5,3},{6,0},{7,1},{8,14},{9,15},{10,... | collective-permute-start | bytes 135176 | tf_op jit(solution)/shard_map/ppermute | solution.py:443
  21.3 0.6 %collective-permute-start.9 = (s16[16,1408]{1,0:T(8,128)(2,1)S(1)}, s16[16,1408]{1,0:T(8,128)(2,1)S(1)}, u32[]{:S(2)}, u32[]{:S(2)}) collective-permute-start(s16[16,1408]{1,0:T(8,128)(2,1)S(1)} %get-tuple-element.28), channel_id=1, source_target_pairs={{0,4},{1,5},{2,6},{3,7},{4,0},{5,1},{6,2},{7,3},{8,12},{9,13},{10,... | collective-permute-start | bytes 135176 | tf_op jit(solution)/shard_map/ppermute | solution.py:443
  21.9 1.0 %collective-permute-start.11 = (s16[16,1408]{1,0:T(8,128)(2,1)S(1)}, s16[16,1408]{1,0:T(8,128)(2,1)S(1)}, u32[]{:S(2)}, u32[]{:S(2)}) collective-permute-start(s16[16,1408]{1,0:T(8,128)(2,1)S(1)} %get-tuple-element.30), channel_id=1, source_target_pairs={{0,2},{1,3},{2,0},{3,1},{4,6},{5,7},{6,4},{7,5},{8,10},{9,11},{10,... | collective-permute-start | bytes 135176 | tf_op jit(solution)/shard_map/ppermute | solution.py:443
  22.9 1.5 %collective-permute-done.10.refs_1_ = s16[16,1408]{1,0:T(8,128)(2,1)S(1)} collective-permute-done((s16[16,1408]{1,0:T(8,128)(2,1)S(1)}, s16[16,1408]{1,0:T(8,128)(2,1)S(1)}, u32[]{:S(2)}, u32[]{:S(2)}) %collective-permute-start.10) | collective-permute-done | bytes 45088 | tf_op jit(solution)/shard_map/ppermute | solution.py:443
  24.4 1.0 %collective-permute-done.9.refs_0_ = s16[16,1408]{1,0:T(8,128)(2,1)S(1)} collective-permute-done((s16[16,1408]{1,0:T(8,128)(2,1)S(1)}, s16[16,1408]{1,0:T(8,128)(2,1)S(1)}, u32[]{:S(2)}, u32[]{:S(2)}) %collective-permute-start.9) | collective-permute-done | bytes 45088 | tf_op jit(solution)/shard_map/ppermute | solution.py:443
  25.3 0.1 add_early.1.own_ref
  25.4 0.5 %collective-permute-done.11.refs_0_ = s16[16,1408]{1,0:T(8,128)(2,1)S(1)} collective-permute-done((s16[16,1408]{1,0:T(8,128)(2,1)S(1)}, s16[16,1408]{1,0:T(8,128)(2,1)S(1)}, u32[]{:S(2)}, u32[]{:S(2)}) %collective-permute-start.11) | collective-permute-done | bytes 45088 | tf_op jit(solution)/shard_map/ppermute | solution.py:443
  25.9 0.7 %add_up.1 = f32[8,2,1280]{2,1,0:T(2,128)} custom-call(f32[16,1280]{1,0:T(8,128)S(1)} %add_early.1.own_ref, s16[16,1408]{1,0:T(8,128)(2,1)S(1)} %collective-permute-done.11.refs_0_), custom_call_target="tpu_custom_call" | custom-call | tf_op jit(solution)/shard_map/add_up/pallas_call | solution.py:423
  (1 shorter events, 0.0 us)
Async XLA Ops:
  0.0 2.1 %collective-permute-start = (bf16[32,2,1024]{2,1,0:T(2,128)(2,1)}, bf16[32,2,1024]{2,1,0:T(2,128)(2,1)S(1)}, u32[]{:S(2)}, u32[]{:S(2)}) collective-permute-start(bf16[32,2,1024]{2,1,0:T(2,128)(2,1)} %bitcast.3), channel_id=1, source_target_pairs={{0,1},{1,0},{2,3},{3,2},{4,5},{5,4},{6,7},{7,6},{8,9},{9,8},{10,11... | collective-permute-start | bytes 393224 | tf_op jit(solution)/shard_map/ppermute | solution.py:443
  0.5 1.7 %collective-permute-start.1 = (bf16[16,16,256]{2,1,0:T(8,128)(2,1)}, bf16[16,16,256]{2,1,0:T(8,128)(2,1)S(1)}, u32[]{:S(2)}, u32[]{:S(2)}) collective-permute-start(bf16[16,16,256]{2,1,0:T(8,128)(2,1)} %slip_hbm.1), channel_id=1, source_target_pairs={{0,1},{1,0},{2,3},{3,2},{4,5},{5,4},{6,7},{7,6},{8,9},{9,8},{10,11... | collective-permute-start | bytes 393224 | tf_op jit(solution)/shard_map/ppermute | solution.py:443
  2.3 11.0 %collective-permute-start.6 = (bf16[128,512]{1,0:T(8,128)(2,1)S(1)}, bf16[128,512]{1,0:T(8,128)(2,1)S(1)}, u32[]{:S(2)}, u32[]{:S(2)}) collective-permute-start(bf16[128,512]{1,0:T(8,128)(2,1)S(1)} %arrange_other.1.after_ref.refs_0_), channel_id=1, source_target_pairs={{0,16},{8,24},{16,0},{24,8},{1,17},{9,25},{17,1},{25,9},{2,18},{10... | collective-permute-start | bytes 393224 | tf_op jit(solution)/shard_map/ppermute | solution.py:474
  6.9 6.4 %collective-permute-start.2 = (bf16[32,1024]{1,0:T(8,128)(2,1)S(1)}, bf16[32,1024]{1,0:T(8,128)(2,1)S(1)}, u32[]{:S(2)}, u32[]{:S(2)}) collective-permute-start(bf16[32,1024]{1,0:T(8,128)(2,1)S(1)} %get-tuple-element.23), channel_id=1, source_target_pairs={{0,2},{1,5},{2,0},{3,7},{4,6},{5,1},{6,4},{7,3},{8,10},{9,13},{10,... | collective-permute-start | bytes 196616 | tf_op jit(solution)/shard_map/ppermute | solution.py:463
  8.5 4.8 %collective-permute-start.4 = (bf16[16,1024]{1,0:T(8,128)(2,1)S(1)}, bf16[16,1024]{1,0:T(8,128)(2,1)S(1)}, u32[]{:S(2)}, u32[]{:S(2)}) collective-permute-start(bf16[16,1024]{1,0:T(8,128)(2,1)S(1)} %get-tuple-element.24), channel_id=1, source_target_pairs={{0,6},{1,7},{2,4},{3,5},{4,2},{5,3},{6,0},{7,1},{8,14},{9,15},{10,... | collective-permute-start | bytes 98312 | tf_op jit(solution)/shard_map/ppermute | solution.py:463
  10.0 7.2 %collective-permute-start.8 = (bf16[128,512]{1,0:T(8,128)(2,1)S(1)}, bf16[128,512]{1,0:T(8,128)(2,1)S(1)}, u32[]{:S(2)}, u32[]{:S(2)}) collective-permute-start(bf16[128,512]{1,0:T(8,128)(2,1)S(1)} %arrange_other.1.after_ref.refs_0_), channel_id=1, source_target_pairs={{0,8},{8,0},{16,24},{24,16},{1,9},{9,1},{17,25},{25,17},{2,10},{10... | collective-permute-start | bytes 393224 | tf_op jit(solution)/shard_map/ppermute | solution.py:474
  13.3 5.2 %collective-permute-start.7 = (bf16[128,512]{1,0:T(8,128)(2,1)S(1)}, bf16[128,512]{1,0:T(8,128)(2,1)S(1)}, u32[]{:S(2)}, u32[]{:S(2)}) collective-permute-start(bf16[128,512]{1,0:T(8,128)(2,1)S(1)} %pass_on.1.refs_2_), channel_id=1, source_target_pairs={{0,8},{8,0},{16,24},{24,16},{1,9},{9,1},{17,25},{25,17},{2,10},{10... | collective-permute-start | bytes 393224 | tf_op jit(solution)/shard_map/ppermute | solution.py:474
  15.0 1.4 %collective-permute-start.3 = (bf16[32,1024]{1,0:T(8,128)(2,1)S(1)}, bf16[32,1024]{1,0:T(8,128)(2,1)S(1)}, u32[]{:S(2)}, u32[]{:S(2)}) collective-permute-start(bf16[32,1024]{1,0:T(8,128)(2,1)S(1)} %collective-permute-done.2.refs_1_), channel_id=1, source_target_pairs={{0,1},{1,0},{2,3},{3,2},{4,5},{5,4},{6,7},{7,6},{8,9},{9,8},{10,11... | collective-permute-start | bytes 196616 | tf_op jit(solution)/shard_map/ppermute | solution.py:443
  15.0 1.4 %collective-permute-start.5 = (bf16[16,1024]{1,0:T(8,128)(2,1)S(1)}, bf16[16,1024]{1,0:T(8,128)(2,1)S(1)}, u32[]{:S(2)}, u32[]{:S(2)}) collective-permute-start(bf16[16,1024]{1,0:T(8,128)(2,1)S(1)} %collective-permute-done.4.refs_3_.refs_2_), channel_id=1, source_target_pairs={{0,1},{1,0},{2,3},{3,2},{4,5},{5,4},{6,7},{7,6},{8,9},{9,8},{10,11... | collective-permute-start | bytes 98312 | tf_op jit(solution)/shard_map/ppermute | solution.py:443
  19.3 5.1 %collective-permute-start.10 = (s16[16,1408]{1,0:T(8,128)(2,1)S(1)}, s16[16,1408]{1,0:T(8,128)(2,1)S(1)}, u32[]{:S(2)}, u32[]{:S(2)}) collective-permute-start(s16[16,1408]{1,0:T(8,128)(2,1)S(1)} %get-tuple-element.29), channel_id=1, source_target_pairs={{0,6},{1,7},{2,4},{3,5},{4,2},{5,3},{6,0},{7,1},{8,14},{9,15},{10,... | collective-permute-start | bytes 135176 | tf_op jit(solution)/shard_map/ppermute | solution.py:443
  21.3 4.0 %collective-permute-start.9 = (s16[16,1408]{1,0:T(8,128)(2,1)S(1)}, s16[16,1408]{1,0:T(8,128)(2,1)S(1)}, u32[]{:S(2)}, u32[]{:S(2)}) collective-permute-start(s16[16,1408]{1,0:T(8,128)(2,1)S(1)} %get-tuple-element.28), channel_id=1, source_target_pairs={{0,4},{1,5},{2,6},{3,7},{4,0},{5,1},{6,2},{7,3},{8,12},{9,13},{10,... | collective-permute-start | bytes 135176 | tf_op jit(solution)/shard_map/ppermute | solution.py:443
  21.9 4.0 %collective-permute-start.11 = (s16[16,1408]{1,0:T(8,128)(2,1)S(1)}, s16[16,1408]{1,0:T(8,128)(2,1)S(1)}, u32[]{:S(2)}, u32[]{:S(2)}) collective-permute-start(s16[16,1408]{1,0:T(8,128)(2,1)S(1)} %get-tuple-element.30), channel_id=1, source_target_pairs={{0,2},{1,3},{2,0},{3,1},{4,6},{5,7},{6,4},{7,5},{8,10},{9,11},{10,... | collective-permute-start | bytes 135176 | tf_op jit(solution)/shard_map/ppermute | solution.py:443

commit v7 on v5

--- a/solution.py
+++ b/solution.py
@@ -146,7 +146,6 @@
 
 
 def mark_tiles(chips, per_chip, capacity, width, slots_ref, send_ref, pick_ref):
-    half = capacity // 2
     count = slots_ref.shape[1]
     own = lax.axis_index("patch")
     chip, core = own // 2, lax.rem(own, 2)
@@ -171,20 +170,14 @@
         one_hot(marks), earlier_in_chip(per_chip, per_chip), preferred_element_type=jnp.float32
     )
     rank = jnp.sum(jnp.where(marks, rank, 0.0), axis=0, keepdims=True).astype(jnp.int32)
-    from_other = jnp.where(owner == chips - 1, rank // half, 1 - owner % 2) != core
-    base = (owner - jnp.where(owner == chips - 1, 0, 1 - owner % 2)) * capacity
-    code = base + jnp.where(
-        owner == chips - 1,
-        jnp.where(from_other, half, 0) + rank % half,
-        jnp.where(from_other, capacity, 0) + rank,
-    )
-    code = jnp.where(owner == 0, rank, code)
+    other = (owner > 0) & (owner < chips - 1) & (1 - owner % 2 != core)
+    base = owner - jnp.where((owner > 0) & (owner < chips - 1), 1 - owner % 2, 0)
+    code = (base + jnp.where(other, 1, 0)) * capacity + rank
     pick_ref[...] = one_hot(lax.broadcasted_iota(jnp.int32, pick_ref.shape, 0) == code)
 
 
 def route_kernel(chips, send_ref, own_ref, other_ref, after_ref, *out_refs):
     capacity = send_ref.shape[0] // chips
-    half = capacity // 2
     core = lax.rem(lax.axis_index("patch"), 2)
     width, components, _ = other_ref.shape
     tiles = other_ref[...].astype(jnp.float32)
@@ -196,11 +189,10 @@
         )
         chosen = jnp.dot(send_ref[...], both, preferred_element_type=jnp.float32)
         chosen = [chosen[step * capacity : (step + 1) * capacity] for step in range(chips)]
-        last = chosen[-1]
         sent = [chosen[0]]
         for step in range(1, chips - 1, 2):
             sent.append(jnp.where(core == 0, chosen[step], chosen[step + 1]))
-        sent.append(jnp.where(core == 0, last[:half], last[half:]))
+        sent.append(chosen[-1])
         by_comp.append(sent)
     for values, out_ref in zip(zip(*by_comp), out_refs):
         out_ref[...] = jnp.concatenate(values, axis=0).astype(jnp.bfloat16)
@@ -210,12 +202,11 @@
     components, lags = other.shape[1:]
     rows = components * send.shape[0] // chips
     shape = jax.ShapeDtypeStruct((rows, lags), jnp.bfloat16)
-    part = jax.ShapeDtypeStruct((rows // 2, lags), jnp.bfloat16)
     return pl.pallas_call(
         functools.partial(route_kernel, chips),
         in_specs=[pl.BlockSpec(memory_space=pltpu.VMEM)] * 3
         + [pl.BlockSpec(memory_space=pl.ANY)],
-        out_shape=(shape,) * (chips // 2) + (part,),
+        out_shape=(shape,) * (1 + chips // 2),
         compiler_params=params(),
         name="route_tiles",
     )(send, own, other, after)
@@ -239,16 +230,15 @@
 def shift_kernel(pick_ref, *refs):
     pieces, out_ref = refs[:-1], refs[-1]
     count = pick_ref.shape[1]
-    components = sum(piece.shape[0] for piece in pieces) // pick_ref.shape[0]
+    capacity = pick_ref.shape[0] // len(pieces)
+    components = pieces[0].shape[0] // capacity
     lags = pieces[0].shape[1]
     span = out_ref.shape[1] // components
     tail = jnp.zeros((BLOCK, span - lags), jnp.float32)
     for comp in range(components):
-        arrived = []
-        for piece in pieces:
-            size = piece.shape[0] // components
-            arrived.append(piece[...].astype(jnp.float32)[comp * size : (comp + 1) * size])
-        arrived = jnp.concatenate(arrived, axis=0).astype(jnp.bfloat16)
+        arrived = jnp.concatenate(
+            [piece[comp * capacity : (comp + 1) * capacity, :] for piece in pieces], axis=0
+        )
         tiles = lax.dot_general(
             pick_ref[...], arrived, (((0,), (0,)), ((), ())), preferred_element_type=jnp.float32
         )
@@ -437,8 +427,9 @@
             pieces[1 + index], "patch", [(i, i ^ (2 * hops[i % 2])) for i in range(devices)]
         )
     pieces = pieces[:1]
-    for piece in arrived:
+    for piece in arrived[:-1]:
         pieces += [piece, over_patch(piece, 1)]
+    pieces.append(arrived[-1])
 
     blocks = {0: block}
     for step in [2**i for i in range(sites.bit_length())] + list(range(sites)):
@@ -448,13 +439,13 @@
                 blocks[step - low], "site", [(i, i ^ low) for i in range(sites)]
             )
             if step == sites // 2:
-                blocks[step] = pass_on(blocks[step], *arrived)
+                blocks[step] = pass_on(pass_on(pass_on(blocks[step], arrived[-1]), arrived[-1]), *arrived)
     shifted = shift_tiles(pick, pieces, components)
 
     slips = [blocks[step] for step in range(sites)]
     first, early = convolve_first(shifted, slips[:-1], rows, components, length)
     sums = convolve_last(shifted, slips[-1], first, early, rows, components)
-    order = [1, chips - 1] + list(range(2, chips - 1))
+    order = list(range(1, chips))
     sent = [over_patch(sums[step], 2 * step) for step in order]
     return add_up(sums[0], sent, part, components)[None]
 

time: 26.8 us -> 27.2 us (1.015)
  waiting for transfers between devices: 5.73 us -> 6.78 us
  starting transfers between devices: 14.9 us -> 14.4 us
    ppermute x3, waiting for transfers between devices: 0.02 us -> 0.82 us  [local(): lax.ppermute(blocks[step - low], 'site', [(i, i ^ low) for i in range(sit...]
    ppermute x7 -> x6, waiting for transfers between devices: 3.96 us -> 4.62 us  [over_patch(): lax.ppermute(value, 'patch', [(i, i ^ offset) for i in range(devices)])]
    ppermute x7 -> x6, starting transfers between devices: 4.57 us -> 4.07 us  [over_patch(): lax.ppermute(value, 'patch', [(i, i ^ offset) for i in range(devices)])]
    ppermute x2, waiting for transfers between devices: 1.75 us -> 1.34 us  [local(): lax.ppermute(pieces[1 + index], 'patch', [(i, i ^ 2 * hops[i % 2]) for i...]
  transfers between devices with their start and end apart: 12 -> 11, of which waited for: 5 -> 7; matrix products, arithmetic and copies ran while one was open for 0% -> 0% of each run, Pallas kernels for 16% -> 15%
where the time goes in v7:
time: 27.2 us; the launch traced here: 27.1 us
  starting transfers between devices  14.4 us (53%)
  waiting for transfers between devices  6.78 us (25%)
  Pallas kernels  5.87 us (22%)
    ppermute x3, starting transfers between devices, local(): lax.ppermute(blocks[step - low], 'site', [(i, i ^ low) for i in range(sit...  7.25 us
    ppermute x6, waiting for transfers between devices, over_patch(): lax.ppermute(value, 'patch', [(i, i ^ offset) for i in range(devices)])  4.62 us
    ppermute x6, starting transfers between devices, over_patch(): lax.ppermute(value, 'patch', [(i, i ^ offset) for i in range(devices)])  4.07 us
    ppermute x2, starting transfers between devices, local(): lax.ppermute(pieces[1 + index], 'patch', [(i, i ^ 2 * hops[i % 2]) for i...  3.05 us
    pallas_call x1, Pallas kernels, arrange_own(): pl.pallas_call(functools.partial(arrange_own_kernel, chips, per_chip, cap...  1.48 us
    pallas_call x1, Pallas kernels, convolve_first(): pl.pallas_call(functools.partial(convolve_first_kernel, rows), out_shape=...  1.38 us
    ppermute x2, waiting for transfers between devices, local(): lax.ppermute(pieces[1 + index], 'patch', [(i, i ^ 2 * hops[i % 2]) for i...  1.34 us
    ppermute x3, waiting for transfers between devices, local(): lax.ppermute(blocks[step - low], 'site', [(i, i ^ low) for i in range(sit...  0.82 us
  transfers between devices with their start and end apart: 11, of which 7 were waited for; matrix products, arithmetic and copies ran while one was open for 0% of the time, Pallas kernels for 15%

profile of v7, /device:TPU:0, one launch (start us, length us, event | category | flops | bytes accessed | tf_op | source)
XLA Modules:
  0.0 27.1 jit_solution(12058134529882203539)
XLA Ops:
  0.0 0.5 %collective-permute-start = (bf16[32,2,1024]{2,1,0:T(2,128)(2,1)}, bf16[32,2,1024]{2,1,0:T(2,128)(2,1)S(1)}, u32[]{:S(2)}, u32[]{:S(2)}) collective-permute-start(bf16[32,2,1024]{2,1,0:T(2,128)(2,1)} %bitcast.3), channel_id=1, source_target_pairs={{0,1},{1,0},{2,3},{3,2},{4,5},{5,4},{6,7},{7,6},{8,9},{9,8},{10,11... | collective-permute-start | bytes 393224 | tf_op jit(solution)/shard_map/ppermute | solution.py:406
  0.5 0.1 collective-permute-start.1
  0.5 1.5 %arrange_own.1 = (bf16[128,512]{1,0:T(8,128)(2,1)S(1)}, bf16[64,64]{1,0:T(8,128)(2,1)S(1)}, bf16[64,32]{1,0:T(8,128)(2,1)S(1)}, bf16[64,1024]{1,0:T(8,128)(2,1)S(1)}) custom-call(bf16[16,16,256]{2,1,0:T(8,128)(2,1)} %slip_hbm.1, s32[1,128]{1,0:T(1,128)} %bitcast.5, bf16[32,2,1024]{2,1,0:T(2,128)(2,1)} %bitcast.4), custom_call_target="tpu_custom_call" | custom-call | tf_op jit(solution)/shard_map/arrange_own/pallas_call | solution.py:103
  2.0 0.0 collective-permute-done.green_ref.other_ref
  2.0 0.0 collective-permute-done.1.slip_ref
  2.0 0.2 arrange_other.1.after_ref.refs_0_
  2.2 4.1 %collective-permute-start.5 = (bf16[128,512]{1,0:T(8,128)(2,1)S(1)}, bf16[128,512]{1,0:T(8,128)(2,1)S(1)}, u32[]{:S(2)}, u32[]{:S(2)}) collective-permute-start(bf16[128,512]{1,0:T(8,128)(2,1)S(1)} %arrange_other.1.after_ref.refs_0_), channel_id=1, source_target_pairs={{0,16},{8,24},{16,0},{24,8},{1,17},{9,25},{17,1},{25,9},{2,18},{10... | collective-permute-start | bytes 393224 | tf_op jit(solution)/shard_map/ppermute | solution.py:438
  6.3 0.5 %route_tiles.1 = (bf16[32,1024]{1,0:T(8,128)(2,1)S(1)}, bf16[32,1024]{1,0:T(8,128)(2,1)S(1)}, bf16[32,1024]{1,0:T(8,128)(2,1)S(1)}) custom-call(bf16[64,64]{1,0:T(8,128)(2,1)S(1)} %get-tuple-element.19.send_ref, bf16[64,1024]{1,0:T(8,128)(2,1)S(1)} %get-tuple-element.20.own_ref, bf16[32,2,1024]{2,1,0:T(2,128)(2,1)S(1)} %collective-permute-done.green_ref.other_ref, ...), custom_call_target="tpu_custom_call" | custom-call | tf_op jit(solution)/shard_map/route_tiles/pallas_call | solution.py:205
  6.8 2.5 %collective-permute-start.4 = (bf16[32,1024]{1,0:T(8,128)(2,1)S(1)}, bf16[32,1024]{1,0:T(8,128)(2,1)S(1)}, u32[]{:S(2)}, u32[]{:S(2)}) collective-permute-start(bf16[32,1024]{1,0:T(8,128)(2,1)S(1)} %get-tuple-element.24), channel_id=1, source_target_pairs={{0,6},{1,7},{2,4},{3,5},{4,2},{5,3},{6,0},{7,1},{8,14},{9,15},{10,... | collective-permute-start | bytes 196616 | tf_op jit(solution)/shard_map/ppermute | solution.py:426
  9.3 0.5 %collective-permute-start.2 = (bf16[32,1024]{1,0:T(8,128)(2,1)S(1)}, bf16[32,1024]{1,0:T(8,128)(2,1)S(1)}, u32[]{:S(2)}, u32[]{:S(2)}) collective-permute-start(bf16[32,1024]{1,0:T(8,128)(2,1)S(1)} %get-tuple-element.23), channel_id=1, source_target_pairs={{0,2},{1,5},{2,0},{3,7},{4,6},{5,1},{6,4},{7,3},{8,10},{9,13},{10,... | collective-permute-start | bytes 196616 | tf_op jit(solution)/shard_map/ppermute | solution.py:426
  9.9 1.6 %collective-permute-start.7 = (bf16[128,512]{1,0:T(8,128)(2,1)S(1)}, bf16[128,512]{1,0:T(8,128)(2,1)S(1)}, u32[]{:S(2)}, u32[]{:S(2)}) collective-permute-start(bf16[128,512]{1,0:T(8,128)(2,1)S(1)} %arrange_other.1.after_ref.refs_0_), channel_id=1, source_target_pairs={{0,8},{8,0},{16,24},{24,16},{1,9},{9,1},{17,25},{25,17},{2,10},{10... | collective-permute-start | bytes 393224 | tf_op jit(solution)/shard_map/ppermute | solution.py:438
  11.5 0.7 %collective-permute-done.4.refs_3_.refs_1_.refs_2_ = bf16[32,1024]{1,0:T(8,128)(2,1)S(1)} collective-permute-done((bf16[32,1024]{1,0:T(8,128)(2,1)S(1)}, bf16[32,1024]{1,0:T(8,128)(2,1)S(1)}, u32[]{:S(2)}, u32[]{:S(2)}) %collective-permute-start.4) | collective-permute-done | bytes 65568 | tf_op jit(solution)/shard_map/ppermute | solution.py:426
  12.1 0.8 %collective-permute-done.5.refs_0_ = bf16[128,512]{1,0:T(8,128)(2,1)S(1)} collective-permute-done((bf16[128,512]{1,0:T(8,128)(2,1)S(1)}, bf16[128,512]{1,0:T(8,128)(2,1)S(1)}, u32[]{:S(2)}, u32[]{:S(2)}) %collective-permute-start.5) | collective-permute-done | bytes 131104 | tf_op jit(solution)/shard_map/ppermute | solution.py:438
  12.9 0.7 %collective-permute-done.2.refs_1_ = bf16[32,1024]{1,0:T(8,128)(2,1)S(1)} collective-permute-done((bf16[32,1024]{1,0:T(8,128)(2,1)S(1)}, bf16[32,1024]{1,0:T(8,128)(2,1)S(1)}, u32[]{:S(2)}, u32[]{:S(2)}) %collective-permute-start.2) | collective-permute-done | bytes 65568 | tf_op jit(solution)/shard_map/ppermute | solution.py:426
  13.6 1.6 %collective-permute-start.6 = (bf16[128,512]{1,0:T(8,128)(2,1)S(1)}, bf16[128,512]{1,0:T(8,128)(2,1)S(1)}, u32[]{:S(2)}, u32[]{:S(2)}) collective-permute-start(bf16[128,512]{1,0:T(8,128)(2,1)S(1)} %pass_on.5.refs_2_), channel_id=1, source_target_pairs={{0,8},{8,0},{16,24},{24,16},{1,9},{9,1},{17,25},{25,17},{2,10},{10... | collective-permute-start | bytes 393224 | tf_op jit(solution)/shard_map/ppermute | solution.py:438
  15.2 0.0 collective-permute-start.3
  15.2 1.3 %collective-permute-done.3.refs_2_ = bf16[32,1024]{1,0:T(8,128)(2,1)S(1)} collective-permute-done((bf16[32,1024]{1,0:T(8,128)(2,1)S(1)}, bf16[32,1024]{1,0:T(8,128)(2,1)S(1)}, u32[]{:S(2)}, u32[]{:S(2)}) %collective-permute-start.3) | collective-permute-done | bytes 65568 | tf_op jit(solution)/shard_map/ppermute | solution.py:406
  16.4 0.8 %shift_tiles.1.shifted_ref = bf16[512,2304]{1,0:T(8,128)(2,1)S(1)} custom-call(bf16[64,32]{1,0:T(8,128)(2,1)S(1)} %get-tuple-element.18.pick_ref, bf16[32,1024]{1,0:T(8,128)(2,1)S(1)} %get-tuple-element.22.refs_0_, bf16[32,1024]{1,0:T(8,128)(2,1)S(1)} %collective-permute-done.2.refs_1_, bf16[32,1024]{1,0:T(8,128)(2,1)S(1)} %collective-permute-done.3.refs_2_, ...), custom_call_target="tpu_custom_call" | custom-call | tf_op jit(solution)/shard_map/shift_tiles/pallas_call | solution.py:258
  17.3 0.0 collective-permute-done.7.refs_1_
  17.3 1.4 %convolve_first.1 = (f32[3,16,1280]{2,1,0:T(8,128)S(1)}, s16[3,16,1408]{2,1,0:T(8,128)(2,1)S(1)}) custom-call(bf16[512,2304]{1,0:T(8,128)(2,1)S(1)} %shift_tiles.1.shifted_ref, bf16[128,512]{1,0:T(8,128)(2,1)S(1)} %arrange_other.1.after_ref.refs_0_, bf16[128,512]{1,0:T(8,128)(2,1)S(1)} %collective-permute-done.7.refs_1_, bf16[128,512]{1,0:T(8,128)(2,1)S(1)} %pass_on.5.refs_2_), custom_call_target="tpu_custom_call" | custom-call | tf_op jit(solution)/shard_map/convolve_first/pallas_call | solution.py:327
  18.7 0.0 collective-permute-done.6.slip_ref
  18.7 0.7 %convolve_last.1 = (f32[16,1280]{1,0:T(8,128)S(1)}, s16[16,1408]{1,0:T(8,128)(2,1)S(1)}, s16[16,1408]{1,0:T(8,128)(2,1)S(1)}, s16[16,1408]{1,0:T(8,128)(2,1)S(1)}) custom-call(bf16[512,2304]{1,0:T(8,128)(2,1)S(1)} %shift_tiles.1.shifted_ref, bf16[128,512]{1,0:T(8,128)(2,1)S(1)} %collective-permute-done.6.slip_ref, ...), custom_call_target="tpu_custom_call" | custom-call | tf_op jit(solution)/shard_map/convolve_last/pallas_call | solution.py:363
  19.4 1.8 %collective-permute-start.10 = (s16[16,1408]{1,0:T(8,128)(2,1)S(1)}, s16[16,1408]{1,0:T(8,128)(2,1)S(1)}, u32[]{:S(2)}, u32[]{:S(2)}) collective-permute-start(s16[16,1408]{1,0:T(8,128)(2,1)S(1)} %get-tuple-element.30), channel_id=1, source_target_pairs={{0,6},{1,7},{2,4},{3,5},{4,2},{5,3},{6,0},{7,1},{8,14},{9,15},{10,... | collective-permute-start | bytes 135176 | tf_op jit(solution)/shard_map/ppermute | solution.py:406
  21.2 1.1 %collective-permute-start.8 = (s16[16,1408]{1,0:T(8,128)(2,1)S(1)}, s16[16,1408]{1,0:T(8,128)(2,1)S(1)}, u32[]{:S(2)}, u32[]{:S(2)}) collective-permute-start(s16[16,1408]{1,0:T(8,128)(2,1)S(1)} %get-tuple-element.28), channel_id=1, source_target_pairs={{0,2},{1,3},{2,0},{3,1},{4,6},{5,7},{6,4},{7,5},{8,10},{9,11},{10,... | collective-permute-start | bytes 135176 | tf_op jit(solution)/shard_map/ppermute | solution.py:406
  22.3 0.7 %collective-permute-start.9 = (s16[16,1408]{1,0:T(8,128)(2,1)S(1)}, s16[16,1408]{1,0:T(8,128)(2,1)S(1)}, u32[]{:S(2)}, u32[]{:S(2)}) collective-permute-start(s16[16,1408]{1,0:T(8,128)(2,1)S(1)} %get-tuple-element.29), channel_id=1, source_target_pairs={{0,4},{1,5},{2,6},{3,7},{4,0},{5,1},{6,2},{7,3},{8,12},{9,13},{10,... | collective-permute-start | bytes 135176 | tf_op jit(solution)/shard_map/ppermute | solution.py:406
  23.0 1.6 %collective-permute-done.10.refs_2_ = s16[16,1408]{1,0:T(8,128)(2,1)S(1)} collective-permute-done((s16[16,1408]{1,0:T(8,128)(2,1)S(1)}, s16[16,1408]{1,0:T(8,128)(2,1)S(1)}, u32[]{:S(2)}, u32[]{:S(2)}) %collective-permute-start.10) | collective-permute-done | bytes 45088 | tf_op jit(solution)/shard_map/ppermute | solution.py:406
  24.6 0.7 %collective-permute-done.8.refs_0_ = s16[16,1408]{1,0:T(8,128)(2,1)S(1)} collective-permute-done((s16[16,1408]{1,0:T(8,128)(2,1)S(1)}, s16[16,1408]{1,0:T(8,128)(2,1)S(1)}, u32[]{:S(2)}, u32[]{:S(2)}) %collective-permute-start.8) | collective-permute-done | bytes 45088 | tf_op jit(solution)/shard_map/ppermute | solution.py:406
  25.3 1.1 %collective-permute-done.9.refs_1_ = s16[16,1408]{1,0:T(8,128)(2,1)S(1)} collective-permute-done((s16[16,1408]{1,0:T(8,128)(2,1)S(1)}, s16[16,1408]{1,0:T(8,128)(2,1)S(1)}, u32[]{:S(2)}, u32[]{:S(2)}) %collective-permute-start.9) | collective-permute-done | bytes 45088 | tf_op jit(solution)/shard_map/ppermute | solution.py:406
  26.4 0.7 %add_up.1 = f32[8,2,1280]{2,1,0:T(2,128)} custom-call(f32[16,1280]{1,0:T(8,128)S(1)} %get-tuple-element.27.own_ref, s16[16,1408]{1,0:T(8,128)(2,1)S(1)} %collective-permute-done.8.refs_0_, s16[16,1408]{1,0:T(8,128)(2,1)S(1)} %collective-permute-done.9.refs_1_, s16[16,1408]{1,0:T(8,128)(2,1)S(1)} %collective-permute-done.10.refs_2_), custom_call_target="tpu_custom_call" | custom-call | tf_op jit(solution)/shard_map/add_up/pallas_call | solution.py:386
  (3 shorter events, 0.0 us)
Async XLA Ops:
  0.0 2.0 %collective-permute-start = (bf16[32,2,1024]{2,1,0:T(2,128)(2,1)}, bf16[32,2,1024]{2,1,0:T(2,128)(2,1)S(1)}, u32[]{:S(2)}, u32[]{:S(2)}) collective-permute-start(bf16[32,2,1024]{2,1,0:T(2,128)(2,1)} %bitcast.3), channel_id=1, source_target_pairs={{0,1},{1,0},{2,3},{3,2},{4,5},{5,4},{6,7},{7,6},{8,9},{9,8},{10,11... | collective-permute-start | bytes 393224 | tf_op jit(solution)/shard_map/ppermute | solution.py:406
  0.5 1.6 %collective-permute-start.1 = (bf16[16,16,256]{2,1,0:T(8,128)(2,1)}, bf16[16,16,256]{2,1,0:T(8,128)(2,1)S(1)}, u32[]{:S(2)}, u32[]{:S(2)}) collective-permute-start(bf16[16,16,256]{2,1,0:T(8,128)(2,1)} %slip_hbm.1), channel_id=1, source_target_pairs={{0,1},{1,0},{2,3},{3,2},{4,5},{5,4},{6,7},{7,6},{8,9},{9,8},{10,11... | collective-permute-start | bytes 393224 | tf_op jit(solution)/shard_map/ppermute | solution.py:406
  2.2 10.7 %collective-permute-start.5 = (bf16[128,512]{1,0:T(8,128)(2,1)S(1)}, bf16[128,512]{1,0:T(8,128)(2,1)S(1)}, u32[]{:S(2)}, u32[]{:S(2)}) collective-permute-start(bf16[128,512]{1,0:T(8,128)(2,1)S(1)} %arrange_other.1.after_ref.refs_0_), channel_id=1, source_target_pairs={{0,16},{8,24},{16,0},{24,8},{1,17},{9,25},{17,1},{25,9},{2,18},{10... | collective-permute-start | bytes 393224 | tf_op jit(solution)/shard_map/ppermute | solution.py:438
  6.8 5.3 %collective-permute-start.4 = (bf16[32,1024]{1,0:T(8,128)(2,1)S(1)}, bf16[32,1024]{1,0:T(8,128)(2,1)S(1)}, u32[]{:S(2)}, u32[]{:S(2)}) collective-permute-start(bf16[32,1024]{1,0:T(8,128)(2,1)S(1)} %get-tuple-element.24), channel_id=1, source_target_pairs={{0,6},{1,7},{2,4},{3,5},{4,2},{5,3},{6,0},{7,1},{8,14},{9,15},{10,... | collective-permute-start | bytes 196616 | tf_op jit(solution)/shard_map/ppermute | solution.py:426
  9.3 4.3 %collective-permute-start.2 = (bf16[32,1024]{1,0:T(8,128)(2,1)S(1)}, bf16[32,1024]{1,0:T(8,128)(2,1)S(1)}, u32[]{:S(2)}, u32[]{:S(2)}) collective-permute-start(bf16[32,1024]{1,0:T(8,128)(2,1)S(1)} %get-tuple-element.23), channel_id=1, source_target_pairs={{0,2},{1,5},{2,0},{3,7},{4,6},{5,1},{6,4},{7,3},{8,10},{9,13},{10,... | collective-permute-start | bytes 196616 | tf_op jit(solution)/shard_map/ppermute | solution.py:426
  9.9 7.4 %collective-permute-start.7 = (bf16[128,512]{1,0:T(8,128)(2,1)S(1)}, bf16[128,512]{1,0:T(8,128)(2,1)S(1)}, u32[]{:S(2)}, u32[]{:S(2)}) collective-permute-start(bf16[128,512]{1,0:T(8,128)(2,1)S(1)} %arrange_other.1.after_ref.refs_0_), channel_id=1, source_target_pairs={{0,8},{8,0},{16,24},{24,16},{1,9},{9,1},{17,25},{25,17},{2,10},{10... | collective-permute-start | bytes 393224 | tf_op jit(solution)/shard_map/ppermute | solution.py:438
  13.6 5.1 %collective-permute-start.6 = (bf16[128,512]{1,0:T(8,128)(2,1)S(1)}, bf16[128,512]{1,0:T(8,128)(2,1)S(1)}, u32[]{:S(2)}, u32[]{:S(2)}) collective-permute-start(bf16[128,512]{1,0:T(8,128)(2,1)S(1)} %pass_on.5.refs_2_), channel_id=1, source_target_pairs={{0,8},{8,0},{16,24},{24,16},{1,9},{9,1},{17,25},{25,17},{2,10},{10... | collective-permute-start | bytes 393224 | tf_op jit(solution)/shard_map/ppermute | solution.py:438
  15.2 1.3 %collective-permute-start.3 = (bf16[32,1024]{1,0:T(8,128)(2,1)S(1)}, bf16[32,1024]{1,0:T(8,128)(2,1)S(1)}, u32[]{:S(2)}, u32[]{:S(2)}) collective-permute-start(bf16[32,1024]{1,0:T(8,128)(2,1)S(1)} %collective-permute-done.2.refs_1_), channel_id=1, source_target_pairs={{0,1},{1,0},{2,3},{3,2},{4,5},{5,4},{6,7},{7,6},{8,9},{9,8},{10,11... | collective-permute-start | bytes 196616 | tf_op jit(solution)/shard_map/ppermute | solution.py:406
  19.4 5.2 %collective-permute-start.10 = (s16[16,1408]{1,0:T(8,128)(2,1)S(1)}, s16[16,1408]{1,0:T(8,128)(2,1)S(1)}, u32[]{:S(2)}, u32[]{:S(2)}) collective-permute-start(s16[16,1408]{1,0:T(8,128)(2,1)S(1)} %get-tuple-element.30), channel_id=1, source_target_pairs={{0,6},{1,7},{2,4},{3,5},{4,2},{5,3},{6,0},{7,1},{8,14},{9,15},{10,... | collective-permute-start | bytes 135176 | tf_op jit(solution)/shard_map/ppermute | solution.py:406
  21.2 4.0 %collective-permute-start.8 = (s16[16,1408]{1,0:T(8,128)(2,1)S(1)}, s16[16,1408]{1,0:T(8,128)(2,1)S(1)}, u32[]{:S(2)}, u32[]{:S(2)}) collective-permute-start(s16[16,1408]{1,0:T(8,128)(2,1)S(1)} %get-tuple-element.28), channel_id=1, source_target_pairs={{0,2},{1,3},{2,0},{3,1},{4,6},{5,7},{6,4},{7,5},{8,10},{9,11},{10,... | collective-permute-start | bytes 135176 | tf_op jit(solution)/shard_map/ppermute | solution.py:406
  22.3 4.0 %collective-permute-start.9 = (s16[16,1408]{1,0:T(8,128)(2,1)S(1)}, s16[16,1408]{1,0:T(8,128)(2,1)S(1)}, u32[]{:S(2)}, u32[]{:S(2)}) collective-permute-start(s16[16,1408]{1,0:T(8,128)(2,1)S(1)} %get-tuple-element.29), channel_id=1, source_target_pairs={{0,4},{1,5},{2,6},{3,7},{4,0},{5,1},{6,2},{7,3},{8,12},{9,13},{10,... | collective-permute-start | bytes 135176 | tf_op jit(solution)/shard_map/ppermute | solution.py:406

commit v8 on v5

--- a/solution.py
+++ b/solution.py
@@ -61,10 +61,9 @@
     out_ref,
     send_ref,
     pick_ref,
-    tiles_ref,
+    green_ref,
     slip_ref,
     slots_ref,
-    green_ref,
     sems,
 ):
     width = green_ref.shape[0]
@@ -80,12 +79,9 @@
     core = lax.rem(lax.axis_index("patch"), 2)
     arrange_half(slip_ref, out_ref, core, core)
     fetch_greens.wait()
-    tiles = green_ref[...].astype(jnp.float32)
-    for comp in range(green_ref.shape[1]):
-        tiles_ref[comp * width : (comp + 1) * width, :] = tiles[:, comp, :].astype(jnp.bfloat16)
-
-
-def arrange_other_kernel(slip_ref, green_ref, block_ref, out_ref):
+
+
+def arrange_other_kernel(slip_ref, block_ref, out_ref):
     core = lax.rem(lax.axis_index("patch"), 2)
     arrange_half(slip_ref, out_ref, core, 1 - core)
 
@@ -96,7 +92,7 @@
 
 def arrange_own(slips, slots, greens, chips, per_chip, capacity):
     patches, both, samples = slips.shape
-    width, components, lags = greens.shape
+    width = greens.shape[0]
     block = jax.ShapeDtypeStruct(
         (samples // BLOCK * both // 2, 2 * patches * BLOCK), jnp.bfloat16
     )
@@ -107,12 +103,11 @@
             block,
             jax.ShapeDtypeStruct((chips * capacity, 2 * width), jnp.bfloat16),
             jax.ShapeDtypeStruct((chips * capacity, per_chip), jnp.bfloat16),
-            jax.ShapeDtypeStruct((components * width, lags), jnp.bfloat16),
+            jax.ShapeDtypeStruct(greens.shape, greens.dtype),
         ),
         scratch_shapes=[
             pltpu.VMEM(slips.shape, slips.dtype),
             pltpu.VMEM(slots.shape, slots.dtype),
-            pltpu.VMEM(greens.shape, greens.dtype),
             pltpu.SemaphoreType.DMA((3,)),
         ],
         compiler_params=params(),
@@ -120,19 +115,14 @@
     )(*in_hbm(slips, slots, greens))
 
 
-def arrange_other(slips, greens, block):
+def arrange_other(slips, block):
     return pl.pallas_call(
         arrange_other_kernel,
-        in_specs=[
-            pl.BlockSpec(memory_space=pltpu.VMEM),
-            pl.BlockSpec(memory_space=pl.ANY),
-            pl.BlockSpec(memory_space=pltpu.VMEM),
-        ],
         out_shape=jax.ShapeDtypeStruct(block.shape, block.dtype),
-        input_output_aliases={2: 0},
+        input_output_aliases={1: 0},
         compiler_params=params(),
         name="arrange_other",
-    )(slips, greens, block)
+    )(slips, block)
 
 
 def earlier_in_chip(count, per_chip):
@@ -186,14 +176,10 @@
     capacity = send_ref.shape[0] // chips
     half = capacity // 2
     core = lax.rem(lax.axis_index("patch"), 2)
-    width, components, _ = other_ref.shape
-    tiles = other_ref[...].astype(jnp.float32)
+    tiles = jnp.concatenate([own_ref[...], other_ref[...]], axis=0).astype(jnp.float32)
     by_comp = []
-    for comp in range(components):
-        both = jnp.concatenate(
-            [own_ref[comp * width : (comp + 1) * width, :], tiles[:, comp, :].astype(jnp.bfloat16)],
-            axis=0,
-        )
+    for comp in range(own_ref.shape[1]):
+        both = tiles[:, comp, :].astype(jnp.bfloat16)
         chosen = jnp.dot(send_ref[...], both, preferred_element_type=jnp.float32)
         chosen = [chosen[step * capacity : (step + 1) * capacity] for step in range(chips)]
         last = chosen[-1]
@@ -427,7 +413,7 @@
     block, send, pick, own_tiles = arrange_own(
         slips, patch_slot.reshape(1, -1), greens, chips, 2 * patches, capacity
     )
-    block = arrange_other(other, other_tiles, block)
+    block = arrange_other(other, block)
 
     pieces = list(route_tiles(send, own_tiles, other_tiles, block, chips))
     arrived = [None] * (len(pieces) - 1)

time: 26.8 us -> 26.7 us (level)
    pallas_call x1, Pallas kernels: 1.48 us -> 1.14 us  [arrange_own(): pl.pallas_call(functools.partial(arrange_own_kernel, chips, per_chip, cap...]
    pallas_call x1, Pallas kernels: 0.51 us -> 0.84 us  [route_tiles(): pl.pallas_call(functools.partial(route_kernel, chips), in_specs=[pl.Block...]
where the time goes in v8:
time: 26.7 us; the launch traced here: 26.6 us
  starting transfers between devices  14.9 us (56%)
  Pallas kernels  5.86 us (22%)
  waiting for transfers between devices  5.71 us (21%)
    ppermute x3, starting transfers between devices, local(): lax.ppermute(blocks[step - low], 'site', [(i, i ^ low) for i in range(sit...  7.31 us
    ppermute x7, starting transfers between devices, over_patch(): lax.ppermute(value, 'patch', [(i, i ^ offset) for i in range(devices)])  4.57 us
    ppermute x7, waiting for transfers between devices, over_patch(): lax.ppermute(value, 'patch', [(i, i ^ offset) for i in range(devices)])  3.95 us
    ppermute x2, starting transfers between devices, local(): lax.ppermute(pieces[1 + index], 'patch', [(i, i ^ 2 * hops[i % 2]) for i...  3.05 us
    ppermute x2, waiting for transfers between devices, local(): lax.ppermute(pieces[1 + index], 'patch', [(i, i ^ 2 * hops[i % 2]) for i...  1.75 us
    pallas_call x1, Pallas kernels, convolve_first(): pl.pallas_call(functools.partial(convolve_first_kernel, rows), out_shape=...  1.38 us
    pallas_call x1, Pallas kernels, arrange_own(): pl.pallas_call(functools.partial(arrange_own_kernel, chips, per_chip, cap...  1.14 us
    pallas_call x1, Pallas kernels, route_tiles(): pl.pallas_call(functools.partial(route_kernel, chips), in_specs=[pl.Block...  0.84 us
  transfers between devices with their start and end apart: 12, of which 5 were waited for; matrix products, arithmetic and copies ran while one was open for 0% of the time, Pallas kernels for 16%

profile of v8, /device:TPU:0, one launch (start us, length us, event | category | flops | bytes accessed | tf_op | source)
XLA Modules:
  0.0 26.6 jit_solution(16086753824465002658)
XLA Ops:
  0.0 0.5 %collective-permute-start.1 = (bf16[16,16,256]{2,1,0:T(8,128)(2,1)}, bf16[16,16,256]{2,1,0:T(8,128)(2,1)S(1)}, u32[]{:S(2)}, u32[]{:S(2)}) collective-permute-start(bf16[16,16,256]{2,1,0:T(8,128)(2,1)} %slip_hbm.1), channel_id=1, source_target_pairs={{0,1},{1,0},{2,3},{3,2},{4,5},{5,4},{6,7},{7,6},{8,9},{9,8},{10,11... | collective-permute-start | bytes 393224 | tf_op jit(solution)/shard_map/ppermute | solution.py:402
  0.5 0.1 collective-permute-start
  0.5 1.1 %arrange_own.1 = (bf16[128,512]{1,0:T(8,128)(2,1)S(1)}, bf16[64,64]{1,0:T(8,128)(2,1)S(1)}, bf16[64,32]{1,0:T(8,128)(2,1)S(1)}, bf16[32,2,1024]{2,1,0:T(2,128)(2,1)S(1)}) custom-call(bf16[16,16,256]{2,1,0:T(8,128)(2,1)} %slip_hbm.1, s32[1,128]{1,0:T(1,128)} %bitcast.5, bf16[32,2,1024]{2,1,0:T(2,128)(2,1)} %bitcast.4), custom_call_target="tpu_custom_call" | custom-call | tf_op jit(solution)/shard_map/arrange_own/pallas_call | solution.py:99
  1.7 0.0 collective-permute-done.1.slip_ref
  1.7 0.2 arrange_other.1.after_ref.refs_0_
  1.9 4.1 %collective-permute-start.6 = (bf16[128,512]{1,0:T(8,128)(2,1)S(1)}, bf16[128,512]{1,0:T(8,128)(2,1)S(1)}, u32[]{:S(2)}, u32[]{:S(2)}) collective-permute-start(bf16[128,512]{1,0:T(8,128)(2,1)S(1)} %arrange_other.1.after_ref.refs_0_), channel_id=1, source_target_pairs={{0,16},{8,24},{16,0},{24,8},{1,17},{9,25},{17,1},{25,9},{2,18},{10... | collective-permute-start | bytes 393224 | tf_op jit(solution)/shard_map/ppermute | solution.py:433
  6.0 0.0 collective-permute-done.other_ref
  6.0 0.8 %route_tiles.1 = (bf16[32,1024]{1,0:T(8,128)(2,1)S(1)}, bf16[32,1024]{1,0:T(8,128)(2,1)S(1)}, bf16[16,1024]{1,0:T(8,128)(2,1)S(1)}) custom-call(bf16[64,64]{1,0:T(8,128)(2,1)S(1)} %get-tuple-element.19.send_ref, bf16[32,2,1024]{2,1,0:T(2,128)(2,1)S(1)} %get-tuple-element.20.own_ref, bf16[32,2,1024]{2,1,0:T(2,128)(2,1)S(1)} %collective-permute-done.other_ref, ...), custom_call_target="tpu_custom_call" | custom-call | tf_op jit(solution)/shard_map/route_tiles/pallas_call | solution.py:200
  6.8 1.6 %collective-permute-start.2 = (bf16[32,1024]{1,0:T(8,128)(2,1)S(1)}, bf16[32,1024]{1,0:T(8,128)(2,1)S(1)}, u32[]{:S(2)}, u32[]{:S(2)}) collective-permute-start(bf16[32,1024]{1,0:T(8,128)(2,1)S(1)} %get-tuple-element.23), channel_id=1, source_target_pairs={{0,2},{1,5},{2,0},{3,7},{4,6},{5,1},{6,4},{7,3},{8,10},{9,13},{10,... | collective-permute-start | bytes 196616 | tf_op jit(solution)/shard_map/ppermute | solution.py:422
  8.4 1.5 %collective-permute-start.4 = (bf16[16,1024]{1,0:T(8,128)(2,1)S(1)}, bf16[16,1024]{1,0:T(8,128)(2,1)S(1)}, u32[]{:S(2)}, u32[]{:S(2)}) collective-permute-start(bf16[16,1024]{1,0:T(8,128)(2,1)S(1)} %get-tuple-element.24), channel_id=1, source_target_pairs={{0,6},{1,7},{2,4},{3,5},{4,2},{5,3},{6,0},{7,1},{8,14},{9,15},{10,... | collective-permute-start | bytes 98312 | tf_op jit(solution)/shard_map/ppermute | solution.py:422
  9.9 1.6 %collective-permute-start.8 = (bf16[128,512]{1,0:T(8,128)(2,1)S(1)}, bf16[128,512]{1,0:T(8,128)(2,1)S(1)}, u32[]{:S(2)}, u32[]{:S(2)}) collective-permute-start(bf16[128,512]{1,0:T(8,128)(2,1)S(1)} %arrange_other.1.after_ref.refs_0_), channel_id=1, source_target_pairs={{0,8},{8,0},{16,24},{24,16},{1,9},{9,1},{17,25},{25,17},{2,10},{10... | collective-permute-start | bytes 393224 | tf_op jit(solution)/shard_map/ppermute | solution.py:433
  11.4 1.7 %collective-permute-done.4.refs_3_.refs_2_ = bf16[16,1024]{1,0:T(8,128)(2,1)S(1)} collective-permute-done((bf16[16,1024]{1,0:T(8,128)(2,1)S(1)}, bf16[16,1024]{1,0:T(8,128)(2,1)S(1)}, u32[]{:S(2)}, u32[]{:S(2)}) %collective-permute-start.4) | collective-permute-done | bytes 32800 | tf_op jit(solution)/shard_map/ppermute | solution.py:422
  13.2 0.0 collective-permute-done.2.refs_1_
  13.2 0.0 collective-permute-done.6.refs_0_
  13.2 1.6 %collective-permute-start.7 = (bf16[128,512]{1,0:T(8,128)(2,1)S(1)}, bf16[128,512]{1,0:T(8,128)(2,1)S(1)}, u32[]{:S(2)}, u32[]{:S(2)}) collective-permute-start(bf16[128,512]{1,0:T(8,128)(2,1)S(1)} %pass_on.1.refs_2_), channel_id=1, source_target_pairs={{0,8},{8,0},{16,24},{24,16},{1,9},{9,1},{17,25},{25,17},{2,10},{10... | collective-permute-start | bytes 393224 | tf_op jit(solution)/shard_map/ppermute | solution.py:433
  14.8 0.0 collective-permute-start.3
  14.8 0.5 %collective-permute-start.5 = (bf16[16,1024]{1,0:T(8,128)(2,1)S(1)}, bf16[16,1024]{1,0:T(8,128)(2,1)S(1)}, u32[]{:S(2)}, u32[]{:S(2)}) collective-permute-start(bf16[16,1024]{1,0:T(8,128)(2,1)S(1)} %collective-permute-done.4.refs_3_.refs_2_), channel_id=1, source_target_pairs={{0,1},{1,0},{2,3},{3,2},{4,5},{5,4},{6,7},{7,6},{8,9},{9,8},{10,11... | collective-permute-start | bytes 98312 | tf_op jit(solution)/shard_map/ppermute | solution.py:402
  15.4 0.9 %collective-permute-done.5.refs_4_ = bf16[16,1024]{1,0:T(8,128)(2,1)S(1)} collective-permute-done((bf16[16,1024]{1,0:T(8,128)(2,1)S(1)}, bf16[16,1024]{1,0:T(8,128)(2,1)S(1)}, u32[]{:S(2)}, u32[]{:S(2)}) %collective-permute-start.5) | collective-permute-done | bytes 32800 | tf_op jit(solution)/shard_map/ppermute | solution.py:402
  16.2 0.0 collective-permute-done.3.refs_2_
  16.2 0.8 %shift_tiles.1.shifted_ref = bf16[512,2304]{1,0:T(8,128)(2,1)S(1)} custom-call(bf16[64,32]{1,0:T(8,128)(2,1)S(1)} %get-tuple-element.18.pick_ref, bf16[32,1024]{1,0:T(8,128)(2,1)S(1)} %get-tuple-element.22.refs_0_, bf16[32,1024]{1,0:T(8,128)(2,1)S(1)} %collective-permute-done.2.refs_1_, bf16[32,1024]{1,0:T(8,128)(2,1)S(1)} %collective-permute-done.3.refs_2_, ...), custom_call_target="tpu_custom_call" | custom-call | tf_op jit(solution)/shard_map/shift_tiles/pallas_call | solution.py:254
  17.0 0.0 collective-permute-done.8.refs_1_
  17.0 1.4 %convolve_first.1 = (f32[3,16,1280]{2,1,0:T(8,128)S(1)}, s16[3,16,1408]{2,1,0:T(8,128)(2,1)S(1)}) custom-call(bf16[512,2304]{1,0:T(8,128)(2,1)S(1)} %shift_tiles.1.shifted_ref, bf16[128,512]{1,0:T(8,128)(2,1)S(1)} %arrange_other.1.after_ref.refs_0_, bf16[128,512]{1,0:T(8,128)(2,1)S(1)} %collective-permute-done.8.refs_1_, bf16[128,512]{1,0:T(8,128)(2,1)S(1)} %pass_on.1.refs_2_), custom_call_target="tpu_custom_call" | custom-call | tf_op jit(solution)/shard_map/convolve_first/pallas_call | solution.py:323
  18.4 0.0 collective-permute-done.7.slip_ref
  18.4 0.7 %convolve_last.1 = (f32[16,1280]{1,0:T(8,128)S(1)}, s16[16,1408]{1,0:T(8,128)(2,1)S(1)}, s16[16,1408]{1,0:T(8,128)(2,1)S(1)}, s16[16,1408]{1,0:T(8,128)(2,1)S(1)}) custom-call(bf16[512,2304]{1,0:T(8,128)(2,1)S(1)} %shift_tiles.1.shifted_ref, bf16[128,512]{1,0:T(8,128)(2,1)S(1)} %collective-permute-done.7.slip_ref, ...), custom_call_target="tpu_custom_call" | custom-call | tf_op jit(solution)/shard_map/convolve_last/pallas_call | solution.py:359
  19.2 2.0 %collective-permute-start.10 = (s16[16,1408]{1,0:T(8,128)(2,1)S(1)}, s16[16,1408]{1,0:T(8,128)(2,1)S(1)}, u32[]{:S(2)}, u32[]{:S(2)}) collective-permute-start(s16[16,1408]{1,0:T(8,128)(2,1)S(1)} %get-tuple-element.29), channel_id=1, source_target_pairs={{0,6},{1,7},{2,4},{3,5},{4,2},{5,3},{6,0},{7,1},{8,14},{9,15},{10,... | collective-permute-start | bytes 135176 | tf_op jit(solution)/shard_map/ppermute | solution.py:402
  21.2 0.6 %collective-permute-start.11 = (s16[16,1408]{1,0:T(8,128)(2,1)S(1)}, s16[16,1408]{1,0:T(8,128)(2,1)S(1)}, u32[]{:S(2)}, u32[]{:S(2)}) collective-permute-start(s16[16,1408]{1,0:T(8,128)(2,1)S(1)} %get-tuple-element.30), channel_id=1, source_target_pairs={{0,4},{1,5},{2,6},{3,7},{4,0},{5,1},{6,2},{7,3},{8,12},{9,13},{10,... | collective-permute-start | bytes 135176 | tf_op jit(solution)/shard_map/ppermute | solution.py:402
  21.8 1.0 %collective-permute-start.9 = (s16[16,1408]{1,0:T(8,128)(2,1)S(1)}, s16[16,1408]{1,0:T(8,128)(2,1)S(1)}, u32[]{:S(2)}, u32[]{:S(2)}) collective-permute-start(s16[16,1408]{1,0:T(8,128)(2,1)S(1)} %get-tuple-element.28), channel_id=1, source_target_pairs={{0,2},{1,3},{2,0},{3,1},{4,6},{5,7},{6,4},{7,5},{8,10},{9,11},{10,... | collective-permute-start | bytes 135176 | tf_op jit(solution)/shard_map/ppermute | solution.py:402
  22.7 1.5 %collective-permute-done.10.refs_1_ = s16[16,1408]{1,0:T(8,128)(2,1)S(1)} collective-permute-done((s16[16,1408]{1,0:T(8,128)(2,1)S(1)}, s16[16,1408]{1,0:T(8,128)(2,1)S(1)}, u32[]{:S(2)}, u32[]{:S(2)}) %collective-permute-start.10) | collective-permute-done | bytes 45088 | tf_op jit(solution)/shard_map/ppermute | solution.py:402
  24.3 1.0 %collective-permute-done.11.refs_2_ = s16[16,1408]{1,0:T(8,128)(2,1)S(1)} collective-permute-done((s16[16,1408]{1,0:T(8,128)(2,1)S(1)}, s16[16,1408]{1,0:T(8,128)(2,1)S(1)}, u32[]{:S(2)}, u32[]{:S(2)}) %collective-permute-start.11) | collective-permute-done | bytes 45088 | tf_op jit(solution)/shard_map/ppermute | solution.py:402
  25.3 0.6 %collective-permute-done.9.refs_0_ = s16[16,1408]{1,0:T(8,128)(2,1)S(1)} collective-permute-done((s16[16,1408]{1,0:T(8,128)(2,1)S(1)}, s16[16,1408]{1,0:T(8,128)(2,1)S(1)}, u32[]{:S(2)}, u32[]{:S(2)}) %collective-permute-start.9) | collective-permute-done | bytes 45088 | tf_op jit(solution)/shard_map/ppermute | solution.py:402
  25.8 0.7 %add_up.1 = f32[8,2,1280]{2,1,0:T(2,128)} custom-call(f32[16,1280]{1,0:T(8,128)S(1)} %get-tuple-element.27.own_ref, s16[16,1408]{1,0:T(8,128)(2,1)S(1)} %collective-permute-done.9.refs_0_, s16[16,1408]{1,0:T(8,128)(2,1)S(1)} %collective-permute-done.10.refs_1_, s16[16,1408]{1,0:T(8,128)(2,1)S(1)} %collective-permute-done.11.refs_2_), custom_call_target="tpu_custom_call" | custom-call | tf_op jit(solution)/shard_map/add_up/pallas_call | solution.py:382
  (1 shorter events, 0.0 us)
Async XLA Ops:
  0.0 1.7 %collective-permute-start.1 = (bf16[16,16,256]{2,1,0:T(8,128)(2,1)}, bf16[16,16,256]{2,1,0:T(8,128)(2,1)S(1)}, u32[]{:S(2)}, u32[]{:S(2)}) collective-permute-start(bf16[16,16,256]{2,1,0:T(8,128)(2,1)} %slip_hbm.1), channel_id=1, source_target_pairs={{0,1},{1,0},{2,3},{3,2},{4,5},{5,4},{6,7},{7,6},{8,9},{9,8},{10,11... | collective-permute-start | bytes 393224 | tf_op jit(solution)/shard_map/ppermute | solution.py:402
  0.5 5.5 %collective-permute-start = (bf16[32,2,1024]{2,1,0:T(2,128)(2,1)}, bf16[32,2,1024]{2,1,0:T(2,128)(2,1)S(1)}, u32[]{:S(2)}, u32[]{:S(2)}) collective-permute-start(bf16[32,2,1024]{2,1,0:T(2,128)(2,1)} %bitcast.3), channel_id=1, source_target_pairs={{0,1},{1,0},{2,3},{3,2},{4,5},{5,4},{6,7},{7,6},{8,9},{9,8},{10,11... | collective-permute-start | bytes 393224 | tf_op jit(solution)/shard_map/ppermute | solution.py:402
  1.9 11.3 %collective-permute-start.6 = (bf16[128,512]{1,0:T(8,128)(2,1)S(1)}, bf16[128,512]{1,0:T(8,128)(2,1)S(1)}, u32[]{:S(2)}, u32[]{:S(2)}) collective-permute-start(bf16[128,512]{1,0:T(8,128)(2,1)S(1)} %arrange_other.1.after_ref.refs_0_), channel_id=1, source_target_pairs={{0,16},{8,24},{16,0},{24,8},{1,17},{9,25},{17,1},{25,9},{2,18},{10... | collective-permute-start | bytes 393224 | tf_op jit(solution)/shard_map/ppermute | solution.py:433
  6.8 6.4 %collective-permute-start.2 = (bf16[32,1024]{1,0:T(8,128)(2,1)S(1)}, bf16[32,1024]{1,0:T(8,128)(2,1)S(1)}, u32[]{:S(2)}, u32[]{:S(2)}) collective-permute-start(bf16[32,1024]{1,0:T(8,128)(2,1)S(1)} %get-tuple-element.23), channel_id=1, source_target_pairs={{0,2},{1,5},{2,0},{3,7},{4,6},{5,1},{6,4},{7,3},{8,10},{9,13},{10,... | collective-permute-start | bytes 196616 | tf_op jit(solution)/shard_map/ppermute | solution.py:422
  8.4 4.8 %collective-permute-start.4 = (bf16[16,1024]{1,0:T(8,128)(2,1)S(1)}, bf16[16,1024]{1,0:T(8,128)(2,1)S(1)}, u32[]{:S(2)}, u32[]{:S(2)}) collective-permute-start(bf16[16,1024]{1,0:T(8,128)(2,1)S(1)} %get-tuple-element.24), channel_id=1, source_target_pairs={{0,6},{1,7},{2,4},{3,5},{4,2},{5,3},{6,0},{7,1},{8,14},{9,15},{10,... | collective-permute-start | bytes 98312 | tf_op jit(solution)/shard_map/ppermute | solution.py:422
  9.9 7.2 %collective-permute-start.8 = (bf16[128,512]{1,0:T(8,128)(2,1)S(1)}, bf16[128,512]{1,0:T(8,128)(2,1)S(1)}, u32[]{:S(2)}, u32[]{:S(2)}) collective-permute-start(bf16[128,512]{1,0:T(8,128)(2,1)S(1)} %arrange_other.1.after_ref.refs_0_), channel_id=1, source_target_pairs={{0,8},{8,0},{16,24},{24,16},{1,9},{9,1},{17,25},{25,17},{2,10},{10... | collective-permute-start | bytes 393224 | tf_op jit(solution)/shard_map/ppermute | solution.py:433
  13.2 5.2 %collective-permute-start.7 = (bf16[128,512]{1,0:T(8,128)(2,1)S(1)}, bf16[128,512]{1,0:T(8,128)(2,1)S(1)}, u32[]{:S(2)}, u32[]{:S(2)}) collective-permute-start(bf16[128,512]{1,0:T(8,128)(2,1)S(1)} %pass_on.1.refs_2_), channel_id=1, source_target_pairs={{0,8},{8,0},{16,24},{24,16},{1,9},{9,1},{17,25},{25,17},{2,10},{10... | collective-permute-start | bytes 393224 | tf_op jit(solution)/shard_map/ppermute | solution.py:433
  14.8 1.4 %collective-permute-start.3 = (bf16[32,1024]{1,0:T(8,128)(2,1)S(1)}, bf16[32,1024]{1,0:T(8,128)(2,1)S(1)}, u32[]{:S(2)}, u32[]{:S(2)}) collective-permute-start(bf16[32,1024]{1,0:T(8,128)(2,1)S(1)} %collective-permute-done.2.refs_1_), channel_id=1, source_target_pairs={{0,1},{1,0},{2,3},{3,2},{4,5},{5,4},{6,7},{7,6},{8,9},{9,8},{10,11... | collective-permute-start | bytes 196616 | tf_op jit(solution)/shard_map/ppermute | solution.py:402
  14.8 1.4 %collective-permute-start.5 = (bf16[16,1024]{1,0:T(8,128)(2,1)S(1)}, bf16[16,1024]{1,0:T(8,128)(2,1)S(1)}, u32[]{:S(2)}, u32[]{:S(2)}) collective-permute-start(bf16[16,1024]{1,0:T(8,128)(2,1)S(1)} %collective-permute-done.4.refs_3_.refs_2_), channel_id=1, source_target_pairs={{0,1},{1,0},{2,3},{3,2},{4,5},{5,4},{6,7},{7,6},{8,9},{9,8},{10,11... | collective-permute-start | bytes 98312 | tf_op jit(solution)/shard_map/ppermute | solution.py:402
  19.2 5.1 %collective-permute-start.10 = (s16[16,1408]{1,0:T(8,128)(2,1)S(1)}, s16[16,1408]{1,0:T(8,128)(2,1)S(1)}, u32[]{:S(2)}, u32[]{:S(2)}) collective-permute-start(s16[16,1408]{1,0:T(8,128)(2,1)S(1)} %get-tuple-element.29), channel_id=1, source_target_pairs={{0,6},{1,7},{2,4},{3,5},{4,2},{5,3},{6,0},{7,1},{8,14},{9,15},{10,... | collective-permute-start | bytes 135176 | tf_op jit(solution)/shard_map/ppermute | solution.py:402
  21.2 4.0 %collective-permute-start.11 = (s16[16,1408]{1,0:T(8,128)(2,1)S(1)}, s16[16,1408]{1,0:T(8,128)(2,1)S(1)}, u32[]{:S(2)}, u32[]{:S(2)}) collective-permute-start(s16[16,1408]{1,0:T(8,128)(2,1)S(1)} %get-tuple-element.30), channel_id=1, source_target_pairs={{0,4},{1,5},{2,6},{3,7},{4,0},{5,1},{6,2},{7,3},{8,12},{9,13},{10,... | collective-permute-start | bytes 135176 | tf_op jit(solution)/shard_map/ppermute | solution.py:402
  21.8 4.0 %collective-permute-start.9 = (s16[16,1408]{1,0:T(8,128)(2,1)S(1)}, s16[16,1408]{1,0:T(8,128)(2,1)S(1)}, u32[]{:S(2)}, u32[]{:S(2)}) collective-permute-start(s16[16,1408]{1,0:T(8,128)(2,1)S(1)} %get-tuple-element.28), channel_id=1, source_target_pairs={{0,2},{1,3},{2,0},{3,1},{4,6},{5,7},{6,4},{7,5},{8,10},{9,11},{10,... | collective-permute-start | bytes 135176 | tf_op jit(solution)/shard_map/ppermute | solution.py:402

commit v9 on v8

--- a/solution.py
+++ b/solution.py
@@ -266,11 +266,12 @@
     for step, ref in enumerate(slip_refs):
         stack_ref[step * height : (step + 1) * height] = ref[...]
     for comp in range(components):
-        product_ref[...] = jnp.dot(
+        product_ref[comp] = jnp.dot(
             stack_ref[...],
             shifted_ref[:, comp * width : (comp + 1) * width],
             preferred_element_type=jnp.float32,
         )
+    for comp in range(components):
         for step in range(len(slip_refs)):
             total = None
             for inner in range(per_reg):
@@ -278,7 +279,7 @@
                 for outer in range(inner, blocks, per_reg):
                     lead = outer // per_reg * LANES
                     start = step * height + outer * rows
-                    block = product_ref[start : start + rows, :]
+                    block = product_ref[comp, start : start + rows, :]
                     pieces = [jnp.zeros((rows, lead), jnp.float32)] if lead else []
                     pieces.append(block[:, : min(width, length - lead)])
                     if length > lead + width:
@@ -313,7 +314,7 @@
 def convolve_scratch(shifted, count, height, depth, components):
     return [
         pltpu.VMEM((count * height, depth), jnp.bfloat16),
-        pltpu.VMEM((count * height, shifted.shape[1] // components), jnp.float32),
+        pltpu.VMEM((components, count * height, shifted.shape[1] // components), jnp.float32),
     ]
 
 

time: 26.7 us -> 26.7 us (level)
  no operation moved by 1% of the time
where the time goes in v9:
time: 26.7 us; the launch traced here: 26.6 us
  starting transfers between devices  14.9 us (56%)
  Pallas kernels  5.86 us (22%)
  waiting for transfers between devices  5.71 us (21%)
    ppermute x3, starting transfers between devices, local(): lax.ppermute(blocks[step - low], 'site', [(i, i ^ low) for i in range(sit...  7.31 us
    ppermute x7, starting transfers between devices, over_patch(): lax.ppermute(value, 'patch', [(i, i ^ offset) for i in range(devices)])  4.57 us
    ppermute x7, waiting for transfers between devices, over_patch(): lax.ppermute(value, 'patch', [(i, i ^ offset) for i in range(devices)])  3.95 us
    ppermute x2, starting transfers between devices, local(): lax.ppermute(pieces[1 + index], 'patch', [(i, i ^ 2 * hops[i % 2]) for i...  3.05 us
    ppermute x2, waiting for transfers between devices, local(): lax.ppermute(pieces[1 + index], 'patch', [(i, i ^ 2 * hops[i % 2]) for i...  1.75 us
    pallas_call x1, Pallas kernels, convolve_first(): pl.pallas_call(functools.partial(convolve_first_kernel, rows), out_shape=...  1.38 us
    pallas_call x1, Pallas kernels, arrange_own(): pl.pallas_call(functools.partial(arrange_own_kernel, chips, per_chip, cap...  1.14 us
    pallas_call x1, Pallas kernels, route_tiles(): pl.pallas_call(functools.partial(route_kernel, chips), in_specs=[pl.Block...  0.84 us
  transfers between devices with their start and end apart: 12, of which 5 were waited for; matrix products, arithmetic and copies ran while one was open for 0% of the time, Pallas kernels for 16%

profile of v9, /device:TPU:0, one launch (start us, length us, event | category | flops | bytes accessed | tf_op | source)
XLA Modules:
  0.0 26.6 jit_solution(16086753824465002658)
XLA Ops:
  0.0 0.5 %collective-permute-start.1 = (bf16[16,16,256]{2,1,0:T(8,128)(2,1)}, bf16[16,16,256]{2,1,0:T(8,128)(2,1)S(1)}, u32[]{:S(2)}, u32[]{:S(2)}) collective-permute-start(bf16[16,16,256]{2,1,0:T(8,128)(2,1)} %slip_hbm.1), channel_id=1, source_target_pairs={{0,1},{1,0},{2,3},{3,2},{4,5},{5,4},{6,7},{7,6},{8,9},{9,8},{10,11... | collective-permute-start | bytes 393224 | tf_op jit(solution)/shard_map/ppermute | solution.py:403
  0.5 0.1 collective-permute-start
  0.5 1.1 %arrange_own.1 = (bf16[128,512]{1,0:T(8,128)(2,1)S(1)}, bf16[64,64]{1,0:T(8,128)(2,1)S(1)}, bf16[64,32]{1,0:T(8,128)(2,1)S(1)}, bf16[32,2,1024]{2,1,0:T(2,128)(2,1)S(1)}) custom-call(bf16[16,16,256]{2,1,0:T(8,128)(2,1)} %slip_hbm.1, s32[1,128]{1,0:T(1,128)} %bitcast.5, bf16[32,2,1024]{2,1,0:T(2,128)(2,1)} %bitcast.4), custom_call_target="tpu_custom_call" | custom-call | tf_op jit(solution)/shard_map/arrange_own/pallas_call | solution.py:99
  1.7 0.0 collective-permute-done.1.slip_ref
  1.7 0.2 arrange_other.1.after_ref.refs_0_
  1.9 4.1 %collective-permute-start.6 = (bf16[128,512]{1,0:T(8,128)(2,1)S(1)}, bf16[128,512]{1,0:T(8,128)(2,1)S(1)}, u32[]{:S(2)}, u32[]{:S(2)}) collective-permute-start(bf16[128,512]{1,0:T(8,128)(2,1)S(1)} %arrange_other.1.after_ref.refs_0_), channel_id=1, source_target_pairs={{0,16},{8,24},{16,0},{24,8},{1,17},{9,25},{17,1},{25,9},{2,18},{10... | collective-permute-start | bytes 393224 | tf_op jit(solution)/shard_map/ppermute | solution.py:434
  6.0 0.0 collective-permute-done.other_ref
  6.0 0.8 %route_tiles.1 = (bf16[32,1024]{1,0:T(8,128)(2,1)S(1)}, bf16[32,1024]{1,0:T(8,128)(2,1)S(1)}, bf16[16,1024]{1,0:T(8,128)(2,1)S(1)}) custom-call(bf16[64,64]{1,0:T(8,128)(2,1)S(1)} %get-tuple-element.19.send_ref, bf16[32,2,1024]{2,1,0:T(2,128)(2,1)S(1)} %get-tuple-element.20.own_ref, bf16[32,2,1024]{2,1,0:T(2,128)(2,1)S(1)} %collective-permute-done.other_ref, ...), custom_call_target="tpu_custom_call" | custom-call | tf_op jit(solution)/shard_map/route_tiles/pallas_call | solution.py:200
  6.8 1.6 %collective-permute-start.2 = (bf16[32,1024]{1,0:T(8,128)(2,1)S(1)}, bf16[32,1024]{1,0:T(8,128)(2,1)S(1)}, u32[]{:S(2)}, u32[]{:S(2)}) collective-permute-start(bf16[32,1024]{1,0:T(8,128)(2,1)S(1)} %get-tuple-element.23), channel_id=1, source_target_pairs={{0,2},{1,5},{2,0},{3,7},{4,6},{5,1},{6,4},{7,3},{8,10},{9,13},{10,... | collective-permute-start | bytes 196616 | tf_op jit(solution)/shard_map/ppermute | solution.py:423
  8.4 1.5 %collective-permute-start.4 = (bf16[16,1024]{1,0:T(8,128)(2,1)S(1)}, bf16[16,1024]{1,0:T(8,128)(2,1)S(1)}, u32[]{:S(2)}, u32[]{:S(2)}) collective-permute-start(bf16[16,1024]{1,0:T(8,128)(2,1)S(1)} %get-tuple-element.24), channel_id=1, source_target_pairs={{0,6},{1,7},{2,4},{3,5},{4,2},{5,3},{6,0},{7,1},{8,14},{9,15},{10,... | collective-permute-start | bytes 98312 | tf_op jit(solution)/shard_map/ppermute | solution.py:423
  9.9 1.6 %collective-permute-start.8 = (bf16[128,512]{1,0:T(8,128)(2,1)S(1)}, bf16[128,512]{1,0:T(8,128)(2,1)S(1)}, u32[]{:S(2)}, u32[]{:S(2)}) collective-permute-start(bf16[128,512]{1,0:T(8,128)(2,1)S(1)} %arrange_other.1.after_ref.refs_0_), channel_id=1, source_target_pairs={{0,8},{8,0},{16,24},{24,16},{1,9},{9,1},{17,25},{25,17},{2,10},{10... | collective-permute-start | bytes 393224 | tf_op jit(solution)/shard_map/ppermute | solution.py:434
  11.4 1.7 %collective-permute-done.4.refs_3_.refs_2_ = bf16[16,1024]{1,0:T(8,128)(2,1)S(1)} collective-permute-done((bf16[16,1024]{1,0:T(8,128)(2,1)S(1)}, bf16[16,1024]{1,0:T(8,128)(2,1)S(1)}, u32[]{:S(2)}, u32[]{:S(2)}) %collective-permute-start.4) | collective-permute-done | bytes 32800 | tf_op jit(solution)/shard_map/ppermute | solution.py:423
  13.2 0.0 collective-permute-done.2.refs_1_
  13.2 0.0 collective-permute-done.6.refs_0_
  13.2 1.6 %collective-permute-start.7 = (bf16[128,512]{1,0:T(8,128)(2,1)S(1)}, bf16[128,512]{1,0:T(8,128)(2,1)S(1)}, u32[]{:S(2)}, u32[]{:S(2)}) collective-permute-start(bf16[128,512]{1,0:T(8,128)(2,1)S(1)} %pass_on.1.refs_2_), channel_id=1, source_target_pairs={{0,8},{8,0},{16,24},{24,16},{1,9},{9,1},{17,25},{25,17},{2,10},{10... | collective-permute-start | bytes 393224 | tf_op jit(solution)/shard_map/ppermute | solution.py:434
  14.8 0.0 collective-permute-start.3
  14.8 0.5 %collective-permute-start.5 = (bf16[16,1024]{1,0:T(8,128)(2,1)S(1)}, bf16[16,1024]{1,0:T(8,128)(2,1)S(1)}, u32[]{:S(2)}, u32[]{:S(2)}) collective-permute-start(bf16[16,1024]{1,0:T(8,128)(2,1)S(1)} %collective-permute-done.4.refs_3_.refs_2_), channel_id=1, source_target_pairs={{0,1},{1,0},{2,3},{3,2},{4,5},{5,4},{6,7},{7,6},{8,9},{9,8},{10,11... | collective-permute-start | bytes 98312 | tf_op jit(solution)/shard_map/ppermute | solution.py:403
  15.4 0.9 %collective-permute-done.5.refs_4_ = bf16[16,1024]{1,0:T(8,128)(2,1)S(1)} collective-permute-done((bf16[16,1024]{1,0:T(8,128)(2,1)S(1)}, bf16[16,1024]{1,0:T(8,128)(2,1)S(1)}, u32[]{:S(2)}, u32[]{:S(2)}) %collective-permute-start.5) | collective-permute-done | bytes 32800 | tf_op jit(solution)/shard_map/ppermute | solution.py:403
  16.2 0.0 collective-permute-done.3.refs_2_
  16.2 0.8 %shift_tiles.1.shifted_ref = bf16[512,2304]{1,0:T(8,128)(2,1)S(1)} custom-call(bf16[64,32]{1,0:T(8,128)(2,1)S(1)} %get-tuple-element.18.pick_ref, bf16[32,1024]{1,0:T(8,128)(2,1)S(1)} %get-tuple-element.22.refs_0_, bf16[32,1024]{1,0:T(8,128)(2,1)S(1)} %collective-permute-done.2.refs_1_, bf16[32,1024]{1,0:T(8,128)(2,1)S(1)} %collective-permute-done.3.refs_2_, ...), custom_call_target="tpu_custom_call" | custom-call | tf_op jit(solution)/shard_map/shift_tiles/pallas_call | solution.py:254
  17.0 0.0 collective-permute-done.8.refs_1_
  17.0 1.4 %convolve_first.1 = (f32[3,16,1280]{2,1,0:T(8,128)S(1)}, s16[3,16,1408]{2,1,0:T(8,128)(2,1)S(1)}) custom-call(bf16[512,2304]{1,0:T(8,128)(2,1)S(1)} %shift_tiles.1.shifted_ref, bf16[128,512]{1,0:T(8,128)(2,1)S(1)} %arrange_other.1.after_ref.refs_0_, bf16[128,512]{1,0:T(8,128)(2,1)S(1)} %collective-permute-done.8.refs_1_, bf16[128,512]{1,0:T(8,128)(2,1)S(1)} %pass_on.1.refs_2_), custom_call_target="tpu_custom_call" | custom-call | tf_op jit(solution)/shard_map/convolve_first/pallas_call | solution.py:324
  18.4 0.0 collective-permute-done.7.slip_ref
  18.4 0.7 %convolve_last.1 = (f32[16,1280]{1,0:T(8,128)S(1)}, s16[16,1408]{1,0:T(8,128)(2,1)S(1)}, s16[16,1408]{1,0:T(8,128)(2,1)S(1)}, s16[16,1408]{1,0:T(8,128)(2,1)S(1)}) custom-call(bf16[512,2304]{1,0:T(8,128)(2,1)S(1)} %shift_tiles.1.shifted_ref, bf16[128,512]{1,0:T(8,128)(2,1)S(1)} %collective-permute-done.7.slip_ref, ...), custom_call_target="tpu_custom_call" | custom-call | tf_op jit(solution)/shard_map/convolve_last/pallas_call | solution.py:360
  19.2 2.0 %collective-permute-start.10 = (s16[16,1408]{1,0:T(8,128)(2,1)S(1)}, s16[16,1408]{1,0:T(8,128)(2,1)S(1)}, u32[]{:S(2)}, u32[]{:S(2)}) collective-permute-start(s16[16,1408]{1,0:T(8,128)(2,1)S(1)} %get-tuple-element.29), channel_id=1, source_target_pairs={{0,6},{1,7},{2,4},{3,5},{4,2},{5,3},{6,0},{7,1},{8,14},{9,15},{10,... | collective-permute-start | bytes 135176 | tf_op jit(solution)/shard_map/ppermute | solution.py:403
  21.2 0.6 %collective-permute-start.11 = (s16[16,1408]{1,0:T(8,128)(2,1)S(1)}, s16[16,1408]{1,0:T(8,128)(2,1)S(1)}, u32[]{:S(2)}, u32[]{:S(2)}) collective-permute-start(s16[16,1408]{1,0:T(8,128)(2,1)S(1)} %get-tuple-element.30), channel_id=1, source_target_pairs={{0,4},{1,5},{2,6},{3,7},{4,0},{5,1},{6,2},{7,3},{8,12},{9,13},{10,... | collective-permute-start | bytes 135176 | tf_op jit(solution)/shard_map/ppermute | solution.py:403
  21.8 1.0 %collective-permute-start.9 = (s16[16,1408]{1,0:T(8,128)(2,1)S(1)}, s16[16,1408]{1,0:T(8,128)(2,1)S(1)}, u32[]{:S(2)}, u32[]{:S(2)}) collective-permute-start(s16[16,1408]{1,0:T(8,128)(2,1)S(1)} %get-tuple-element.28), channel_id=1, source_target_pairs={{0,2},{1,3},{2,0},{3,1},{4,6},{5,7},{6,4},{7,5},{8,10},{9,11},{10,... | collective-permute-start | bytes 135176 | tf_op jit(solution)/shard_map/ppermute | solution.py:403
  22.7 1.5 %collective-permute-done.10.refs_1_ = s16[16,1408]{1,0:T(8,128)(2,1)S(1)} collective-permute-done((s16[16,1408]{1,0:T(8,128)(2,1)S(1)}, s16[16,1408]{1,0:T(8,128)(2,1)S(1)}, u32[]{:S(2)}, u32[]{:S(2)}) %collective-permute-start.10) | collective-permute-done | bytes 45088 | tf_op jit(solution)/shard_map/ppermute | solution.py:403
  24.3 1.0 %collective-permute-done.11.refs_2_ = s16[16,1408]{1,0:T(8,128)(2,1)S(1)} collective-permute-done((s16[16,1408]{1,0:T(8,128)(2,1)S(1)}, s16[16,1408]{1,0:T(8,128)(2,1)S(1)}, u32[]{:S(2)}, u32[]{:S(2)}) %collective-permute-start.11) | collective-permute-done | bytes 45088 | tf_op jit(solution)/shard_map/ppermute | solution.py:403
  25.3 0.6 %collective-permute-done.9.refs_0_ = s16[16,1408]{1,0:T(8,128)(2,1)S(1)} collective-permute-done((s16[16,1408]{1,0:T(8,128)(2,1)S(1)}, s16[16,1408]{1,0:T(8,128)(2,1)S(1)}, u32[]{:S(2)}, u32[]{:S(2)}) %collective-permute-start.9) | collective-permute-done | bytes 45088 | tf_op jit(solution)/shard_map/ppermute | solution.py:403
  25.8 0.7 %add_up.1 = f32[8,2,1280]{2,1,0:T(2,128)} custom-call(f32[16,1280]{1,0:T(8,128)S(1)} %get-tuple-element.27.own_ref, s16[16,1408]{1,0:T(8,128)(2,1)S(1)} %collective-permute-done.9.refs_0_, s16[16,1408]{1,0:T(8,128)(2,1)S(1)} %collective-permute-done.10.refs_1_, s16[16,1408]{1,0:T(8,128)(2,1)S(1)} %collective-permute-done.11.refs_2_), custom_call_target="tpu_custom_call" | custom-call | tf_op jit(solution)/shard_map/add_up/pallas_call | solution.py:383
  (1 shorter events, 0.0 us)
Async XLA Ops:
  0.0 1.7 %collective-permute-start.1 = (bf16[16,16,256]{2,1,0:T(8,128)(2,1)}, bf16[16,16,256]{2,1,0:T(8,128)(2,1)S(1)}, u32[]{:S(2)}, u32[]{:S(2)}) collective-permute-start(bf16[16,16,256]{2,1,0:T(8,128)(2,1)} %slip_hbm.1), channel_id=1, source_target_pairs={{0,1},{1,0},{2,3},{3,2},{4,5},{5,4},{6,7},{7,6},{8,9},{9,8},{10,11... | collective-permute-start | bytes 393224 | tf_op jit(solution)/shard_map/ppermute | solution.py:403
  0.5 5.5 %collective-permute-start = (bf16[32,2,1024]{2,1,0:T(2,128)(2,1)}, bf16[32,2,1024]{2,1,0:T(2,128)(2,1)S(1)}, u32[]{:S(2)}, u32[]{:S(2)}) collective-permute-start(bf16[32,2,1024]{2,1,0:T(2,128)(2,1)} %bitcast.3), channel_id=1, source_target_pairs={{0,1},{1,0},{2,3},{3,2},{4,5},{5,4},{6,7},{7,6},{8,9},{9,8},{10,11... | collective-permute-start | bytes 393224 | tf_op jit(solution)/shard_map/ppermute | solution.py:403
  1.9 11.3 %collective-permute-start.6 = (bf16[128,512]{1,0:T(8,128)(2,1)S(1)}, bf16[128,512]{1,0:T(8,128)(2,1)S(1)}, u32[]{:S(2)}, u32[]{:S(2)}) collective-permute-start(bf16[128,512]{1,0:T(8,128)(2,1)S(1)} %arrange_other.1.after_ref.refs_0_), channel_id=1, source_target_pairs={{0,16},{8,24},{16,0},{24,8},{1,17},{9,25},{17,1},{25,9},{2,18},{10... | collective-permute-start | bytes 393224 | tf_op jit(solution)/shard_map/ppermute | solution.py:434
  6.8 6.4 %collective-permute-start.2 = (bf16[32,1024]{1,0:T(8,128)(2,1)S(1)}, bf16[32,1024]{1,0:T(8,128)(2,1)S(1)}, u32[]{:S(2)}, u32[]{:S(2)}) collective-permute-start(bf16[32,1024]{1,0:T(8,128)(2,1)S(1)} %get-tuple-element.23), channel_id=1, source_target_pairs={{0,2},{1,5},{2,0},{3,7},{4,6},{5,1},{6,4},{7,3},{8,10},{9,13},{10,... | collective-permute-start | bytes 196616 | tf_op jit(solution)/shard_map/ppermute | solution.py:423
  8.4 4.8 %collective-permute-start.4 = (bf16[16,1024]{1,0:T(8,128)(2,1)S(1)}, bf16[16,1024]{1,0:T(8,128)(2,1)S(1)}, u32[]{:S(2)}, u32[]{:S(2)}) collective-permute-start(bf16[16,1024]{1,0:T(8,128)(2,1)S(1)} %get-tuple-element.24), channel_id=1, source_target_pairs={{0,6},{1,7},{2,4},{3,5},{4,2},{5,3},{6,0},{7,1},{8,14},{9,15},{10,... | collective-permute-start | bytes 98312 | tf_op jit(solution)/shard_map/ppermute | solution.py:423
  9.9 7.2 %collective-permute-start.8 = (bf16[128,512]{1,0:T(8,128)(2,1)S(1)}, bf16[128,512]{1,0:T(8,128)(2,1)S(1)}, u32[]{:S(2)}, u32[]{:S(2)}) collective-permute-start(bf16[128,512]{1,0:T(8,128)(2,1)S(1)} %arrange_other.1.after_ref.refs_0_), channel_id=1, source_target_pairs={{0,8},{8,0},{16,24},{24,16},{1,9},{9,1},{17,25},{25,17},{2,10},{10... | collective-permute-start | bytes 393224 | tf_op jit(solution)/shard_map/ppermute | solution.py:434
  13.2 5.2 %collective-permute-start.7 = (bf16[128,512]{1,0:T(8,128)(2,1)S(1)}, bf16[128,512]{1,0:T(8,128)(2,1)S(1)}, u32[]{:S(2)}, u32[]{:S(2)}) collective-permute-start(bf16[128,512]{1,0:T(8,128)(2,1)S(1)} %pass_on.1.refs_2_), channel_id=1, source_target_pairs={{0,8},{8,0},{16,24},{24,16},{1,9},{9,1},{17,25},{25,17},{2,10},{10... | collective-permute-start | bytes 393224 | tf_op jit(solution)/shard_map/ppermute | solution.py:434
  14.8 1.4 %collective-permute-start.3 = (bf16[32,1024]{1,0:T(8,128)(2,1)S(1)}, bf16[32,1024]{1,0:T(8,128)(2,1)S(1)}, u32[]{:S(2)}, u32[]{:S(2)}) collective-permute-start(bf16[32,1024]{1,0:T(8,128)(2,1)S(1)} %collective-permute-done.2.refs_1_), channel_id=1, source_target_pairs={{0,1},{1,0},{2,3},{3,2},{4,5},{5,4},{6,7},{7,6},{8,9},{9,8},{10,11... | collective-permute-start | bytes 196616 | tf_op jit(solution)/shard_map/ppermute | solution.py:403
  14.8 1.4 %collective-permute-start.5 = (bf16[16,1024]{1,0:T(8,128)(2,1)S(1)}, bf16[16,1024]{1,0:T(8,128)(2,1)S(1)}, u32[]{:S(2)}, u32[]{:S(2)}) collective-permute-start(bf16[16,1024]{1,0:T(8,128)(2,1)S(1)} %collective-permute-done.4.refs_3_.refs_2_), channel_id=1, source_target_pairs={{0,1},{1,0},{2,3},{3,2},{4,5},{5,4},{6,7},{7,6},{8,9},{9,8},{10,11... | collective-permute-start | bytes 98312 | tf_op jit(solution)/shard_map/ppermute | solution.py:403
  19.2 5.1 %collective-permute-start.10 = (s16[16,1408]{1,0:T(8,128)(2,1)S(1)}, s16[16,1408]{1,0:T(8,128)(2,1)S(1)}, u32[]{:S(2)}, u32[]{:S(2)}) collective-permute-start(s16[16,1408]{1,0:T(8,128)(2,1)S(1)} %get-tuple-element.29), channel_id=1, source_target_pairs={{0,6},{1,7},{2,4},{3,5},{4,2},{5,3},{6,0},{7,1},{8,14},{9,15},{10,... | collective-permute-start | bytes 135176 | tf_op jit(solution)/shard_map/ppermute | solution.py:403
  21.2 4.0 %collective-permute-start.11 = (s16[16,1408]{1,0:T(8,128)(2,1)S(1)}, s16[16,1408]{1,0:T(8,128)(2,1)S(1)}, u32[]{:S(2)}, u32[]{:S(2)}) collective-permute-start(s16[16,1408]{1,0:T(8,128)(2,1)S(1)} %get-tuple-element.30), channel_id=1, source_target_pairs={{0,4},{1,5},{2,6},{3,7},{4,0},{5,1},{6,2},{7,3},{8,12},{9,13},{10,... | collective-permute-start | bytes 135176 | tf_op jit(solution)/shard_map/ppermute | solution.py:403
  21.8 4.0 %collective-permute-start.9 = (s16[16,1408]{1,0:T(8,128)(2,1)S(1)}, s16[16,1408]{1,0:T(8,128)(2,1)S(1)}, u32[]{:S(2)}, u32[]{:S(2)}) collective-permute-start(s16[16,1408]{1,0:T(8,128)(2,1)S(1)} %get-tuple-element.28), channel_id=1, source_target_pairs={{0,2},{1,3},{2,0},{3,1},{4,6},{5,7},{6,4},{7,5},{8,10},{9,11},{10,... | collective-permute-start | bytes 135176 | tf_op jit(solution)/shard_map/ppermute | solution.py:403

commit v10 on v9

--- a/solution.py
+++ b/solution.py
@@ -305,10 +305,8 @@
 
 
 def convolve_first_kernel(rows, shifted_ref, *refs):
-    slip_refs, (out_ref, sent_ref, stack_ref, product_ref) = refs[:-4], refs[-4:]
+    slip_refs, (out_ref, stack_ref, product_ref) = refs[:-3], refs[-3:]
     convolve_blocks(shifted_ref, slip_refs, stack_ref, product_ref, out_ref, rows)
-    for step in range(out_ref.shape[0]):
-        sent_ref[step] = as_sent(out_ref[step], sent_ref.shape[2])
 
 
 def convolve_scratch(shifted, count, height, depth, components):
@@ -319,44 +317,32 @@
 
 
 def convolve_first(shifted, slips, rows, components, length):
-    size = (len(slips), components * rows)
-    lanes = round_up(length, LANES) + LANES
+    shape = jax.ShapeDtypeStruct((len(slips), components * rows, length), jnp.float32)
     return pl.pallas_call(
         functools.partial(convolve_first_kernel, rows),
-        out_shape=(
-            jax.ShapeDtypeStruct(size + (length,), jnp.float32),
-            jax.ShapeDtypeStruct(size + (lanes,), jnp.int16),
-        ),
+        out_shape=shape,
         scratch_shapes=convolve_scratch(shifted, len(slips), *slips[0].shape, components),
         compiler_params=params(),
         name="convolve_first",
     )(shifted, *slips)
 
 
-def convolve_last_kernel(rows, shifted_ref, slip_ref, first_ref, early_ref, *refs):
+def convolve_last_kernel(rows, shifted_ref, slip_ref, first_ref, *refs):
     out_refs, (stack_ref, product_ref, last_ref) = refs[:-3], refs[-3:]
     convolve_blocks(shifted_ref, [slip_ref], stack_ref, product_ref, last_ref, rows)
     count = first_ref.shape[0]
     turn = lax.axis_index("site") ^ (lax.axis_index("patch") // 2)
     last = last_ref[0]
-    late = as_sent(last, early_ref.shape[2])
     for step, ref in enumerate(out_refs):
         source = step ^ turn
-        before = jnp.minimum(source, count - 1)
-
-        @pl.when(source == count)
-        def _():
-            ref[...] = late if step else last
-
-        @pl.when(source < count)
-        def _():
-            ref[...] = early_ref[before] if step else first_ref[before]
-
-
-def convolve_last(shifted, slip, first, early, rows, components):
+        total = jnp.where(source == count, last, first_ref[jnp.minimum(source, count - 1)])
+        ref[...] = as_sent(total, ref.shape[1]) if step else total
+
+
+def convolve_last(shifted, slip, first, rows, components):
     count, height, length = first.shape
     own = jax.ShapeDtypeStruct((height, length), jnp.float32)
-    sent = jax.ShapeDtypeStruct(early.shape[1:], jnp.int16)
+    sent = jax.ShapeDtypeStruct((height, round_up(length, LANES) + LANES), jnp.int16)
     return pl.pallas_call(
         functools.partial(convolve_last_kernel, rows),
         out_shape=(own,) + (sent,) * count,
@@ -364,7 +350,7 @@
         + [pltpu.VMEM((1, height, length), jnp.float32)],
         compiler_params=params(),
         name="convolve_last",
-    )(shifted, slip, first, early)
+    )(shifted, slip, first)
 
 
 def add_kernel(own_ref, *refs):
@@ -439,8 +425,8 @@
     shifted = shift_tiles(pick, pieces, components)
 
     slips = [blocks[step] for step in range(sites)]
-    first, early = convolve_first(shifted, slips[:-1], rows, components, length)
-    sums = convolve_last(shifted, slips[-1], first, early, rows, components)
+    first = convolve_first(shifted, slips[:-1], rows, components, length)
+    sums = convolve_last(shifted, slips[-1], first, rows, components)
     order = [1, chips - 1] + list(range(2, chips - 1))
     sent = [over_patch(sums[step], 2 * step) for step in order]
     return add_up(sums[0], sent, part, components)[None]

time: 26.7 us -> 26.7 us (level)
  no operation moved by 1% of the time
where the time goes in v10:
time: 26.7 us; the launch traced here: 26.5 us
  starting transfers between devices  14.9 us (56%)
  waiting for transfers between devices  5.77 us (22%)
  Pallas kernels  5.74 us (21%)
    ppermute x3, starting transfers between devices, local(): lax.ppermute(blocks[step - low], 'site', [(i, i ^ low) for i in range(sit...  7.31 us
    ppermute x7, starting transfers between devices, over_patch(): lax.ppermute(value, 'patch', [(i, i ^ offset) for i in range(devices)])  4.57 us
    ppermute x7, waiting for transfers between devices, over_patch(): lax.ppermute(value, 'patch', [(i, i ^ offset) for i in range(devices)])  4.02 us
    ppermute x2, starting transfers between devices, local(): lax.ppermute(pieces[1 + index], 'patch', [(i, i ^ 2 * hops[i % 2]) for i...  3.05 us
    ppermute x2, waiting for transfers between devices, local(): lax.ppermute(pieces[1 + index], 'patch', [(i, i ^ 2 * hops[i % 2]) for i...  1.75 us
    pallas_call x1, Pallas kernels, convolve_first(): pl.pallas_call(functools.partial(convolve_first_kernel, rows), out_shape=...  1.27 us
    pallas_call x1, Pallas kernels, arrange_own(): pl.pallas_call(functools.partial(arrange_own_kernel, chips, per_chip, cap...  1.14 us
    pallas_call x1, Pallas kernels, route_tiles(): pl.pallas_call(functools.partial(route_kernel, chips), in_specs=[pl.Block...  0.84 us
  transfers between devices with their start and end apart: 12, of which 5 were waited for; matrix products, arithmetic and copies ran while one was open for 0% of the time, Pallas kernels for 16%

profile of v10, /device:TPU:0, one launch (start us, length us, event | category | flops | bytes accessed | tf_op | source)
XLA Modules:
  0.0 26.5 jit_solution(8860484675395644783)
XLA Ops:
  0.0 0.5 %collective-permute-start.1 = (bf16[16,16,256]{2,1,0:T(8,128)(2,1)}, bf16[16,16,256]{2,1,0:T(8,128)(2,1)S(1)}, u32[]{:S(2)}, u32[]{:S(2)}) collective-permute-start(bf16[16,16,256]{2,1,0:T(8,128)(2,1)} %slip_hbm.1), channel_id=1, source_target_pairs={{0,1},{1,0},{2,3},{3,2},{4,5},{5,4},{6,7},{7,6},{8,9},{9,8},{10,11... | collective-permute-start | bytes 393224 | tf_op jit(solution)/shard_map/ppermute | solution.py:389
  0.5 0.1 collective-permute-start
  0.5 1.1 %arrange_own.1 = (bf16[128,512]{1,0:T(8,128)(2,1)S(1)}, bf16[64,64]{1,0:T(8,128)(2,1)S(1)}, bf16[64,32]{1,0:T(8,128)(2,1)S(1)}, bf16[32,2,1024]{2,1,0:T(2,128)(2,1)S(1)}) custom-call(bf16[16,16,256]{2,1,0:T(8,128)(2,1)} %slip_hbm.1, s32[1,128]{1,0:T(1,128)} %bitcast.5, bf16[32,2,1024]{2,1,0:T(2,128)(2,1)} %bitcast.4), custom_call_target="tpu_custom_call" | custom-call | tf_op jit(solution)/shard_map/arrange_own/pallas_call | solution.py:99
  1.7 0.0 collective-permute-done.1.slip_ref
  1.7 0.2 arrange_other.1.after_ref.refs_0_
  1.9 4.1 %collective-permute-start.6 = (bf16[128,512]{1,0:T(8,128)(2,1)S(1)}, bf16[128,512]{1,0:T(8,128)(2,1)S(1)}, u32[]{:S(2)}, u32[]{:S(2)}) collective-permute-start(bf16[128,512]{1,0:T(8,128)(2,1)S(1)} %arrange_other.1.after_ref.refs_0_), channel_id=1, source_target_pairs={{0,16},{8,24},{16,0},{24,8},{1,17},{9,25},{17,1},{25,9},{2,18},{10... | collective-permute-start | bytes 393224 | tf_op jit(solution)/shard_map/ppermute | solution.py:420
  6.0 0.0 collective-permute-done.other_ref
  6.0 0.8 %route_tiles.1 = (bf16[32,1024]{1,0:T(8,128)(2,1)S(1)}, bf16[32,1024]{1,0:T(8,128)(2,1)S(1)}, bf16[16,1024]{1,0:T(8,128)(2,1)S(1)}) custom-call(bf16[64,64]{1,0:T(8,128)(2,1)S(1)} %get-tuple-element.17.send_ref, bf16[32,2,1024]{2,1,0:T(2,128)(2,1)S(1)} %get-tuple-element.18.own_ref, bf16[32,2,1024]{2,1,0:T(2,128)(2,1)S(1)} %collective-permute-done.other_ref, ...), custom_call_target="tpu_custom_call" | custom-call | tf_op jit(solution)/shard_map/route_tiles/pallas_call | solution.py:200
  6.8 1.6 %collective-permute-start.2 = (bf16[32,1024]{1,0:T(8,128)(2,1)S(1)}, bf16[32,1024]{1,0:T(8,128)(2,1)S(1)}, u32[]{:S(2)}, u32[]{:S(2)}) collective-permute-start(bf16[32,1024]{1,0:T(8,128)(2,1)S(1)} %get-tuple-element.21), channel_id=1, source_target_pairs={{0,2},{1,5},{2,0},{3,7},{4,6},{5,1},{6,4},{7,3},{8,10},{9,13},{10,... | collective-permute-start | bytes 196616 | tf_op jit(solution)/shard_map/ppermute | solution.py:409
  8.4 1.5 %collective-permute-start.4 = (bf16[16,1024]{1,0:T(8,128)(2,1)S(1)}, bf16[16,1024]{1,0:T(8,128)(2,1)S(1)}, u32[]{:S(2)}, u32[]{:S(2)}) collective-permute-start(bf16[16,1024]{1,0:T(8,128)(2,1)S(1)} %get-tuple-element.22), channel_id=1, source_target_pairs={{0,6},{1,7},{2,4},{3,5},{4,2},{5,3},{6,0},{7,1},{8,14},{9,15},{10,... | collective-permute-start | bytes 98312 | tf_op jit(solution)/shard_map/ppermute | solution.py:409
  9.9 1.6 %collective-permute-start.8 = (bf16[128,512]{1,0:T(8,128)(2,1)S(1)}, bf16[128,512]{1,0:T(8,128)(2,1)S(1)}, u32[]{:S(2)}, u32[]{:S(2)}) collective-permute-start(bf16[128,512]{1,0:T(8,128)(2,1)S(1)} %arrange_other.1.after_ref.refs_0_), channel_id=1, source_target_pairs={{0,8},{8,0},{16,24},{24,16},{1,9},{9,1},{17,25},{25,17},{2,10},{10... | collective-permute-start | bytes 393224 | tf_op jit(solution)/shard_map/ppermute | solution.py:420
  11.4 1.7 %collective-permute-done.4.refs_3_.refs_2_ = bf16[16,1024]{1,0:T(8,128)(2,1)S(1)} collective-permute-done((bf16[16,1024]{1,0:T(8,128)(2,1)S(1)}, bf16[16,1024]{1,0:T(8,128)(2,1)S(1)}, u32[]{:S(2)}, u32[]{:S(2)}) %collective-permute-start.4) | collective-permute-done | bytes 32800 | tf_op jit(solution)/shard_map/ppermute | solution.py:409
  13.2 0.0 collective-permute-done.2.refs_1_
  13.2 0.0 collective-permute-done.6.refs_0_
  13.2 1.6 %collective-permute-start.7 = (bf16[128,512]{1,0:T(8,128)(2,1)S(1)}, bf16[128,512]{1,0:T(8,128)(2,1)S(1)}, u32[]{:S(2)}, u32[]{:S(2)}) collective-permute-start(bf16[128,512]{1,0:T(8,128)(2,1)S(1)} %pass_on.1.refs_2_), channel_id=1, source_target_pairs={{0,8},{8,0},{16,24},{24,16},{1,9},{9,1},{17,25},{25,17},{2,10},{10... | collective-permute-start | bytes 393224 | tf_op jit(solution)/shard_map/ppermute | solution.py:420
  14.8 0.0 collective-permute-start.3
  14.8 0.5 %collective-permute-start.5 = (bf16[16,1024]{1,0:T(8,128)(2,1)S(1)}, bf16[16,1024]{1,0:T(8,128)(2,1)S(1)}, u32[]{:S(2)}, u32[]{:S(2)}) collective-permute-start(bf16[16,1024]{1,0:T(8,128)(2,1)S(1)} %collective-permute-done.4.refs_3_.refs_2_), channel_id=1, source_target_pairs={{0,1},{1,0},{2,3},{3,2},{4,5},{5,4},{6,7},{7,6},{8,9},{9,8},{10,11... | collective-permute-start | bytes 98312 | tf_op jit(solution)/shard_map/ppermute | solution.py:389
  15.4 0.9 %collective-permute-done.5.refs_4_ = bf16[16,1024]{1,0:T(8,128)(2,1)S(1)} collective-permute-done((bf16[16,1024]{1,0:T(8,128)(2,1)S(1)}, bf16[16,1024]{1,0:T(8,128)(2,1)S(1)}, u32[]{:S(2)}, u32[]{:S(2)}) %collective-permute-start.5) | collective-permute-done | bytes 32800 | tf_op jit(solution)/shard_map/ppermute | solution.py:389
  16.2 0.0 collective-permute-done.3.refs_2_
  16.2 0.8 %shift_tiles.1.shifted_ref = bf16[512,2304]{1,0:T(8,128)(2,1)S(1)} custom-call(bf16[64,32]{1,0:T(8,128)(2,1)S(1)} %get-tuple-element.16.pick_ref, bf16[32,1024]{1,0:T(8,128)(2,1)S(1)} %get-tuple-element.20.refs_0_, bf16[32,1024]{1,0:T(8,128)(2,1)S(1)} %collective-permute-done.2.refs_1_, bf16[32,1024]{1,0:T(8,128)(2,1)S(1)} %collective-permute-done.3.refs_2_, ...), custom_call_target="tpu_custom_call" | custom-call | tf_op jit(solution)/shard_map/shift_tiles/pallas_call | solution.py:254
  17.0 0.0 collective-permute-done.8.refs_1_
  17.0 1.3 %convolve_first.1.first_ref = f32[3,16,1280]{2,1,0:T(8,128)S(1)} custom-call(bf16[512,2304]{1,0:T(8,128)(2,1)S(1)} %shift_tiles.1.shifted_ref, bf16[128,512]{1,0:T(8,128)(2,1)S(1)} %arrange_other.1.after_ref.refs_0_, bf16[128,512]{1,0:T(8,128)(2,1)S(1)} %collective-permute-done.8.refs_1_, bf16[128,512]{1,0:T(8,128)(2,1)S(1)} %pass_on.1.refs_2_), custom_call_target="tpu_custom_call" | custom-call | tf_op jit(solution)/shard_map/convolve_first/pallas_call | solution.py:321
  18.3 0.0 collective-permute-done.7.slip_ref
  18.3 0.7 %convolve_last.1 = (f32[16,1280]{1,0:T(8,128)S(1)}, s16[16,1408]{1,0:T(8,128)(2,1)S(1)}, s16[16,1408]{1,0:T(8,128)(2,1)S(1)}, s16[16,1408]{1,0:T(8,128)(2,1)S(1)}) custom-call(bf16[512,2304]{1,0:T(8,128)(2,1)S(1)} %shift_tiles.1.shifted_ref, bf16[128,512]{1,0:T(8,128)(2,1)S(1)} %collective-permute-done.7.slip_ref, f32[3,16,1280]{2,1,0:T(8,128)S(1)} %convolve_first.1.first_ref), custom_call_target="tpu_custom_call" | custom-call | tf_op jit(solution)/shard_map/convolve_last/pallas_call | solution.py:346
  19.1 2.2 %collective-permute-start.10 = (s16[16,1408]{1,0:T(8,128)(2,1)S(1)}, s16[16,1408]{1,0:T(8,128)(2,1)S(1)}, u32[]{:S(2)}, u32[]{:S(2)}) collective-permute-start(s16[16,1408]{1,0:T(8,128)(2,1)S(1)} %get-tuple-element.25), channel_id=1, source_target_pairs={{0,6},{1,7},{2,4},{3,5},{4,2},{5,3},{6,0},{7,1},{8,14},{9,15},{10,... | collective-permute-start | bytes 135176 | tf_op jit(solution)/shard_map/ppermute | solution.py:389
  21.2 0.5 %collective-permute-start.11 = (s16[16,1408]{1,0:T(8,128)(2,1)S(1)}, s16[16,1408]{1,0:T(8,128)(2,1)S(1)}, u32[]{:S(2)}, u32[]{:S(2)}) collective-permute-start(s16[16,1408]{1,0:T(8,128)(2,1)S(1)} %get-tuple-element.26), channel_id=1, source_target_pairs={{0,4},{1,5},{2,6},{3,7},{4,0},{5,1},{6,2},{7,3},{8,12},{9,13},{10,... | collective-permute-start | bytes 135176 | tf_op jit(solution)/shard_map/ppermute | solution.py:389
  21.7 0.9 %collective-permute-start.9 = (s16[16,1408]{1,0:T(8,128)(2,1)S(1)}, s16[16,1408]{1,0:T(8,128)(2,1)S(1)}, u32[]{:S(2)}, u32[]{:S(2)}) collective-permute-start(s16[16,1408]{1,0:T(8,128)(2,1)S(1)} %get-tuple-element.24), channel_id=1, source_target_pairs={{0,2},{1,3},{2,0},{3,1},{4,6},{5,7},{6,4},{7,5},{8,10},{9,11},{10,... | collective-permute-start | bytes 135176 | tf_op jit(solution)/shard_map/ppermute | solution.py:389
  22.6 1.5 %collective-permute-done.10.refs_1_ = s16[16,1408]{1,0:T(8,128)(2,1)S(1)} collective-permute-done((s16[16,1408]{1,0:T(8,128)(2,1)S(1)}, s16[16,1408]{1,0:T(8,128)(2,1)S(1)}, u32[]{:S(2)}, u32[]{:S(2)}) %collective-permute-start.10) | collective-permute-done | bytes 45088 | tf_op jit(solution)/shard_map/ppermute | solution.py:389
  24.1 1.1 %collective-permute-done.11.refs_2_ = s16[16,1408]{1,0:T(8,128)(2,1)S(1)} collective-permute-done((s16[16,1408]{1,0:T(8,128)(2,1)S(1)}, s16[16,1408]{1,0:T(8,128)(2,1)S(1)}, u32[]{:S(2)}, u32[]{:S(2)}) %collective-permute-start.11) | collective-permute-done | bytes 45088 | tf_op jit(solution)/shard_map/ppermute | solution.py:389
  25.3 0.5 %collective-permute-done.9.refs_0_ = s16[16,1408]{1,0:T(8,128)(2,1)S(1)} collective-permute-done((s16[16,1408]{1,0:T(8,128)(2,1)S(1)}, s16[16,1408]{1,0:T(8,128)(2,1)S(1)}, u32[]{:S(2)}, u32[]{:S(2)}) %collective-permute-start.9) | collective-permute-done | bytes 45088 | tf_op jit(solution)/shard_map/ppermute | solution.py:389
  25.8 0.7 %add_up.1 = f32[8,2,1280]{2,1,0:T(2,128)} custom-call(f32[16,1280]{1,0:T(8,128)S(1)} %get-tuple-element.23.own_ref, s16[16,1408]{1,0:T(8,128)(2,1)S(1)} %collective-permute-done.9.refs_0_, s16[16,1408]{1,0:T(8,128)(2,1)S(1)} %collective-permute-done.10.refs_1_, s16[16,1408]{1,0:T(8,128)(2,1)S(1)} %collective-permute-done.11.refs_2_), custom_call_target="tpu_custom_call" | custom-call | tf_op jit(solution)/shard_map/add_up/pallas_call | solution.py:369
  (1 shorter events, 0.0 us)
Async XLA Ops:
  0.0 1.7 %collective-permute-start.1 = (bf16[16,16,256]{2,1,0:T(8,128)(2,1)}, bf16[16,16,256]{2,1,0:T(8,128)(2,1)S(1)}, u32[]{:S(2)}, u32[]{:S(2)}) collective-permute-start(bf16[16,16,256]{2,1,0:T(8,128)(2,1)} %slip_hbm.1), channel_id=1, source_target_pairs={{0,1},{1,0},{2,3},{3,2},{4,5},{5,4},{6,7},{7,6},{8,9},{9,8},{10,11... | collective-permute-start | bytes 393224 | tf_op jit(solution)/shard_map/ppermute | solution.py:389
  0.5 5.5 %collective-permute-start = (bf16[32,2,1024]{2,1,0:T(2,128)(2,1)}, bf16[32,2,1024]{2,1,0:T(2,128)(2,1)S(1)}, u32[]{:S(2)}, u32[]{:S(2)}) collective-permute-start(bf16[32,2,1024]{2,1,0:T(2,128)(2,1)} %bitcast.3), channel_id=1, source_target_pairs={{0,1},{1,0},{2,3},{3,2},{4,5},{5,4},{6,7},{7,6},{8,9},{9,8},{10,11... | collective-permute-start | bytes 393224 | tf_op jit(solution)/shard_map/ppermute | solution.py:389
  1.9 11.3 %collective-permute-start.6 = (bf16[128,512]{1,0:T(8,128)(2,1)S(1)}, bf16[128,512]{1,0:T(8,128)(2,1)S(1)}, u32[]{:S(2)}, u32[]{:S(2)}) collective-permute-start(bf16[128,512]{1,0:T(8,128)(2,1)S(1)} %arrange_other.1.after_ref.refs_0_), channel_id=1, source_target_pairs={{0,16},{8,24},{16,0},{24,8},{1,17},{9,25},{17,1},{25,9},{2,18},{10... | collective-permute-start | bytes 393224 | tf_op jit(solution)/shard_map/ppermute | solution.py:420
  6.8 6.4 %collective-permute-start.2 = (bf16[32,1024]{1,0:T(8,128)(2,1)S(1)}, bf16[32,1024]{1,0:T(8,128)(2,1)S(1)}, u32[]{:S(2)}, u32[]{:S(2)}) collective-permute-start(bf16[32,1024]{1,0:T(8,128)(2,1)S(1)} %get-tuple-element.21), channel_id=1, source_target_pairs={{0,2},{1,5},{2,0},{3,7},{4,6},{5,1},{6,4},{7,3},{8,10},{9,13},{10,... | collective-permute-start | bytes 196616 | tf_op jit(solution)/shard_map/ppermute | solution.py:409
  8.4 4.8 %collective-permute-start.4 = (bf16[16,1024]{1,0:T(8,128)(2,1)S(1)}, bf16[16,1024]{1,0:T(8,128)(2,1)S(1)}, u32[]{:S(2)}, u32[]{:S(2)}) collective-permute-start(bf16[16,1024]{1,0:T(8,128)(2,1)S(1)} %get-tuple-element.22), channel_id=1, source_target_pairs={{0,6},{1,7},{2,4},{3,5},{4,2},{5,3},{6,0},{7,1},{8,14},{9,15},{10,... | collective-permute-start | bytes 98312 | tf_op jit(solution)/shard_map/ppermute | solution.py:409
  9.9 7.2 %collective-permute-start.8 = (bf16[128,512]{1,0:T(8,128)(2,1)S(1)}, bf16[128,512]{1,0:T(8,128)(2,1)S(1)}, u32[]{:S(2)}, u32[]{:S(2)}) collective-permute-start(bf16[128,512]{1,0:T(8,128)(2,1)S(1)} %arrange_other.1.after_ref.refs_0_), channel_id=1, source_target_pairs={{0,8},{8,0},{16,24},{24,16},{1,9},{9,1},{17,25},{25,17},{2,10},{10... | collective-permute-start | bytes 393224 | tf_op jit(solution)/shard_map/ppermute | solution.py:420
  13.2 5.1 %collective-permute-start.7 = (bf16[128,512]{1,0:T(8,128)(2,1)S(1)}, bf16[128,512]{1,0:T(8,128)(2,1)S(1)}, u32[]{:S(2)}, u32[]{:S(2)}) collective-permute-start(bf16[128,512]{1,0:T(8,128)(2,1)S(1)} %pass_on.1.refs_2_), channel_id=1, source_target_pairs={{0,8},{8,0},{16,24},{24,16},{1,9},{9,1},{17,25},{25,17},{2,10},{10... | collective-permute-start | bytes 393224 | tf_op jit(solution)/shard_map/ppermute | solution.py:420
  14.8 1.4 %collective-permute-start.3 = (bf16[32,1024]{1,0:T(8,128)(2,1)S(1)}, bf16[32,1024]{1,0:T(8,128)(2,1)S(1)}, u32[]{:S(2)}, u32[]{:S(2)}) collective-permute-start(bf16[32,1024]{1,0:T(8,128)(2,1)S(1)} %collective-permute-done.2.refs_1_), channel_id=1, source_target_pairs={{0,1},{1,0},{2,3},{3,2},{4,5},{5,4},{6,7},{7,6},{8,9},{9,8},{10,11... | collective-permute-start | bytes 196616 | tf_op jit(solution)/shard_map/ppermute | solution.py:389
  14.8 1.4 %collective-permute-start.5 = (bf16[16,1024]{1,0:T(8,128)(2,1)S(1)}, bf16[16,1024]{1,0:T(8,128)(2,1)S(1)}, u32[]{:S(2)}, u32[]{:S(2)}) collective-permute-start(bf16[16,1024]{1,0:T(8,128)(2,1)S(1)} %collective-permute-done.4.refs_3_.refs_2_), channel_id=1, source_target_pairs={{0,1},{1,0},{2,3},{3,2},{4,5},{5,4},{6,7},{7,6},{8,9},{9,8},{10,11... | collective-permute-start | bytes 98312 | tf_op jit(solution)/shard_map/ppermute | solution.py:389
  19.1 5.1 %collective-permute-start.10 = (s16[16,1408]{1,0:T(8,128)(2,1)S(1)}, s16[16,1408]{1,0:T(8,128)(2,1)S(1)}, u32[]{:S(2)}, u32[]{:S(2)}) collective-permute-start(s16[16,1408]{1,0:T(8,128)(2,1)S(1)} %get-tuple-element.25), channel_id=1, source_target_pairs={{0,6},{1,7},{2,4},{3,5},{4,2},{5,3},{6,0},{7,1},{8,14},{9,15},{10,... | collective-permute-start | bytes 135176 | tf_op jit(solution)/shard_map/ppermute | solution.py:389
  21.2 4.0 %collective-permute-start.11 = (s16[16,1408]{1,0:T(8,128)(2,1)S(1)}, s16[16,1408]{1,0:T(8,128)(2,1)S(1)}, u32[]{:S(2)}, u32[]{:S(2)}) collective-permute-start(s16[16,1408]{1,0:T(8,128)(2,1)S(1)} %get-tuple-element.26), channel_id=1, source_target_pairs={{0,4},{1,5},{2,6},{3,7},{4,0},{5,1},{6,2},{7,3},{8,12},{9,13},{10,... | collective-permute-start | bytes 135176 | tf_op jit(solution)/shard_map/ppermute | solution.py:389
  21.7 4.0 %collective-permute-start.9 = (s16[16,1408]{1,0:T(8,128)(2,1)S(1)}, s16[16,1408]{1,0:T(8,128)(2,1)S(1)}, u32[]{:S(2)}, u32[]{:S(2)}) collective-permute-start(s16[16,1408]{1,0:T(8,128)(2,1)S(1)} %get-tuple-element.24), channel_id=1, source_target_pairs={{0,2},{1,3},{2,0},{3,1},{4,6},{5,7},{6,4},{7,5},{8,10},{9,11},{10,... | collective-permute-start | bytes 135176 | tf_op jit(solution)/shard_map/ppermute | solution.py:389
